TPU v7x, 32 devices: a whole 2x2x4 slice. The times are simulated.
32 devices in a mesh: wide: 8 (over y, x, core), narrow: 4 (over z).
Axes of the slice: x: 2, y: 2, z: 4, core: 2. Of those that a mesh axis runs over, the one named last changes fastest.
Arguments:
- block_input: bfloat16 [65536, 768], P(('wide', 'narrow')), may hold values from -6 to 6
- doc_lengths: int32 [32, 4], P(('wide', 'narrow')), may hold values from 0 to 2048, as said below
- cotangent: bfloat16 [65536, 768], P(('wide', 'narrow')), may hold values from -6 to 6
- weight_query: float32 [768, 768], P(('wide', 'narrow')), may hold values from -0.21875 to 0.21875
- weight_keyval: float32 [768, 128], P(('wide', 'narrow')), may hold values from -0.21875 to 0.21875
- weight_output: float32 [768, 768], P(('wide', 'narrow')), may hold values from -0.625 to 0.625
- weight_expand: float32 [768, 3072], P(('wide', 'narrow')), may hold values from -0.21875 to 0.21875
- weight_reduce: float32 [3072, 768], P(('wide', 'narrow')), may hold values from -0.109375 to 0.109375
- momentum_query: float32 [768, 768], P(('wide', 'narrow')), may hold values from -2560 to 2560
- momentum_keyval: float32 [768, 128], P(('wide', 'narrow')), may hold values from -2560 to 2560
- momentum_output: float32 [768, 768], P(('wide', 'narrow')), may hold values from -2560 to 2560
- momentum_expand: float32 [768, 3072], P(('wide', 'narrow')), may hold values from -2560 to 2560
- momentum_reduce: float32 [3072, 768], P(('wide', 'narrow')), may hold values from -2560 to 2560
- norm_gains: float32 [2, 768], replicated, may hold values from 0.5 to 1.5
- norm_biases: float32 [2, 768], replicated, may hold values from -4 to 4
- proj_biases: float32 [5504], replicated, may hold values from -4 to 4
- adam_first: float32 [8576], replicated, may hold values from -1280 to 1280
- adam_second: float32 [8576], replicated, may hold values from 655.36 to 131072
Outputs:
- block_output: bfloat16 [65536, 768], P(('wide', 'narrow'))
- input_grad: float32 [65536, 768], P(('wide', 'narrow'))
- new_momentum_query: float32 [768, 768], P(('wide', 'narrow'))
- new_momentum_keyval: float32 [768, 128], P(('wide', 'narrow'))
- new_momentum_output: float32 [768, 768], P(('wide', 'narrow'))
- new_momentum_expand: float32 [768, 3072], P(('wide', 'narrow'))
- new_momentum_reduce: float32 [3072, 768], P(('wide', 'narrow'))
- new_weight_query: float32 [768, 768], P(('wide', 'narrow'))
- new_weight_keyval: float32 [768, 128], P(('wide', 'narrow'))
- new_weight_output: float32 [768, 768], P(('wide', 'narrow'))
- new_weight_expand: float32 [768, 3072], P(('wide', 'narrow'))
- new_weight_reduce: float32 [3072, 768], P(('wide', 'narrow'))
- vector_first: float32 [8576], replicated
- vector_second: float32 [8576], replicated
- vector_new: float32 [8576], replicated
Inputs may be any that keep to these rules, and one draw needn't show every extreme that they name: `doc_lengths`: row s lists the sequence lengths of device s: nonzero ones first, each 2048, 1024 or 512, zeros for unused slots, summing to 2048.
All inputs are finite; a program needn't handle non-finite values.
Results may differ from a plain program's by a relative error of at most 0.0094.
Values may be sent and summed in bfloat16 or wider, within the bound.
No kernel may reach another device: no remote copies, remote signals or barrier semaphores. Data moves between devices by JAX's collectives and lax.ppermute only.
A program may use at most 576 MiB of HBM per device.

v0:
```python
from functools import partial
import math

import jax
import jax.numpy as jnp
from jax import lax
from jax.sharding import PartitionSpec as P

D = 768
HEADS = 12
HEAD_DIM = 64
ROT = 16
FF = 3072
TOK_DEV = 2048
NS_STEPS = 5
STEP = 10
QBLOCK = 512


HIGHEST = lax.Precision.HIGHEST
ROPE_BASE = 10000.0
NORM_EPS = 1e-05
NS_COEFFS = (3.4445, -4.775, 2.0315)
MUON_RATE = 0.5
MUON_MOMENTUM = 0.5
ADAM_RATE = 0.3
BETA_FIRST = 0.9
BETA_SECOND = 0.95
ADAM_EPS = 1e-08


def for_sending(x):
    return jax.tree.map(lambda a: a.astype(jnp.bfloat16) if a.dtype == jnp.float32 else a, x)


def broadcast(x, axis, root):
    mine = lax.axis_index(axis) == root
    return lax.psum(jnp.where(mine, x, jnp.zeros_like(x)), axis)


def matmul(left, right):
    return jnp.dot(left, right, precision=HIGHEST, preferred_element_type=jnp.float32)


def contract_rows(left, right):
    return lax.dot_general(
        left, right, (((0,), (0,)), ((), ())), preferred_element_type=jnp.float32
    )


def times_transposed(left, right):
    return lax.dot_general(
        left, right, (((1,), (1,)), ((), ())), preferred_element_type=jnp.float32
    )


def layer_norm(tokens, gain_row, shift_row):
    centred = tokens - jnp.mean(tokens, axis=-1, keepdims=True)
    spread = jnp.mean(centred * centred, axis=-1, keepdims=True)
    return centred * lax.rsqrt(spread + NORM_EPS) * gain_row + shift_row


def rotary(values, positions):
    half_rot = ROT // 2
    frequency = ROPE_BASE ** (-(2.0 * jnp.arange(half_rot, dtype=jnp.float32)) / ROT)
    angles = positions.astype(jnp.float32)[:, None] * frequency[None, :]
    cosine_table = jnp.concatenate([jnp.cos(angles), jnp.cos(angles)], axis=-1)
    sine_table = jnp.concatenate([jnp.sin(angles), jnp.sin(angles)], axis=-1)
    if values.ndim == 3:
        cosine_table = cosine_table[:, None, :]
        sine_table = sine_table[:, None, :]
    leading = values[..., :half_rot]
    trailing = values[..., half_rot:ROT]
    turned = (
        values[..., :ROT] * cosine_table
        + jnp.concatenate([-trailing, leading], axis=-1) * sine_table
    )
    return jnp.concatenate([turned, values[..., ROT:]], axis=-1)


def locate(lengths):
    doc_ends = jnp.cumsum(lengths)
    starts = doc_ends - lengths
    token_ids = jnp.arange(TOK_DEV, dtype=jnp.int32)
    doc_ids = jnp.sum((token_ids[:, None] >= doc_ends[None, :]).astype(jnp.int32), axis=1)
    slot_ids = jnp.arange(lengths.shape[0], dtype=jnp.int32)
    doc_starts = jnp.sum(
        jnp.where(doc_ids[:, None] == slot_ids[None, :], starts[None, :], 0), axis=1
    )
    return (doc_ids, token_ids - doc_starts)


def block_scores(query_rows, key_rows, doc_ids, row_lo):
    row_count = query_rows.shape[0]
    key_count = key_rows.shape[0]
    row_ids = row_lo + jnp.arange(row_count, dtype=jnp.int32)
    key_ids = jnp.arange(key_count, dtype=jnp.int32)
    allowed = (doc_ids[row_lo : row_lo + row_count][:, None] == doc_ids[:key_count][None, :]) & (
        key_ids[None, :] <= row_ids[:, None]
    )
    scores = jnp.einsum(
        "qhd,kd->hqk", query_rows, key_rows, preferred_element_type=jnp.float32
    ) / math.sqrt(HEAD_DIM)
    return jnp.where(allowed[None], scores, -1e30)


def newton_schulz(matrix):
    is_tall = matrix.shape[0] > matrix.shape[1]
    iterate = matrix.T if is_tall else matrix
    iterate = iterate / (jnp.sqrt(jnp.sum(iterate * iterate)) + 1e-07)
    for sweep in range(NS_STEPS):
        gram_matrix = matmul(iterate, iterate.T)
        polynomial = NS_COEFFS[1] * gram_matrix + NS_COEFFS[2] * matmul(gram_matrix, gram_matrix)
        iterate = NS_COEFFS[0] * iterate + matmul(polynomial, iterate)
    return iterate.T if is_tall else iterate


def zeros_like_matrix(matrix):
    return jnp.zeros_like(matrix)


def per_device(
    block_input,
    doc_lengths,
    cotangent,
    weight_query,
    weight_keyval,
    weight_output,
    weight_expand,
    weight_reduce,
    momentum_query,
    momentum_keyval,
    momentum_output,
    momentum_expand,
    momentum_reduce,
    norm_gains,
    norm_biases,
    proj_biases,
    adam_first,
    adam_second,
):
    masters = (weight_query, weight_keyval, weight_output, weight_expand, weight_reduce)
    momenta = (momentum_query, momentum_keyval, momentum_output, momentum_expand, momentum_reduce)
    low_copies = tuple((master.astype(jnp.bfloat16) for master in masters))
    gathered = jax.tree.map(
        lambda part, own: part.astype(own.dtype),
        lax.all_gather(for_sending(low_copies), ("wide", "narrow"), axis=0, tiled=True),
        low_copies,
    )
    full_query, full_keyval, full_output, full_expand, full_reduce = gathered
    bias_query = proj_biases[:D]
    bias_keyval = proj_biases[D : D + 2 * HEAD_DIM]
    bias_output = proj_biases[D + 2 * HEAD_DIM : 2 * D + 2 * HEAD_DIM]
    bias_expand = proj_biases[2 * D + 2 * HEAD_DIM : 2 * D + 2 * HEAD_DIM + FF]
    bias_reduce = proj_biases[2 * D + 2 * HEAD_DIM + FF :]
    tokens = block_input.astype(jnp.float32)
    doc_ids, positions = locate(doc_lengths[0])
    normed_attn, attn_norm_pull = jax.vjp(layer_norm, tokens, norm_gains[0], norm_biases[0])
    normed_ffn, ffn_norm_pull = jax.vjp(layer_norm, tokens, norm_gains[1], norm_biases[1])
    normed_attn_low = normed_attn.astype(jnp.bfloat16)
    normed_ffn_low = normed_ffn.astype(jnp.bfloat16)
    query_pre = (
        jnp.dot(normed_attn_low, full_query, preferred_element_type=jnp.float32) + bias_query
    )
    keyval_pre = (
        jnp.dot(normed_attn_low, full_keyval, preferred_element_type=jnp.float32) + bias_keyval
    )
    rotate_here = partial(rotary, positions=positions)
    queries_full, query_rope_pull = jax.vjp(
        rotate_here, query_pre.reshape(TOK_DEV, HEADS, HEAD_DIM)
    )
    keys_full, key_rope_pull = jax.vjp(rotate_here, keyval_pre[:, :HEAD_DIM])
    queries_low = queries_full.astype(jnp.bfloat16)
    keys_low = keys_full.astype(jnp.bfloat16)
    values_low = keyval_pre[:, HEAD_DIM:].astype(jnp.bfloat16)
    block_count = TOK_DEV // QBLOCK
    mixed_parts = []
    lse_parts = []
    for block_index in range(block_count):
        row_lo = block_index * QBLOCK
        key_end = row_lo + QBLOCK
        scores = block_scores(queries_low[row_lo:key_end], keys_low[:key_end], doc_ids, row_lo)
        row_max = jnp.max(scores, axis=-1, keepdims=True)
        exp_terms = jnp.exp(scores - row_max)
        row_total = jnp.sum(exp_terms, axis=-1, keepdims=True)
        attn_probs = exp_terms / row_total
        lse_parts.append(row_max + jnp.log(row_total))
        mixed_parts.append(
            jnp.einsum(
                "hqk,kd->qhd",
                attn_probs.astype(jnp.bfloat16),
                values_low[:key_end],
                preferred_element_type=jnp.float32,
            )
        )
    mixed_low = jnp.concatenate(mixed_parts, axis=0).reshape(TOK_DEV, D).astype(jnp.bfloat16)
    attn_branch = jnp.dot(mixed_low, full_output, preferred_element_type=jnp.float32) + bias_output
    expand_pre = (
        jnp.dot(normed_ffn_low, full_expand, preferred_element_type=jnp.float32) + bias_expand
    )
    activated, gelu_pull = jax.vjp(partial(jax.nn.gelu, approximate=False), expand_pre)
    activated_low = activated.astype(jnp.bfloat16)
    ffn_branch = (
        jnp.dot(activated_low, full_reduce, preferred_element_type=jnp.float32) + bias_reduce
    )
    block_output = (tokens + attn_branch + ffn_branch).astype(jnp.bfloat16)
    back_weights = jax.tree.map(
        lambda part, own: part.astype(own.dtype),
        lax.all_gather(for_sending(low_copies), ("wide", "narrow"), axis=0, tiled=True),
        low_copies,
    )
    back_query, back_keyval, back_output, back_expand, back_reduce = back_weights
    cot_float = cotangent.astype(jnp.float32)
    grad_reduce = contract_rows(activated_low, cotangent)
    grad_output = contract_rows(mixed_low, cotangent)
    cot_sums = jnp.sum(cot_float, axis=0)
    grad_activated = times_transposed(cotangent, back_reduce)
    grad_expand_low = gelu_pull(grad_activated)[0].astype(jnp.bfloat16)
    grad_expand = contract_rows(normed_ffn_low, grad_expand_low)
    grad_bias_expand = jnp.sum(grad_expand_low.astype(jnp.float32), axis=0)
    grad_normed_ffn = times_transposed(grad_expand_low, back_expand)
    grad_mixed = (
        times_transposed(cotangent, back_output)
        .astype(jnp.bfloat16)
        .reshape(TOK_DEV, HEADS, HEAD_DIM)
    )
    grad_query_parts = []
    grad_keys = jnp.zeros((TOK_DEV, HEAD_DIM), jnp.float32)
    grad_values = jnp.zeros((TOK_DEV, HEAD_DIM), jnp.float32)
    for block_index in range(block_count):
        row_lo = block_index * QBLOCK
        key_end = row_lo + QBLOCK
        query_rows = queries_low[row_lo:key_end]
        grad_rows = grad_mixed[row_lo:key_end]
        scores = block_scores(query_rows, keys_low[:key_end], doc_ids, row_lo)
        attn_probs = jnp.exp(scores - lse_parts[block_index])
        grad_probs = jnp.einsum(
            "qhd,kd->hqk", grad_rows, values_low[:key_end], preferred_element_type=jnp.float32
        )
        row_delta = jnp.sum(attn_probs * grad_probs, axis=-1, keepdims=True)
        grad_scores = (attn_probs * (grad_probs - row_delta)).astype(jnp.bfloat16)
        grad_query_parts.append(
            jnp.einsum(
                "hqk,kd->qhd", grad_scores, keys_low[:key_end], preferred_element_type=jnp.float32
            )
            / math.sqrt(HEAD_DIM)
        )
        key_part = jnp.einsum(
            "hqk,qhd->kd", grad_scores, query_rows, preferred_element_type=jnp.float32
        ) / math.sqrt(HEAD_DIM)
        value_part = jnp.einsum(
            "hqk,qhd->kd",
            attn_probs.astype(jnp.bfloat16),
            grad_rows,
            preferred_element_type=jnp.float32,
        )
        grad_keys = grad_keys + jnp.pad(key_part, ((0, TOK_DEV - key_end), (0, 0)))
        grad_values = grad_values + jnp.pad(value_part, ((0, TOK_DEV - key_end), (0, 0)))
    grad_queries = jnp.concatenate(grad_query_parts, axis=0)
    grad_query_low = query_rope_pull(grad_queries)[0].reshape(TOK_DEV, D).astype(jnp.bfloat16)
    grad_keyval_low = jnp.concatenate([key_rope_pull(grad_keys)[0], grad_values], axis=1).astype(
        jnp.bfloat16
    )
    grad_query = contract_rows(normed_attn_low, grad_query_low)
    grad_keyval = contract_rows(normed_attn_low, grad_keyval_low)
    grad_bias_query = jnp.sum(grad_query_low.astype(jnp.float32), axis=0)
    grad_bias_keyval = jnp.sum(grad_keyval_low.astype(jnp.float32), axis=0)
    grad_normed_attn = times_transposed(grad_query_low, back_query) + times_transposed(
        grad_keyval_low, back_keyval
    )
    attn_input, attn_gain, attn_shift = attn_norm_pull(grad_normed_attn)
    ffn_input, ffn_gain, ffn_shift = ffn_norm_pull(grad_normed_ffn)
    input_grad = cot_float + attn_input + ffn_input
    local_vector = jnp.concatenate(
        [
            attn_gain,
            ffn_gain,
            attn_shift,
            ffn_shift,
            grad_bias_query,
            grad_bias_keyval,
            cot_sums,
            grad_bias_expand,
            cot_sums,
        ]
    )
    vector_grad = lax.psum(local_vector, ("wide", "narrow"))
    weight_grads = (grad_query, grad_keyval, grad_output, grad_expand, grad_reduce)
    wide_count = lax.axis_size("wide")
    narrow_count = lax.axis_size("narrow")
    device_count = wide_count * narrow_count
    split_grads = tuple(
        (
            grad.reshape(wide_count, narrow_count, grad.shape[0] // device_count, grad.shape[1])
            for grad in weight_grads
        )
    )
    group_sums = lax.psum_scatter(split_grads, "narrow", scatter_dimension=1, tiled=True)
    total_sums = lax.psum_scatter(group_sums, "wide", scatter_dimension=0, tiled=True)
    summed_grads = tuple((total.reshape(total.shape[2], total.shape[3]) for total in total_sums))
    new_momenta = tuple(
        (MUON_MOMENTUM * momentum + summed for momentum, summed in zip(momenta, summed_grads))
    )
    device_rank = lax.axis_index("wide") * narrow_count + lax.axis_index("narrow")
    owner_ranks = [matrix_index * device_count // 5 for matrix_index in range(5)]
    whole_momenta = lax.all_gather(new_momenta, ("wide", "narrow"), axis=0, tiled=True)
    shares = []
    for matrix_index in range(5):
        orthogonal = lax.cond(
            device_rank == owner_ranks[matrix_index],
            newton_schulz,
            zeros_like_matrix,
            whole_momenta[matrix_index],
        )
        full_matrix = broadcast(orthogonal, ("wide", "narrow"), owner_ranks[matrix_index])
        row_count = masters[matrix_index].shape[0]
        shares.append(lax.dynamic_slice_in_dim(full_matrix, device_rank * row_count, row_count, 0))
    new_weights = []
    for matrix_index in range(5):
        whole_rows = masters[matrix_index].shape[0] * device_count
        columns = masters[matrix_index].shape[1]
        factor = math.sqrt(max(1.0, whole_rows / columns))
        new_weights.append(masters[matrix_index] - MUON_RATE * factor * shares[matrix_index])
    params = jnp.concatenate([norm_gains.reshape(-1), norm_biases.reshape(-1), proj_biases])
    vector_first = BETA_FIRST * adam_first + (1.0 - BETA_FIRST) * vector_grad
    vector_second = BETA_SECOND * adam_second + (1.0 - BETA_SECOND) * vector_grad * vector_grad
    corrected_first = vector_first / (1.0 - BETA_FIRST**STEP)
    corrected_second = vector_second / (1.0 - BETA_SECOND**STEP)
    vector_new = params - ADAM_RATE * corrected_first / (jnp.sqrt(corrected_second) + ADAM_EPS)
    return (
        block_output,
        input_grad,
        new_momenta[0],
        new_momenta[1],
        new_momenta[2],
        new_momenta[3],
        new_momenta[4],
        new_weights[0],
        new_weights[1],
        new_weights[2],
        new_weights[3],
        new_weights[4],
        vector_first,
        vector_second,
        vector_new,
    )


def solution(mesh):
    in_specs = (
        P(("wide", "narrow"), None),
        P(("wide", "narrow"), None),
        P(("wide", "narrow"), None),
        P(("wide", "narrow"), None),
        P(("wide", "narrow"), None),
        P(("wide", "narrow"), None),
        P(("wide", "narrow"), None),
        P(("wide", "narrow"), None),
        P(("wide", "narrow"), None),
        P(("wide", "narrow"), None),
        P(("wide", "narrow"), None),
        P(("wide", "narrow"), None),
        P(("wide", "narrow"), None),
        P(),
        P(),
        P(),
        P(),
        P(),
    )
    out_specs = (
        P(("wide", "narrow"), None),
        P(("wide", "narrow"), None),
        P(("wide", "narrow"), None),
        P(("wide", "narrow"), None),
        P(("wide", "narrow"), None),
        P(("wide", "narrow"), None),
        P(("wide", "narrow"), None),
        P(("wide", "narrow"), None),
        P(("wide", "narrow"), None),
        P(("wide", "narrow"), None),
        P(("wide", "narrow"), None),
        P(("wide", "narrow"), None),
        P(),
        P(),
        P(),
    )
    return jax.shard_map(
        per_device, mesh=mesh, in_specs=in_specs, out_specs=out_specs, check_vma=False
    )
```

profile of v0, /device:TPU:0, one launch (start us, length us, event | category | flops | bytes accessed | tf_op | source)
XLA Modules:
  0.0 2705.5 jit_solution(16566317758742663351)
XLA Ops:
  27.9 71.5 %all_gather.50 = bf16[768,128]{1,0:T(8,128)(2,1)S(1)} all-gather(bf16[24,128]{1,0:T(8,128)(2,1)S(1)} %convert_element_type.138), channel_id=1, replica_groups=mesh['wide'=8,'narrow'=4] {'wide','narrow'}, dimensions={0}, use_global_device_ids=true | all-gather | bytes 202752 | tf_op jit(solution)/shard_map/all_gather | solution.py:147
  143.2 7.5 fusion.240
  150.7 7.5 fusion.242
  168.1 7.2 fusion.231
  177.5 12.7 fusion.303
  190.2 12.1 fusion.305
  202.3 20.1 fusion.221
  222.5 17.9 fusion.223
  248.4 15.4 fusion.387
  263.8 14.7 fusion.216
  278.6 15.4 fusion.302
  293.9 15.5 fusion.285
  309.5 27.8 %fusion.213 = (f32[12,512]{1,0:T(8,128)S(1)}, f32[1536,512,12]{1,0,2:T(8,128)}) fusion(f32[12,512,1536]{1,2,0:T(8,128)} %get-tuple-element.111, f32[12,512]{1,0:T(8,128)S(1)} %log_add_fusion.1, bf16[512,12,64]{0,2,1:T(8,128)(2,1)S(1)} %bitcast.469, bf16[2048,128]{0,1:T(8,128)(2,1)S(1)} %copy-done.28), kind=kOutput, calls=%fused_computation.249 | convolution fusion | flops 1236264960 | bytes 76537856 | tf_op jit(solution)/shard_map/qhd,kd->hqk/dot_general | solution.py:237
  337.3 31.8 %fusion.215 = bf16[12,512,1536]{1,2,0:T(8,128)(2,1)} fusion(f32[1536,512,12]{1,0,2:T(8,128)} %get-tuple-element.120, f32[12,512,1536]{1,2,0:T(8,128)} %get-tuple-element.111, f32[12,512]{1,0:T(8,128)S(1)} %get-tuple-element.119, f32[12,512]{1,0:T(8,128)S(1)} %log_add_fusion.1), kind=kLoop, calls=%fused_computation.251 | loop fusion | flops 37748736 | bytes 94420992 | tf_op jit(solution)/shard_map/convert_element_type | solution.py:241
  369.1 13.0 fusion.288
  386.6 19.6 fusion.237
  406.2 20.9 fusion.211
  427.3 21.3 fusion.301
  448.6 33.8 %fusion.208 = (f32[12,512]{1,0:T(8,128)S(1)}, f32[2048,512,12]{1,0,2:T(8,128)}) fusion(f32[12,512]{1,0:T(8,128)S(1)} %log_add_fusion, f32[2048,512,12]{1,0,2:T(8,128)} %get-tuple-element.109, pred[512,2048]{0,1:T(8,128)(4,1)S(1)} %copy-done.7, bf16[512,12,64]{0,2,1:T(8,128)(2,1)S(1)} %bitcast.477, bf16[2048,128]{0,1:T(8,128)(2,1)S(1)} %copy-done.29), kind=kOutput, calls=%fused_computation.237 | convolution fusion | flops 1673521152 | bytes 102817792 | tf_op jit(solution)/shard_map/qhd,kd->hqk/dot_general | solution.py:237
  482.4 40.8 %fusion.210 = bf16[12,512,2048]{1,2,0:T(8,128)(2,1)} fusion(f32[2048,512,12]{1,0,2:T(8,128)} %get-tuple-element.118, f32[12,512]{1,0:T(8,128)S(1)} %get-tuple-element.117, f32[12,512]{1,0:T(8,128)S(1)} %log_add_fusion, f32[2048,512,12]{1,0,2:T(8,128)} %get-tuple-element.109, pred[512,2048]{0,1:T(8,128)(4,1)S(1)} %copy-done.7), kind=kLoop, calls=%fused_computation.239 | loop fusion | flops 75497472 | bytes 126926848 | tf_op jit(solution)/shard_map/convert_element_type | solution.py:241
  523.3 10.5 multiply_bitcast_fusion
  533.9 12.8 fusion.290
  562.2 21.0 fusion.291
  595.9 70.5 %multiply_convert_fusion = (bf16[2048,3072]{1,0:T(8,128)(2,1)}, f32[2048,3072]{1,0:T(8,128)}, f32[2048,3072]{1,0:T(8,128)}) fusion(f32[3072]{0:T(1024)S(1)} %copy-done.95, bf16[768,3072]{1,0:T(8,128)(2,1)} %all-gather.13.cloned.1.call-done, bf16[2048,768]{1,0:T(8,128)(2,1)S(1)} %copy-done.5, f32[768]{0:T(1024)S(1)} %copy-done.97, f32[768]{0:T(1024)S(1)} %copy-done.82, ...), kind=kOutput, calls=%fused_computation.270 | convolution fusion | flops 10088349696 | bytes 70813696 | tf_op jit(solution)/shard_map/dot_general | solution.py:199
  666.4 34.2 %convert_reduce_fusion = (f32[3072]{0:T(1024)}, bf16[2048,3072]{1,0:T(8,128)(2,1)}) fusion(f32[2048,3072]{1,0:T(8,128)} %get-tuple-element.69, bf16[2048,768]{1,0:T(8,128)(2,1)} %param.30, bf16[3072,768]{1,0:T(8,128)(2,1)} %all-gather.15.cloned.1.call-done, f32[2048,3072]{1,0:T(8,128)} %get-tuple-element.116, f32[3072]{0:T(1024)S(1)} %copy-done.95), kind=kOutput, calls=%fused_computation.266 | convolution fusion | flops 9770628096 | bytes 70803456 | tf_op jit(solution)/shard_map/dot_general | solution.py:52
  700.6 16.1 fusion.373
  716.6 13.3 fusion.427
  731.2 794.8 %all-reduce.27.cloned.1.call-done = (f32[8,4,24,768]{3,2,1,0:T(8,128)}, f32[8,4,24,128]{3,2,1,0:T(8,128)}, f32[8,4,24,768]{3,2,1,0:T(8,128)}, f32[8,4,24,3072]{3,2,1,0:T(8,128)}, f32[8,4,96,768]{3,2,1,0:T(8,128)}) async-done(((f32[8,4,24,768]{3,2,1,0:T(8,128)}, f32[8,4,24,128]{3,2,1,0:T(8,128)}, f32[8,4,24,768]{3,2,1,0:T(8,128)}, f32[8,4,24,3072]{3,2,1,0:T(8,128)}, f32[8,4,96,768]{3,2,1,0:T(8,128)}), ...) | async-done | bytes 23986192
  1541.7 21.1 reduce-scatter.15.cloned.1.call-done
  1564.4 36.2 %reduce-scatter.17.cloned.1.call-done = f32[1,1,24,768]{3,2,1,0:T(8,128)} async-done(((f32[8,1,24,768]{3,2,1,0:T(8,128)}), f32[1,1,24,768]{3,2,1,0:T(8,128)}) %reduce-scatter.17.cloned.1.call-update) | async-done | bytes 73744 | tf_op jit(solution)/shard_map/reduce_scatter | solution.py:299
  1602.2 44.7 %reduce-scatter.21.cloned.1.call-done = f32[1,1,96,768]{3,2,1,0:T(8,128)} async-done(((f32[8,1,96,768]{3,2,1,0:T(8,128)}), f32[1,1,96,768]{3,2,1,0:T(8,128)}) %reduce-scatter.21.cloned.1.call-update) | async-done | bytes 294928 | tf_op jit(solution)/shard_map/reduce_scatter | solution.py:299
  1648.7 44.6 %reduce-scatter.19.cloned.1.call-done = f32[1,1,24,3072]{3,2,1,0:T(8,128)} async-done(((f32[8,1,24,3072]{3,2,1,0:T(8,128)}), f32[1,1,24,3072]{3,2,1,0:T(8,128)}) %reduce-scatter.19.cloned.1.call-update) | async-done | bytes 294928 | tf_op jit(solution)/shard_map/reduce_scatter | solution.py:299
  1695.1 33.8 %reduce-scatter.23.cloned.1.call-done = f32[1,1,24,128]{3,2,1,0:T(8,128)} async-done(((f32[8,1,24,128]{3,2,1,0:T(8,128)}), f32[1,1,24,128]{3,2,1,0:T(8,128)}) %reduce-scatter.23.cloned.1.call-update) | async-done | bytes 12304
  1729.6 70.8 %all_gather.56 = f32[768,128]{1,0:T(8,128)S(1)} all-gather(f32[24,128]{1,0:T(8,128)S(1)} %bitcast_add_fusion.18), channel_id=1, replica_groups=mesh['wide'=8,'narrow'=4] {'wide','narrow'}, dimensions={0}, use_global_device_ids=true | all-gather | bytes 405504 | tf_op jit(solution)/shard_map/all_gather | solution.py:306
  1801.7 98.4 %conditional.5 = (f32[768,768]{1,0:T(8,128)S(1)}) conditional(s32[]{:T(128)} %convert_element_type.166, () %tuple.38, f32[768,768]{1,0:T(8,128)} %all-gather.17.cloned.1.call-done), branch_computations={%region_31.32_spmd, %region_32.34_spmd} | conditional | flops 81554964480 | bytes 106168392 | solution.py:309
  1805.3 8.4 fusion.40
  1819.6 6.4 multiply_add_fusion.4
  1875.1 6.4 multiply_add_fusion.1
  1887.4 6.4 fusion.396
  1900.1 15.6 conditional.7
  1919.8 15.1 all-gather.23.cloned.1.call-done
  1934.9 11.6 conditional.9
  1950.7 68.5 %all-gather.21.cloned.1.call-done = f32[768,3072]{1,0:T(8,128)} async-done(((f32[24,3072]{1,0:T(8,128)}), f32[768,3072]{1,0:T(8,128)}) %all-gather.21.cloned.1.call-update) | async-done | bytes 9437200 | tf_op jit(solution)/shard_map/all_gather | solution.py:306
  2019.2 14.0 conditional.8
  2049.4 14.5 fusion.425
  2079.5 312.2 %psum.47 = f32[8576]{0:T(1024)S(1)} all-reduce(f32[8576]{0:T(1024)S(1)} %constant_dynamic-update-slice_fusion), channel_id=1, replica_groups=mesh['wide'=8,'narrow'=4] {'wide','narrow'}, use_global_device_ids=true, to_apply=%region_59.60 | all-reduce | flops 8576 | bytes 68608 | tf_op jit(solution)/shard_map/psum | solution.py:287
  2392.4 17.6 fusion.269
  2410.0 282.3 %all-reduce.25.cloned.1.call-done = (f32[768,768]{1,0:T(8,128)}, f32[768,128]{1,0:T(8,128)}, f32[768,768]{1,0:T(8,128)}, f32[768,3072]{1,0:T(8,128)}, f32[3072,768]{1,0:T(8,128)}) async-done(((f32[768,768]{1,0:T(8,128)}, f32[768,128]{1,0:T(8,128)}, f32[768,768]{1,0:T(8,128)}, f32[768,3072]{1,0:T(8,128)}, f32[3072,768]{1,0:T(8,128)}), (f32[768,768]{1,0:T(8,128)}, f32[768,128]{1,0:T(8,128)}, ...) | async-done | bytes 23986192 | tf_op jit(solution)/shard_map/psum | solution.py:38
  (366 shorter events, 269.6 us)
Async XLA Ops:
  7.2 14.3 copy-start.4
  7.2 15.4 copy-start.90
  7.2 16.0 copy-start.92
  7.2 107.1 %all-gather.9.cloned.1.call-start = ((), (), s32[]{:S(2)}) async-start(), calls=%async_computation.5 | async-start | bytes 1216512 | tf_op jit(solution)/shard_map/all_gather | solution.py:147
  8.9 123.7 %all-gather.11.cloned.1.call-start = ((), (), s32[]{:S(2)}) async-start(), calls=%async_computation.6 | async-start | bytes 1216512 | tf_op jit(solution)/shard_map/all_gather | solution.py:147
  10.5 585.3 %all-gather.13.cloned.1.call-start = ((), (), s32[]{:S(2)}) async-start(), calls=%async_computation.7 | async-start | bytes 4866048 | tf_op jit(solution)/shard_map/all_gather | solution.py:147
  12.2 654.2 %all-gather.15.cloned.1.call-start = ((), (), s32[]{:S(2)}) async-start(), calls=%async_computation.8 | async-start | bytes 4866048 | tf_op jit(solution)/shard_map/all_gather | solution.py:147
  14.0 1512.0 %all-reduce.27.cloned.1.call-start = ((), (), s32[]{:S(2)}) async-start(), calls=%async_computation.19 | async-start | bytes 47972352
  25.1 76.5 %copy-start.15 = (bf16[2048,768]{1,0:T(8,128)(2,1)}, bf16[2048,768]{1,0:T(8,128)(2,1)S(1)}, u32[]{:S(2)}) copy-start(bf16[2048,768]{1,0:T(8,128)(2,1)S(1)} %fusion.260) | copy-start | bytes 9437188
  263.8 14.8 copy-start.28
  278.6 15.4 copy-start.18
  406.2 21.0 copy-start.29
  427.2 55.2 %copy-start.65 = (f32[12,512]{1,0:T(8,128)}, f32[12,512]{1,0:T(8,128)S(1)}, u32[]{:S(2)}) copy-start(f32[12,512]{1,0:T(8,128)S(1)} %log_add_fusion) | copy-start | bytes 73732
  427.2 21.3 copy-start.30
  562.2 22.2 copy-start.17
  562.2 25.4 copy-start.26
  700.6 16.1 copy-start.38
  700.6 16.1 copy-start.103
  730.0 832.8 %reduce-scatter.15.cloned.1.call-start = ((), (), s32[]{:S(2)}) async-start(), calls=%async_computation.9 | async-start | bytes 663552 | tf_op jit(solution)/shard_map/reduce_scatter | solution.py:299
  1528.6 72.1 %reduce-scatter.17.cloned.1.call-start = ((), (), s32[]{:S(2)}) async-start(), calls=%async_computation.10 | async-start | bytes 663552 | tf_op jit(solution)/shard_map/reduce_scatter | solution.py:299
  1531.2 115.7 %reduce-scatter.21.cloned.1.call-start = ((), (), s32[]{:S(2)}) async-start(), calls=%async_computation.12 | async-start | bytes 2654208 | tf_op jit(solution)/shard_map/reduce_scatter | solution.py:299
  1535.1 27.7 %copy-start.80 = (f32[24,768]{1,0:T(8,128)S(1)}, f32[24,768]{1,0:T(8,128)}, u32[]{:S(2)}) copy-start(f32[24,768]{1,0:T(8,128)} %param.36) | copy-start | bytes 221188
  1535.1 65.5 %copy-start.81 = (f32[24,768]{1,0:T(8,128)S(1)}, f32[24,768]{1,0:T(8,128)}, u32[]{:S(2)}) copy-start(f32[24,768]{1,0:T(8,128)} %param.38) | copy-start | bytes 221188
  1535.1 111.8 %copy-start.69 = (f32[96,768]{1,0:T(8,128)S(1)}, f32[96,768]{1,0:T(8,128)}, u32[]{:S(2)}) copy-start(f32[96,768]{1,0:T(8,128)} %param.40) | copy-start | bytes 884740
  1535.1 158.2 %copy-start.70 = (f32[24,3072]{1,0:T(8,128)S(1)}, f32[24,3072]{1,0:T(8,128)}, u32[]{:S(2)}) copy-start(f32[24,3072]{1,0:T(8,128)} %param.39) | copy-start | bytes 884740
  1535.1 158.2 %reduce-scatter.19.cloned.1.call-start = ((), (), s32[]{:S(2)}) async-start(), calls=%async_computation.11 | async-start | bytes 2654208 | tf_op jit(solution)/shard_map/reduce_scatter | solution.py:299
  1535.2 193.7 %copy-start.96 = (f32[24,128]{1,0:T(8,128)S(1)}, f32[24,128]{1,0:T(8,128)}, u32[]{:S(2)}) copy-start(f32[24,128]{1,0:T(8,128)} %param.37) | copy-start | bytes 36868
  1539.3 189.6 %reduce-scatter.23.cloned.1.call-start = ((), (), s32[]{:S(2)}) async-start(), calls=%async_computation.17 | async-start | bytes 110592
  1541.6 260.1 %all-gather.17.cloned.1.call-start = ((), (), s32[]{:S(2)}) async-start(), calls=%async_computation.13 | async-start | bytes 2433024 | tf_op jit(solution)/shard_map/all_gather | solution.py:306
  1564.3 335.7 %all-gather.19.cloned.1.call-start = ((), (), s32[]{:S(2)}) async-start(), calls=%async_computation.14 | async-start | bytes 2433024 | tf_op jit(solution)/shard_map/all_gather | solution.py:306
  1602.2 332.7 %all-gather.23.cloned.1.call-start = ((), (), s32[]{:S(2)}) async-start(), calls=%async_computation.16 | async-start | bytes 9732096 | tf_op jit(solution)/shard_map/all_gather | solution.py:306
  1648.6 370.5 %all-gather.21.cloned.1.call-start = ((), (), s32[]{:S(2)}) async-start(), calls=%async_computation.15 | async-start | bytes 9732096 | tf_op jit(solution)/shard_map/all_gather | solution.py:306
  1695.1 997.2 %all-reduce.25.cloned.1.call-start = ((), (), s32[]{:S(2)}) async-start(), calls=%async_computation.18 | async-start | bytes 47972352 | tf_op jit(solution)/shard_map/psum | solution.py:38
  1729.6 70.8 %copy-start.84 = (f32[24,128]{1,0:T(8,128)}, f32[24,128]{1,0:T(8,128)S(1)}, u32[]{:S(2)}) copy-start(f32[24,128]{1,0:T(8,128)S(1)} %bitcast_add_fusion.18) | copy-start | bytes 36868
  2049.3 14.5 copy-start.6
  2049.4 14.5 copy-start.46
  2049.4 14.5 copy-start.55
  2049.4 14.5 copy-start.68
  2049.4 14.5 copy-start.76
  2049.4 14.5 copy-start.83
  2073.2 318.5 %copy-start.77 = (f32[5504]{0:T(1024)S(1)}, f32[5504]{0:T(1024)}, u32[]{:S(2)}) copy-start(f32[5504]{0:T(1024)} %param.43) | copy-start | bytes 66052
  2073.2 318.5 %copy-start.87 = (f32[8576]{0:T(1024)S(1)}, f32[8576]{0:T(1024)}, u32[]{:S(2)}) copy-start(f32[8576]{0:T(1024)} %param.45) | copy-start | bytes 102916
  2073.2 318.5 %copy-start.88 = (f32[8576]{0:T(1024)S(1)}, f32[8576]{0:T(1024)}, u32[]{:S(2)}) copy-start(f32[8576]{0:T(1024)} %param.44) | copy-start | bytes 102916
  2073.3 319.2 %copy-start.98 = (f32[768]{0:T(1024)S(1)}, f32[768]{0:T(1024)}, u32[]{:S(2)}) copy-start(f32[768]{0:T(1024)} %get-tuple-element.95) | copy-start | bytes 9220
  2073.3 319.1 %copy-start.99 = (f32[768]{0:T(1024)S(1)}, f32[768]{0:T(1024)}, u32[]{:S(2)}) copy-start(f32[768]{0:T(1024)} %get-tuple-element.97) | copy-start | bytes 9220
  2392.4 299.8 %copy-start.86 = (f32[24,128]{1,0:T(8,128)S(1)}, f32[24,128]{1,0:T(8,128)}, u32[]{:S(2)}) copy-start(f32[24,128]{1,0:T(8,128)} %param.32) | copy-start | bytes 36868
  2392.4 301.1 %copy-start.51 = (f32[24,3072]{1,0:T(8,128)S(1)}, f32[24,3072]{1,0:T(8,128)}, u32[]{:S(2)}) copy-start(f32[24,3072]{1,0:T(8,128)} %param.34) | copy-start | bytes 884740
  2392.4 302.9 %copy-start.71 = (f32[24,768]{1,0:T(8,128)S(1)}, f32[24,768]{1,0:T(8,128)}, u32[]{:S(2)}) copy-start(f32[24,768]{1,0:T(8,128)} %param.31) | copy-start | bytes 221188
  (67 other events, 365.9 us)
Sparse Core Ops, SparseCore 0:
  11.4 57.0 all-gather.8
  71.8 52.7 all-gather.10
  128.1 62.6 all-gather.12
  193.9 62.3 all-gather.14
  730.1 795.8 all-reduce.26
  1529.2 33.4 reduce-scatter.14
  1566.2 34.3 reduce-scatter.16
  1604.3 42.5 reduce-scatter.20
  1650.8 42.4 reduce-scatter.18
  1696.5 32.3 reduce-scatter.22
  1732.7 57.6 all-gather.16
  1794.0 56.1 all-gather.18
  1853.9 80.9 all-gather.22
  1938.5 80.6 all-gather.20
  2038.6 653.6 all-reduce.24
where the time goes:
time: 2710 us
  waiting for transfers between devices  1340 us (49%)
  matrix products  587 us (22%)
  blocking collectives  455 us (17%)
  other arithmetic  222 us (8%)
  local copies, waits for them, and re-layouts  53 us (2%)
  loops' own time  32 us (1%)
    unnamed x17, waiting for transfers between devices  829 us
    psum x1, blocking collectives, per_device(): vector_grad = lax.psum(local_vector, ('wide', 'narrow'))  312 us
    psum x1, waiting for transfers between devices, broadcast(): return lax.psum(jnp.where(mine, x, jnp.zeros_like(x)), axis)  282 us
    reduce_scatter x4, waiting for transfers between devices, per_device(): lax.psum_scatter(group_sums, 'wide', scatter_dimension=0, tiled=True)  147 us
    convert_element_type x4, other arithmetic, per_device(): grad_scores = (attn_probs * (grad_probs - row_delta)).astype(jnp.bfloat16)  98 us
    dot_general x15, matrix products, matmul(): jnp.dot(left, right, precision=HIGHEST, preferred_element_type=jnp.float32)  94.5 us
    dot_general x4, matrix products, per_device(): jnp.einsum('qhd,kd->hqk', grad_rows, values_low[:key_end], preferred_elem...  89.3 us
    all_gather x4, waiting for transfers between devices, per_device(): lax.all_gather(new_momenta, ('wide', 'narrow'), axis=0, tiled=True)  83.6 us
  transfers between devices with their start and end apart: 15, of which 9 were waited for; matrix products, arithmetic and copies ran while one was open for 28% of the time, Pallas kernels for 0%

commit v1 on v0

v1 whole, which is shorter than its diff:
```python
from functools import partial
import math

import jax
import jax.numpy as jnp
from jax import lax
from jax.experimental import pallas as pl
from jax.experimental.pallas import tpu as pltpu
from jax.sharding import Mesh, PartitionSpec as P

D = 768
HEADS = 12
HEAD_DIM = 64
ROT = 16
FF = 3072
TOK = 2048
NS_STEPS = 5
STEP = 10
QB = 512
HALF = 256
NH = 4
GROUP = NH * HEAD_DIM
FC = 768
BF = jnp.bfloat16
F32 = jnp.float32
LOG2E = 1.4426950408889634
MIB = 1024 * 1024


def dot(a, b):
    return jnp.dot(a, b, preferred_element_type=F32)


def dot_nt(a, b):
    return lax.dot_general(a, b, (((1,), (1,)), ((), ())), preferred_element_type=F32)


def dot_tn(a, b):
    return lax.dot_general(a, b, (((0,), (0,)), ((), ())), preferred_element_type=F32)


def attention_kernel(opening, closing, *refs):
    first_ref, q_ref, do_ref, cos_ref, sin_ref, kv_ref = refs[:6]
    start_ref = None if opening else refs[9]
    refs = refs[7:] if opening else refs[10:]
    mix_ref, dq_ref, dkv_ref = refs[:3]
    refs = refs[3:]
    if closing:
        gkv_ref = refs[0]
        refs = refs[1:]
    (k_ref, kt_ref, vx_ref, vt_ref, qz_ref, e_even, e_odd, acc_ref, m_ref, mh_ref, rhs_ref, dl_ref,
     dqa_ref) = refs
    e_ref = (e_even, e_odd)
    hg = pl.program_id(0)
    qi = pl.program_id(1)
    first = first_ref[qi]
    diag = pl.multiple_of(qi * QB, QB)
    here = pl.ds(diag, QB)

    @pl.when((hg == 0) & (qi == 0))
    def _():
        dkv_ref[...] = jnp.zeros_like(dkv_ref) if opening else start_ref[...]
        filler = jnp.where(lax.broadcasted_iota(jnp.int32, (HEAD_DIM, QB), 0) < 2, 1.0, 0.0)
        for j in range(TOK // QB):
            cols = slice(j * QB, (j + 1) * QB)
            c, s = cos_ref[:, cols], sin_ref[:, cols]
            u = kv_ref[0:HEAD_DIM, cols]
            v = kv_ref[HEAD_DIM:, cols]
            k = jnp.concatenate(
                [u[0:8] * c - u[8:16] * s, u[8:16] * c + u[0:8] * s, u[16:]], axis=0
            )
            kt_ref[:, cols] = k.astype(BF)
            vt_ref[0:HEAD_DIM, cols] = v.astype(BF)
            vt_ref[HEAD_DIM:, cols] = jnp.ones((16, QB), BF)
            both = jnp.concatenate([k, v], axis=0).T
            k_ref[cols, :] = both[:, 0:HEAD_DIM].astype(BF)
            vx_ref[cols, :] = jnp.concatenate([filler, v], axis=0).T.astype(BF)

    cos = cos_ref[:, here]
    sin = sin_ref[:, here]
    scale = LOG2E / math.sqrt(HEAD_DIM)
    for h in range(NH):
        u = q_ref[h * HEAD_DIM : (h + 1) * HEAD_DIM, :]
        a, b = u[0:8], u[8:16]
        turned = jnp.concatenate([a * cos - b * sin, b * cos + a * sin, u[16:]], axis=0)
        qz_ref[h, 0:HEAD_DIM, :] = (turned * scale).astype(BF)
        qz_ref[h, HEAD_DIM:, :] = jnp.zeros((HEAD_DIM, QB), BF)

    def edge_mask(c):
        shape = ((c + 1) * HALF, HALF)
        keys_in = lax.broadcasted_iota(jnp.int32, shape, 0)
        return keys_in <= lax.broadcasted_iota(jnp.int32, shape, 1) + c * HALF

    row16 = lax.broadcasted_iota(jnp.int32, (HEAD_DIM, QB), 0)
    zeros = jnp.zeros((HEAD_DIM, QB), BF)

    def edges(h, c):
        q = qz_ref[h, 0:HEAD_DIM, c * HALF : (c + 1) * HALF]
        s = dot(k_ref[pl.ds(diag, (c + 1) * HALF), :], q)
        return jnp.where(edge_mask(c), s, -1e30)

    def forward_diagonal(h, s, c):
        cols = slice(c * HALF, (c + 1) * HALF)
        rows = pl.ds(diag, (c + 1) * HALF)
        m = jnp.max(s, axis=0, keepdims=True)
        e = jnp.exp2(s - m).astype(BF)
        e_ref[h % 2][rows, cols] = e
        acc_ref[h, :, cols] = dot(vt_ref[:, rows], e)
        m_ref[h, :, cols] = m

    def forward(h, s, off, j):
        m_old = m_ref[h]
        m = jnp.maximum(m_old, jnp.max(s, axis=0, keepdims=True))
        e = jnp.exp2(s - m).astype(BF)
        e_ref[h % 2][pl.ds(off, QB), :] = e
        acc_ref[h] = acc_ref[h] * jnp.exp2(m_old - m) + dot(vt_ref[:, pl.ds(off, QB)], e)
        m_ref[h] = m
        mh_ref[j, h] = m

    def between(h):
        rows = slice(h * HEAD_DIM, (h + 1) * HEAD_DIM)
        inv = 1.0 / acc_ref[h, HEAD_DIM : HEAD_DIM + 1, :]
        mixed = acc_ref[h, 0:HEAD_DIM, :] * inv
        mix_ref[rows, :] = mixed.astype(BF)
        do = do_ref[rows, :].astype(F32)
        delta = jnp.sum(do * mixed, axis=0, keepdims=True)
        rhs_ref[h] = do * inv
        dl_ref[h] = -(delta * inv)

    def scaled(h, j):
        r = jnp.exp2(mh_ref[j, h] - m_ref[h])
        dop = (rhs_ref[h] * r).astype(BF)
        dl = dl_ref[h] * r
        hi = dl.astype(BF).astype(F32)
        lo = dl - hi
        head = jnp.where(row16 == 0, hi, jnp.where(row16 == 1, lo, 0.0)).astype(BF)
        return jnp.concatenate([head, dop], axis=0), jnp.concatenate([zeros, dop], axis=0)

    def backward_diagonal(h, rhs, rz, c):
        cols = slice(c * HALF, (c + 1) * HALF)
        rows = pl.ds(diag, (c + 1) * HALF)
        x = dot(vx_ref[rows, :], rhs[:, cols])
        e = e_ref[h % 2][rows, cols]
        ds = e * x.astype(BF)
        dqa_ref[h, :, cols] = dot(kt_ref[:, rows], ds)
        dkv_ref[rows, :] += dot_nt(ds, qz_ref[h, :, cols]) + dot_nt(e, rz[:, cols])

    def backward(h, x, rz, off):
        e = e_ref[h % 2][pl.ds(off, QB), :]
        ds = e * x.astype(BF)
        dqa_ref[h] += dot(kt_ref[:, pl.ds(off, QB)], ds)
        dkv_ref[pl.ds(off, QB), :] += dot_nt(ds, qz_ref[h]) + dot_nt(e, rz)

    for h in range(NH + 1):
        ahead, behind = h < NH, h > 0
        if behind:
            rhs, rz = scaled(h - 1, qi)
        for c in range(2):
            if ahead:
                parts = edges(h, c)
            if behind:
                backward_diagonal(h - 1, rhs, rz, c)
            if ahead:
                forward_diagonal(h, parts, c)
        if ahead:
            mh_ref[qi, h] = m_ref[h]

        def block(j, carry, h=h, ahead=ahead, behind=behind):
            off = pl.multiple_of(j * QB, QB)
            if ahead:
                s = dot(k_ref[pl.ds(off, QB), :], qz_ref[h, 0:HEAD_DIM, :])
            if behind:
                rhs, rz = scaled(h - 1, j)
                x = dot(vx_ref[pl.ds(off, QB), :], rhs)
                backward(h - 1, x, rz, off)
            if ahead:
                forward(h, s, off, j)
            return carry

        lax.fori_loop(first, qi, block, 0)
        if ahead:
            between(h)

    for h in range(NH):
        u = dqa_ref[h] * (1.0 / math.sqrt(HEAD_DIM))
        a, b = u[0:8], u[8:16]
        turned = jnp.concatenate([a * cos + b * sin, b * cos - a * sin, u[16:]], axis=0)
        dq_ref[h * HEAD_DIM : (h + 1) * HEAD_DIM, :] = turned.astype(BF)

    if closing:

        @pl.when((hg == pl.num_programs(0) - 1) & (qi == pl.num_programs(1) - 1))
        def _():
            for j in range(TOK // QB):
                cols = slice(j * QB, (j + 1) * QB)
                c, s = cos_ref[:, cols], sin_ref[:, cols]
                t = dkv_ref[cols, :].T
                u = t[0:HEAD_DIM] * math.log(2.0)
                k = jnp.concatenate(
                    [u[0:8] * c + u[8:16] * s, u[8:16] * c - u[0:8] * s, u[16:], t[HEAD_DIM:]], axis=0
                )
                gkv_ref[:, cols] = k.astype(BF)


def attention(first, qkv_t, grad_mixed, cos, sin, after, group_lo, groups, so_far):
    blocks = TOK // QB
    opening, closing = so_far is None, (group_lo + groups) * GROUP == D
    group_block = pl.BlockSpec((GROUP, QB), lambda g, i, f: (group_lo + g, i))

    def whole(shape, row=0):
        return pl.BlockSpec(shape, lambda g, i, f: (row, 0))

    anywhere = pl.BlockSpec(memory_space=pl.ANY)
    in_specs = [
        group_block, group_block, whole((8, TOK)), whole((8, TOK)), whole((128, TOK), D // 128), anywhere,
    ]
    operands = [first, qkv_t, grad_mixed, cos, sin, qkv_t, after]
    aliases = {}
    if not opening:
        in_specs += [anywhere, anywhere, whole((TOK, 128))]
        operands += list(so_far)
        aliases = {7: 0, 8: 1}
    out_specs = [group_block, group_block, whole((TOK, 128))]
    out_shape = [
        jax.ShapeDtypeStruct((D, TOK), BF),
        jax.ShapeDtypeStruct((D, TOK), BF),
        jax.ShapeDtypeStruct((TOK, 128), F32),
    ]
    if closing:
        out_specs.append(whole((128, TOK)))
        out_shape.append(jax.ShapeDtypeStruct((128, TOK), BF))
    return pl.pallas_call(
        partial(attention_kernel, opening, closing),
        grid_spec=pltpu.PrefetchScalarGridSpec(
            num_scalar_prefetch=1,
            grid=(groups, blocks),
            in_specs=in_specs,
            out_specs=out_specs,
            scratch_shapes=[
                pltpu.VMEM((TOK, HEAD_DIM), BF),
                pltpu.VMEM((HEAD_DIM, TOK), BF),
                pltpu.VMEM((TOK, 128), BF),
                pltpu.VMEM((80, TOK), BF),
                pltpu.VMEM((NH, 128, QB), BF),
                pltpu.VMEM((TOK, QB), BF),
                pltpu.VMEM((TOK, QB), BF),
                pltpu.VMEM((NH, 80, QB), F32),
                pltpu.VMEM((NH, 1, QB), F32),
                pltpu.VMEM((blocks, NH, 1, QB), F32),
                pltpu.VMEM((NH, HEAD_DIM, QB), F32),
                pltpu.VMEM((NH, 1, QB), F32),
                pltpu.VMEM((NH, HEAD_DIM, QB), F32),
            ],
        ),
        out_shape=out_shape,
        input_output_aliases=aliases,
        compiler_params=pltpu.CompilerParams(
            dimension_semantics=("arbitrary", "arbitrary"), vmem_limit_bytes=48 * MIB
        ),
        cost_estimate=pl.CostEstimate(
            flops=groups * NH * 6 * 2 * TOK * TOK // 2 * 256,
            bytes_accessed=groups * GROUP * TOK * 10,
            transcendentals=groups * NH * TOK * TOK // 2,
        ),
        name="attention",
    )(*operands)


ERF = (0.254829592, -0.284496736, 1.421413741, -1.453152027, 1.061405429)


def gelu_pair(x):
    e = jnp.exp2(x * x * (-0.5 * LOG2E))
    den = 1.0 + (0.3275911 / math.sqrt(2.0)) * jnp.abs(x)
    t = 1.0 / den
    p = ERF[4]
    for c in (ERF[3], ERF[2], ERF[1], ERF[0]):
        p = p * t + c
    tail = (0.5 * p) * (t * e)
    phi = jnp.where(x >= 0.0, 1.0 - tail, tail)
    return phi, phi + x * (e * (1.0 / math.sqrt(2.0 * math.pi)))


def ffn_kernel(
    x_ref, xt_ref, g_ref, gt_ref, up_ref, down_ref, bias_ref, _,
    y_ref, dx_ref, dup_ref, ddown_ref, db_ref,
    pre_ref, grad_ref, act_ref, de_ref, dn_ref,
):
    tile = TOK // 2
    part = 256

    @pl.when(pl.program_id(0) == 0)
    def _():
        y_ref[...] = jnp.zeros_like(y_ref)
        dx_ref[...] = jnp.zeros_like(dx_ref)

    fold = FC // 4
    for q in range(4):
        dn_ref[q * fold : (q + 1) * fold, :] = down_ref[:, q * D : (q + 1) * D]

    for t in range(TOK // tile):
        rows = slice(t * tile, (t + 1) * tile)
        pre_ref[rows, :] = dot(x_ref[rows, :], up_ref[...])
        grad_ref[rows, :] = dot_nt(g_ref[rows, :], dn_ref[...])
    db = jnp.zeros((1, FC), F32)
    for t in range(TOK // tile):
        rows = slice(t * tile, (t + 1) * tile)
        for lo in range(t * tile, (t + 1) * tile, part):
            some = slice(lo, lo + part)
            pre = pre_ref[some, :] + bias_ref[...]
            phi, slope = gelu_pair(pre)
            act_ref[some, :] = (pre * phi).astype(BF)
            d = slope * grad_ref[some, :]
            db = db + jnp.sum(d, axis=0, keepdims=True)
            de_ref[some, :] = d.astype(BF)
        y_ref[rows, :] += dot(act_ref[rows, :], dn_ref[...])
        dx_ref[rows, :] += dot_nt(de_ref[rows, :], up_ref[...])
    db_ref[...] = db
    dup_ref[...] = dot(xt_ref[...], de_ref[...]).astype(BF)
    dd = dot(gt_ref[...], act_ref[...]).T.astype(BF)
    for q in range(4):
        ddown_ref[:, q * D : (q + 1) * D] = dd[q * fold : (q + 1) * fold, :]


def ffn(x, xt, g, gt, weights, bias, after):
    once = pl.Buffered(1)

    def whole(shape):
        return pl.BlockSpec(shape, lambda c: (0, 0), pipeline_mode=once)

    return pl.pallas_call(
        ffn_kernel,
        grid=(FF // FC,),
        in_specs=[
            whole((TOK, D)), whole((D, TOK)), whole((TOK, D)), whole((D, TOK)),
            pl.BlockSpec((D, FC), lambda c: (0, c)),
            pl.BlockSpec((FC // 4, FF), lambda c: (c, 1)),
            pl.BlockSpec((1, FC), lambda c: (0, c)),
            pl.BlockSpec(memory_space=pl.ANY),
        ],
        out_specs=[
            whole((TOK, D)), whole((TOK, D)),
            pl.BlockSpec((D, FC), lambda c: (0, c)),
            pl.BlockSpec((FC // 4, FF), lambda c: (c, 0)),
            pl.BlockSpec((1, FC), lambda c: (0, c)),
        ],
        scratch_shapes=[pltpu.VMEM((TOK, FC), F32)] * 2
        + [pltpu.VMEM((TOK, FC), BF)] * 2 + [pltpu.VMEM((FC, D), BF)],
        out_shape=[
            jax.ShapeDtypeStruct((TOK, D), F32),
            jax.ShapeDtypeStruct((TOK, D), F32),
            jax.ShapeDtypeStruct((D, FF), BF),
            jax.ShapeDtypeStruct((D, FF), BF),
            jax.ShapeDtypeStruct((1, FF), F32),
        ],
        compiler_params=pltpu.CompilerParams(
            dimension_semantics=("arbitrary",), vmem_limit_bytes=58 * MIB
        ),
        cost_estimate=pl.CostEstimate(
            flops=12 * TOK * D * FF, bytes_accessed=44 * MIB, transcendentals=2 * TOK * FF
        ),
        name="ffn",
    )(x, xt, g, gt, weights, weights, bias, after)


ROPE_BASE = 10000.0
NORM_EPS = 1e-05
NS_A, NS_B, NS_C = 3.4445, -4.775, 2.0315
MUON_RATE = 0.5
MUON_MOMENTUM = 0.5
ADAM_RATE = 0.3
BETA_FIRST = 0.9
BETA_SECOND = 0.95
ADAM_EPS = 1e-08
QKV = D + 2 * HEAD_DIM


def prepare_kernel(x_ref, g_ref, gain_ref, shift_ref, na_t_ref, nf_ref, nf_t_ref, g_t_ref):
    x = x_ref[...].astype(F32)
    centred = x - jnp.mean(x, axis=-1, keepdims=True)
    hat = centred * lax.rsqrt(jnp.mean(centred * centred, axis=-1, keepdims=True) + NORM_EPS)
    na_t_ref[...] = (hat * gain_ref[0:1, :] + shift_ref[0:1, :]).T.astype(BF)
    nf = hat * gain_ref[1:2, :] + shift_ref[1:2, :]
    nf_ref[...] = nf.astype(BF)
    nf_t_ref[...] = nf.T.astype(BF)
    g_t_ref[...] = g_ref[...].astype(F32).T.astype(BF)


def prepare(x, g, gains, shifts):
    block = 512
    rows = pl.BlockSpec((block, D), lambda i: (i, 0))
    cols = pl.BlockSpec((D, block), lambda i: (0, i))
    fixed = pl.BlockSpec((2, D), lambda i: (0, 0))
    turned = jax.ShapeDtypeStruct((D, TOK), BF)
    return pl.pallas_call(
        prepare_kernel,
        grid=(TOK // block,),
        in_specs=[rows, rows, fixed, fixed],
        out_specs=[cols, rows, cols, cols],
        out_shape=[turned, jax.ShapeDtypeStruct((TOK, D), BF), turned, turned],
        compiler_params=pltpu.CompilerParams(
            dimension_semantics=("arbitrary",), vmem_limit_bytes=48 * MIB
        ),
        cost_estimate=pl.CostEstimate(
            flops=20 * TOK * D, bytes_accessed=12 * TOK * D, transcendentals=TOK
        ),
        name="prepare",
    )(x, g, gains, shifts)


def grads_kernel(g_ref, mix_ref, gq_ref, gkv_ref, nt_ref, dqkv_ref, dout_ref, bsum_ref, qkv_acc, out_acc):
    i = pl.program_id(0)
    gq = gq_ref[...]
    gkv = gkv_ref[...]
    nt = nt_ref[...]

    @pl.when(i == 0)
    def _():
        qkv_acc[...] = jnp.zeros_like(qkv_acc)
        out_acc[...] = jnp.zeros_like(out_acc)
        bsum_ref[...] = jnp.zeros_like(bsum_ref)

    qkv_acc[:, 0:D] += dot_nt(nt, gq)
    qkv_acc[:, D:] += dot_nt(nt, gkv)
    out_acc[...] += dot(mix_ref[...], g_ref[...])
    ones = jnp.ones((8, gq.shape[1]), BF)
    bsum_ref[:, 0:D] += dot_nt(ones, gq)
    bsum_ref[:, D:] += dot_nt(ones, gkv)

    @pl.when(i == pl.num_programs(0) - 1)
    def _():
        dqkv_ref[...] = qkv_acc[...].astype(BF)
        dout_ref[...] = out_acc[...].astype(BF)


def grads(g, mix, gq, gkv, nt):
    block = 1024
    cols = pl.BlockSpec((D, block), lambda i: (0, i))

    def fixed(shape):
        return pl.BlockSpec(shape, lambda i: (0, 0))

    return pl.pallas_call(
        grads_kernel,
        grid=(TOK // block,),
        in_specs=[
            pl.BlockSpec((block, D), lambda i: (i, 0)), cols, cols,
            pl.BlockSpec((128, block), lambda i: (0, i)), cols,
        ],
        out_specs=[fixed((D, QKV)), fixed((D, D)), fixed((8, QKV))],
        scratch_shapes=[pltpu.VMEM((D, QKV), F32), pltpu.VMEM((D, D), F32)],
        out_shape=[
            jax.ShapeDtypeStruct((D, QKV), BF), jax.ShapeDtypeStruct((D, D), BF),
            jax.ShapeDtypeStruct((8, QKV), F32),
        ],
        compiler_params=pltpu.CompilerParams(
            dimension_semantics=("arbitrary",), vmem_limit_bytes=48 * MIB
        ),
        cost_estimate=pl.CostEstimate(
            flops=2 * TOK * D * (QKV + D), bytes_accessed=16 * MIB, transcendentals=0
        ),
        name="grads",
    )(g, mix, gq, gkv, nt)


def final_kernel(
    x_ref, g_ref, y_ref, df_ref, mix_ref, gq_ref, gkv_ref, wt_ref, wo_ref, gain_ref, bias_ref,
    out_ref, ig_ref, sums_ref,
):
    i = pl.program_id(0)
    x = x_ref[...].astype(F32)
    gf = g_ref[...].astype(F32)

    @pl.when(i == 0)
    def _():
        sums_ref[...] = jnp.zeros_like(sums_ref)

    da = dot_tn(gq_ref[...], wt_ref[0:D, :]) + dot_tn(gkv_ref[...], wt_ref[D:, :])
    out_ref[...] = (x + (dot_tn(mix_ref[...], wo_ref[...]) + y_ref[...] + bias_ref[...])).astype(BF)
    mean = jnp.mean(x, axis=-1, keepdims=True)
    centred = x - mean
    rstd = lax.rsqrt(jnp.mean(centred * centred, axis=-1, keepdims=True) + NORM_EPS)
    hat = centred * rstd
    df = df_ref[...]
    d_hat = da * gain_ref[0:1, :] + df * gain_ref[1:2, :]
    m1 = jnp.mean(d_hat, axis=-1, keepdims=True)
    m2 = jnp.mean(d_hat * hat, axis=-1, keepdims=True)
    ig_ref[...] = gf + rstd * (d_hat - m1 - hat * m2)
    for r, v in enumerate((da * hat, df * hat, da, df, gf)):
        sums_ref[r : r + 1, :] += jnp.sum(v, axis=0, keepdims=True)


def final(x, g, y, d_ffn, mix, gq, gkv, wt, wo, gains, bias):
    block = 512

    def rows(i):
        return (i, 0)

    def cols(i):
        return (0, i)

    def fixed(i):
        return (0, 0)

    return pl.pallas_call(
        final_kernel,
        grid=(TOK // block,),
        in_specs=[
            pl.BlockSpec((block, D), rows), pl.BlockSpec((block, D), rows),
            pl.BlockSpec((block, D), rows), pl.BlockSpec((block, D), rows),
            pl.BlockSpec((D, block), cols), pl.BlockSpec((D, block), cols),
            pl.BlockSpec((128, block), cols),
            pl.BlockSpec((QKV, D), fixed), pl.BlockSpec((D, D), fixed),
            pl.BlockSpec((2, D), fixed), pl.BlockSpec((1, D), fixed),
        ],
        out_specs=[
            pl.BlockSpec((block, D), rows), pl.BlockSpec((block, D), rows), pl.BlockSpec((8, D), fixed),
        ],
        out_shape=[
            jax.ShapeDtypeStruct((TOK, D), BF), jax.ShapeDtypeStruct((TOK, D), F32),
            jax.ShapeDtypeStruct((8, D), F32),
        ],
        compiler_params=pltpu.CompilerParams(
            dimension_semantics=("arbitrary",), vmem_limit_bytes=48 * MIB
        ),
        cost_estimate=pl.CostEstimate(
            flops=2 * TOK * D * (QKV + D), bytes_accessed=36 * MIB, transcendentals=TOK
        ),
        name="closing",
    )(x, g, y, d_ffn, mix, gq, gkv, wt, wo, gains, bias)


def eye_block(rows, n, row_lo):
    r = lax.broadcasted_iota(jnp.int32, (rows, n), 0) + row_lo
    return r == lax.broadcasted_iota(jnp.int32, (rows, n), 1)


def diagonal_sum(ref, n, blk):
    total = 0.0
    for r in range(0, n, blk):
        total += jnp.sum(jnp.where(eye_block(blk, blk, 0), ref[r : r + blk, r : r + blk], 0.0))
    return total


def shift_diagonal(ref, low_ref, level, n, blk):
    for r in range(0, n, blk):
        ref[r : r + blk, r : r + blk] -= jnp.where(eye_block(blk, blk, 0), level, 0.0)
        low_ref[r : r + blk, :] = ref[r : r + blk, :].astype(BF)


def recentre(ref, low_ref, n, blk):
    level = diagonal_sum(ref, n, blk) / n
    shift_diagonal(ref, low_ref, level, n, blk)
    return level


def gram_sweep(level, q0, n, blk, a, al, s, sl, t, tl, u, ul, first=False, last=False):
    p0 = NS_A + NS_B * level + NS_C * level * level
    s[...] = (NS_B + 2.0 * NS_C * level) * a[...] + NS_C * dot(al[...], al[...])
    sl[...] = s[...].astype(BF)
    if first:
        u[...] = s[...]
        q0 = p0
    else:
        u[...] = p0 * u[...] + q0 * s[...] + dot(sl[...], ul[...])
        q0 = p0 * q0
    q0 = q0 + recentre(u, ul, n, blk)
    if last:
        return level, q0
    t[...] = p0 * a[...] + level * s[...] + dot(sl[...], al[...])
    t0 = p0 * level + recentre(t, tl, n, blk)
    a[...] = p0 * t[...] + t0 * s[...] + dot(sl[...], tl[...])
    return p0 * t0 + recentre(a, al, n, blk), q0


def wide_kernel(down_ref, m_ref, u_ref, q_ref, a, al, s, sl, t, tl, u, ul):
    blk = 256

    @pl.when(down_ref[0] == 0)
    def _():
        a[...] = dot_nt(m_ref[...], m_ref[...])

    @pl.when(down_ref[0] != 0)
    def _():
        for q in range(4):
            part = m_ref[:, q * D : (q + 1) * D]
            if q == 0:
                a[...] = dot_tn(part, part)
            else:
                a[...] += dot_tn(part, part)

    inverse = 1.0 / (jnp.sqrt(jnp.full((1, D), diagonal_sum(a, D, blk))) + 1e-07)
    a[...] = a[...] * (inverse * inverse)
    level = recentre(a, al, D, blk)
    state = (a, al, s, sl, t, tl, u, ul)

    def sweep(k, carry):
        return gram_sweep(carry[0], carry[1], D, blk, *state)

    carry = gram_sweep(level, None, D, blk, *state, first=True)
    carry = lax.fori_loop(1, NS_STEPS - 1, sweep, carry)
    _, q0 = gram_sweep(carry[0], carry[1], D, blk, *state, last=True)
    u_ref[...] = (u[...] * inverse).astype(BF)
    q_ref[...] = q0 * inverse


def wide_ns(down, m):
    big, low = pltpu.VMEM((D, D), F32), pltpu.VMEM((D, D), BF)

    def fixed(i, d):
        return (0, 0)

    return pl.pallas_call(
        wide_kernel,
        grid_spec=pltpu.PrefetchScalarGridSpec(
            num_scalar_prefetch=1,
            grid=(1,),
            in_specs=[pl.BlockSpec((D, FF), lambda i, d: (0, d[0]), pipeline_mode=pl.Buffered(1))],
            out_specs=[pl.BlockSpec((D, D), fixed), pl.BlockSpec((1, D), fixed)],
            scratch_shapes=[big, low] * 4,
        ),
        out_shape=[jax.ShapeDtypeStruct((D, D), BF), jax.ShapeDtypeStruct((1, D), F32)],
        compiler_params=pltpu.CompilerParams(vmem_limit_bytes=48 * MIB),
        cost_estimate=pl.CostEstimate(flops=2 * 24 * D**3, bytes_accessed=6 * MIB, transcendentals=D),
        name="wide_ns",
    )(down, m)


def square_kernel(m_ref, kv_ref, o_ref, okv_ref, x, xl, a, al, sl, *small):
    blk = 256
    n = 2 * HEAD_DIM
    m = m_ref[...].astype(F32)
    x[...] = m / (jnp.sqrt(jnp.full((1, D), jnp.sum(m * m))) + 1e-07)
    sa, sal, ss, ssl, st, stl, su, sul = small
    kv = kv_ref[...]
    sa[...] = dot_tn(kv, kv)
    inverse = 1.0 / (jnp.sqrt(jnp.full((1, n), diagonal_sum(sa, n, n))) + 1e-07)
    sa[...] = sa[...] * (inverse * inverse)
    su[...] = jnp.zeros_like(su)
    sul[...] = jnp.zeros_like(sul)
    level = recentre(sa, sal, n, n)

    def sweep(k, carry):
        xl[...] = x[...].astype(BF)
        a[...] = dot_nt(xl[...], xl[...])
        lev = recentre(a, al, D, blk)
        p0 = NS_A + NS_B * lev + NS_C * lev * lev
        small_next = gram_sweep(carry[0], carry[1], n, n, sa, sal, ss, ssl, st, stl, su, sul)
        sl[...] = ((NS_B + 2.0 * NS_C * lev) * a[...] + NS_C * dot(al[...], al[...])).astype(BF)
        x[...] = p0 * x[...] + dot(sl[...], xl[...])
        return small_next

    _, q0 = lax.fori_loop(0, NS_STEPS, sweep, (level, jnp.float32(1.0)))
    o_ref[...] = x[...]
    okv_ref[...] = (q0 * kv.astype(F32) + dot(kv, sul[...])) * inverse


def square_ns(m, kv):
    big, low = pltpu.VMEM((D, D), F32), pltpu.VMEM((D, D), BF)
    n = 2 * HEAD_DIM
    return pl.pallas_call(
        square_kernel,
        in_specs=[pl.BlockSpec(memory_space=pltpu.VMEM)] * 2,
        out_specs=[pl.BlockSpec(memory_space=pltpu.VMEM)] * 2,
        scratch_shapes=[big, low, big, low, low]
        + [pltpu.VMEM((n, n), F32), pltpu.VMEM((n, n), BF)] * 4,
        out_shape=[jax.ShapeDtypeStruct((D, D), F32), jax.ShapeDtypeStruct((D, n), F32)],
        compiler_params=pltpu.CompilerParams(vmem_limit_bytes=48 * MIB),
        cost_estimate=pl.CostEstimate(flops=2 * 17 * D**3, bytes_accessed=6 * MIB, transcendentals=D),
        name="square_ns",
    )(m, kv)


def swap(x, axis, bit):
    return lax.ppermute(x, axis, [(i, i ^ bit) for i in range(lax.axis_size(axis))])


def bits_of(size):
    return [1 << b for b in range(size.bit_length() - 1)]


class Grid:
    def __init__(self):
        chip, narrow = bits_of(lax.axis_size("chip")), bits_of(lax.axis_size("narrow"))
        self.axes = [("chip", b) for b in reversed(chip)] + [("core", 1)]
        self.axes += [("narrow", b) for b in reversed(narrow)]
        self.chip = list(range(len(chip)))
        self.core = len(chip)
        self.narrow = list(range(len(chip) + 1, len(self.axes)))

    def bit(self, place):
        axis, bit = self.axes[place]
        return (lax.axis_index(axis) // bit) % 2

    def swap(self, x, place):
        return swap(x, *self.axes[place])

    def gather(self, x, order):
        x = x.reshape((1,) * len(self.axes) + x.shape)
        for place in order:
            other = self.swap(x, place)
            up = self.bit(place) == 1
            x = jnp.concatenate([jnp.where(up, other, x), jnp.where(up, x, other)], axis=place)
        return x.reshape((-1,) + x.shape[len(self.axes) + 1 :])

    def scatter(self, x, order):
        x = x.reshape((2,) * len(self.axes) + (-1,) + x.shape[1:])
        passed = []
        for place in order:
            bit = self.bit(place)
            away = lax.dynamic_index_in_dim(x, 1 - bit, place, keepdims=True).astype(BF)
            keep = lax.dynamic_index_in_dim(x, bit, place, keepdims=True).astype(F32)
            x = keep + self.swap(away, place).astype(F32)
            passed.append(x)
        return x.reshape((-1,) + x.shape[len(self.axes) + 1 :]), passed


def locate(lengths):
    ends = jnp.cumsum(lengths)
    token_ids = jnp.arange(TOK, dtype=jnp.int32)
    starts = jnp.max(jnp.where(ends[None, :] <= token_ids[:, None], ends[None, :], 0), axis=1)
    return starts, token_ids - starts


def up_columns(x):
    return x.reshape(x.shape[0], FF // FC, FC // 4, 4).swapaxes(2, 3).reshape(x.shape[0], FF)


def up_columns_back(x):
    return x.reshape(x.shape[0], FF // FC, 4, FC // 4).swapaxes(2, 3).reshape(x.shape[0], FF)


def per_device(
    block_input, doc_lengths, cotangent,
    weight_query, weight_keyval, weight_output, weight_expand, weight_reduce,
    momentum_query, momentum_keyval, momentum_output, momentum_expand, momentum_reduce,
    norm_gains, norm_biases, proj_biases, adam_first, adam_second,
):
    grid = Grid()
    chips, narrow = lax.axis_size("chip"), lax.axis_size("narrow")
    devices = 2 * chips * narrow
    core = lax.axis_index("core")
    place = lax.axis_index("chip") * narrow + lax.axis_index("narrow")
    masters = (weight_query, weight_keyval, weight_output, weight_expand, weight_reduce)
    own = D // devices
    up_first = grid.narrow[::-1] + grid.chip[::-1] + [grid.core]
    down_first = grid.narrow[::-1] + grid.chip + [grid.core]

    w_qkv = grid.gather(jnp.concatenate([weight_query, weight_keyval], axis=1).astype(BF), up_first)
    w_out = grid.gather(weight_output.astype(BF), down_first)
    ffn_pack = jnp.concatenate(
        [up_columns(weight_expand), weight_reduce.reshape(own, 4 * D)], axis=1
    ).astype(BF)
    ffn_weights = lax.all_gather(ffn_pack, ("chip", "core", "narrow"), axis=0, tiled=True)
    bias_qkv = proj_biases[:QKV]
    bias_output = proj_biases[QKV : QKV + D]
    bias_expand = proj_biases[QKV + D : QKV + D + FF]
    bias_reduce = proj_biases[QKV + D + FF :]

    n_attn_t, n_ffn, n_ffn_t, g_t = prepare(block_input, cotangent, norm_gains, norm_biases)

    starts, positions = locate(doc_lengths[0])
    frequency = ROPE_BASE ** (-(2.0 * jnp.arange(ROT // 2, dtype=F32)) / ROT)
    angles = positions.astype(F32)[None, :] * frequency[:, None]
    cos, sin = jnp.cos(angles), jnp.sin(angles)
    first_block = starts[::QB] // QB

    qkv_t = dot_tn(w_qkv, n_attn_t) + bias_qkv[:, None]
    grad_mixed_t = dot_nt(w_out, cotangent).astype(BF)
    so_far = attention(first_block, qkv_t, grad_mixed_t, cos, sin, cos, 0, 1, None)
    y, d_ffn, d_up, d_down, d_bias_up = ffn(
        n_ffn, n_ffn_t, cotangent, g_t, ffn_weights, up_columns(bias_expand[None, :]), so_far[0]
    )
    halves = [d.reshape(chips, 2, narrow * own, FF) for d in (d_up, d_down)]
    away = [lax.dynamic_index_in_dim(h, 1 - core, 1, keepdims=False) for h in halves]
    keep = [lax.dynamic_index_in_dim(h, core, 1, keepdims=False) for h in halves]
    halves = [
        (k.astype(F32) + swap(a, "core", 1).astype(F32)).astype(BF) for k, a in zip(keep, away)
    ]
    packed = jnp.concatenate(halves, axis=2).reshape(-1, 2 * FF)
    ffn_grads = lax.psum_scatter(packed, "chip", scatter_dimension=0, tiled=True)

    mix_t, gq_t, _, gkv_t = attention(
        first_block, qkv_t, grad_mixed_t, cos, sin, packed, 1, HEADS // NH - 1, so_far
    )
    ffn_grads, _ = lax.optimization_barrier((ffn_grads, gkv_t))
    ffn_grads = lax.psum_scatter(ffn_grads, "narrow", scatter_dimension=0, tiled=True)
    d_qkv, d_out, bias_sums = grads(cotangent, mix_t, gq_t, gkv_t, n_attn_t)
    scatter_up = [grid.core] + grid.chip + grid.narrow
    scatter_down = [grid.core] + grid.chip[::-1] + grid.narrow
    qkv_sum, passed = grid.scatter(d_qkv, scatter_up)
    out_sum, _ = grid.scatter(d_out, scatter_down)
    ffn_grads = lax.optimization_barrier((ffn_grads, passed[len(grid.chip)]))[0].astype(F32)
    block_output, input_grad, sums = final(
        block_input, cotangent, y, d_ffn, mix_t, gq_t, gkv_t, w_qkv.T, w_out,
        norm_gains, (bias_output + bias_reduce)[None, :],
    )
    vector_grad = jnp.concatenate(
        [sums[0], sums[1], sums[2], sums[3], bias_sums[0], sums[4], up_columns_back(d_bias_up)[0], sums[4]]
    )
    for step in up_first:
        vector_grad = vector_grad + grid.swap(vector_grad, step)

    new_expand = MUON_MOMENTUM * momentum_expand + up_columns_back(ffn_grads[:, :FF])
    new_reduce = MUON_MOMENTUM * momentum_reduce + ffn_grads[:, FF:].reshape(-1, D)
    new_query = MUON_MOMENTUM * momentum_query + qkv_sum[:, :D]
    new_keyval = MUON_MOMENTUM * momentum_keyval + qkv_sum[:, D:QKV]
    new_output = MUON_MOMENTUM * momentum_output + out_sum

    def for_core(first, second):
        mine = jnp.where(core == 0, first, second)
        theirs = swap(jnp.where(core == 0, second, first), "core", 1)
        return jnp.concatenate(
            [jnp.where(core == 0, mine, theirs), jnp.where(core == 0, theirs, mine)], axis=0
        )

    rank = (lax.axis_index("chip") * 2 + core) * narrow + lax.axis_index("narrow")
    sibling = rank + (1 - 2 * core) * narrow

    def both_rows(m):
        return jnp.concatenate(
            [lax.dynamic_slice_in_dim(m, r * own, own, 0) for r in (rank, sibling)], axis=0
        )

    ffn_whole = lax.all_gather(
        jnp.concatenate([new_expand, new_reduce.reshape(own, 4 * D)], axis=1).astype(BF),
        ("chip", "core", "narrow"), axis=0, tiled=True,
    )
    u, q0 = wide_ns(core.astype(jnp.int32).reshape(1), ffn_whole)
    rows_m = both_rows(ffn_whole)
    as_up = dot(both_rows(u), ffn_whole[:, :FF])
    as_down = jnp.concatenate(
        [dot(rows_m[:, FF + q * D : FF + (q + 1) * D], u) for q in range(4)], axis=1
    )
    rows_m = rows_m.astype(F32) * q0[0, 0]
    rows_o = jnp.where(core == 0, rows_m[:, :FF] + as_up, rows_m[:, FF:] + as_down)
    mine, theirs = rows_o[:own], swap(rows_o[own:], "core", 1)
    o_expand = jnp.where(core == 0, mine, theirs)
    o_reduce = jnp.where(core == 0, theirs, mine).reshape(-1, D)

    low_keyval = new_keyval.astype(BF)
    pair = for_core(
        jnp.concatenate([new_query.astype(BF), low_keyval], axis=1),
        jnp.concatenate([new_output.astype(BF), low_keyval], axis=1),
    )
    wide = 512
    whole = jnp.concatenate(
        [
            grid.gather(pair[:, :wide], grid.narrow[::-1] + grid.chip[::-1]),
            grid.gather(pair[:, wide:], grid.narrow[::-1] + grid.chip),
        ],
        axis=1,
    )
    o_pair, o_kv = square_ns(whole[:, :D], whole[:, D:QKV])
    row_lo = place * (2 * own)
    mine = lax.dynamic_slice_in_dim(o_pair, row_lo + core * own, own, 0)
    theirs = swap(lax.dynamic_slice_in_dim(o_pair, row_lo + (1 - core) * own, own, 0), "core", 1)
    o_query = jnp.where(core == 0, mine, theirs)
    o_output = jnp.where(core == 0, theirs, mine)
    o_keyval = lax.dynamic_slice_in_dim(o_kv, row_lo + core * own, own, 0)

    new_momenta = (new_query, new_keyval, new_output, new_expand, new_reduce)
    new_weights = []
    for master, o in zip(masters, (o_query, o_keyval, o_output, o_expand, o_reduce)):
        factor = math.sqrt(max(1.0, master.shape[0] * devices / master.shape[1]))
        new_weights.append(master - MUON_RATE * factor * o)

    params = jnp.concatenate([norm_gains.reshape(-1), norm_biases.reshape(-1), proj_biases])
    vector_first = BETA_FIRST * adam_first + (1.0 - BETA_FIRST) * vector_grad
    vector_second = BETA_SECOND * adam_second + (1.0 - BETA_SECOND) * vector_grad * vector_grad
    corrected_first = vector_first / (1.0 - BETA_FIRST**STEP)
    corrected_second = vector_second / (1.0 - BETA_SECOND**STEP)
    vector_new = params - ADAM_RATE * corrected_first / (jnp.sqrt(corrected_second) + ADAM_EPS)
    return (
        block_output, input_grad, *new_momenta, *new_weights, vector_first, vector_second, vector_new
    )


def solution(mesh):
    wide, narrow = mesh.shape["wide"], mesh.shape["narrow"]
    grid = Mesh(mesh.devices.reshape(wide // 2, 2, narrow), ("chip", "core", "narrow"))
    rows = P(("chip", "core", "narrow"), None)
    in_specs = (rows,) * 13 + (P(),) * 5
    out_specs = (rows,) * 12 + (P(),) * 3
    return jax.shard_map(
        per_device, mesh=grid, in_specs=in_specs, out_specs=out_specs, check_vma=False
    )
```

time: 2710 us -> 529 us (0.20)
  waiting for transfers between devices: 1340 us -> 151 us
  matrix products: 587 us -> 11.5 us
  blocking collectives: 455 us -> 0 us
  Pallas kernels: 0 us -> 220 us
  other arithmetic: 222 us -> 21.2 us
  starting transfers between devices: 0.62 us -> 77.9 us
  loops' own time: 32 us -> 0 us
    unnamed x17 -> x4, waiting for transfers between devices: 829 us -> 0.07 us
    dot_general x54 -> x7, matrix products: 587 us -> 11.5 us  [the longest x1 5.1 us: dot_tn(): lax.dot_general(a, b, (((0,), (0,)), ((), ())), preferred_element_type=F32)]
    psum x1 -> x0, blocking collectives: 312 us -> none  [per_device(): vector_grad = lax.psum(local_vector, ('wide', 'narrow'))]
    psum x1 -> x0, waiting for transfers between devices: 282 us -> none  [broadcast(): return lax.psum(jnp.where(mine, x, jnp.zeros_like(x)), axis)]
    pallas_call x0 -> x8, Pallas kernels: none -> 220 us  [the longest x1 77.4 us: ffn(): pl.pallas_call(ffn_kernel, grid=(FF // FC,), in_specs=[whole((TOK, D)), w...]
    all_gather x2 -> x0, blocking collectives: 142 us -> none  [the longest x1 71.5 us: per_device(): lax.all_gather(for_sending(low_copies), ('wide', 'narrow'), axis=0, tiled...]
    reduce_scatter x4 -> x2, waiting for transfers between devices: 147 us -> 28.2 us  [the longest x1 28.2 us: per_device(): lax.psum_scatter(packed, 'chip', scatter_dimension=0, tiled=True)]
    ppermute x0 -> x38, waiting for transfers between devices: none -> 111 us  [swap(): lax.ppermute(x, axis, [(i, i ^ bit) for i in range(lax.axis_size(axis))])]
  transfers between devices with their start and end apart: 15 -> 42, of which waited for: 9 -> 27; matrix products, arithmetic and copies ran while one was open for 28% -> 6% of each run, Pallas kernels for 0% -> 27%
where the time goes in v1:
time: 529 us; the launch traced here: 523 us
  Pallas kernels  220 us (42%)
  waiting for transfers between devices  151 us (29%)
  starting transfers between devices  77.9 us (15%)
  local copies, waits for them, and re-layouts  26.2 us (5%)
  other arithmetic  21.2 us (4%)
  between operations  15.7 us (3%)
  matrix products  11.5 us (2%)
    ppermute x38, waiting for transfers between devices, swap(): lax.ppermute(x, axis, [(i, i ^ bit) for i in range(lax.axis_size(axis))])  111 us
    ppermute x38, starting transfers between devices, swap(): lax.ppermute(x, axis, [(i, i ^ bit) for i in range(lax.axis_size(axis))])  77.7 us
    pallas_call x1, Pallas kernels, ffn(): pl.pallas_call(ffn_kernel, grid=(FF // FC,), in_specs=[whole((TOK, D)), w...  77.4 us
    pallas_call x2, Pallas kernels, attention(): pl.pallas_call(partial(attention_kernel, opening, closing), grid_spec=plt...  57.5 us
    pallas_call x1, Pallas kernels, wide_ns(): pl.pallas_call(wide_kernel, grid_spec=pltpu.PrefetchScalarGridSpec(num_sc...  29.5 us
    reduce_scatter x1, waiting for transfers between devices, per_device(): lax.psum_scatter(packed, 'chip', scatter_dimension=0, tiled=True)  28.2 us
    pallas_call x1, Pallas kernels, square_ns(): pl.pallas_call(square_kernel, in_specs=[pl.BlockSpec(memory_space=pltpu.V...  19.2 us
    pallas_call x1, Pallas kernels, final(): pl.pallas_call(final_kernel, grid=(TOK // block,), in_specs=[pl.BlockSpec...  16.1 us
  transfers between devices with their start and end apart: 42, of which 27 were waited for; matrix products, arithmetic and copies ran while one was open for 6% of the time, Pallas kernels for 27%

profile of v1, /device:TPU:0, one launch (start us, length us, event | category | flops | bytes accessed | tf_op | source)
XLA Modules:
  0.0 523.4 jit_solution(13871176572161571833)
XLA Ops:
  10.6 3.1 collective-permute-start.5
  15.9 9.0 %prepare.1 = (bf16[768,2048]{1,0:T(8,128)(2,1)S(1)}, bf16[2048,768]{1,0:T(8,128)(2,1)}, bf16[768,2048]{1,0:T(8,128)(2,1)}, bf16[768,2048]{1,0:T(8,128)(2,1)}) custom-call(bf16[2048,768]{1,0:T(8,128)(2,1)} %x_ref.3, bf16[2048,768]{1,0:T(8,128)(2,1)} %g_ref.7, f32[2,768]{1,0:T(2,128)S(1)} %copy-done.11, f32[2,768]{1,0:T(2,128)S(1)} %copy-done.13), custom_call_target="tpu_custom_call" | custom-call | flops 31457280 | bytes 18874368 | tf_op jit(solution)/shard_map/prepare/pallas_call | solution.py:395
  25.0 3.1 collective-permute-start.6
  28.2 9.7 %collective-permute-done.6 = bf16[1,1,1,1,2,24,768]{6,5,4,3,2,1,0:T(8,128)(2,1)S(1)} collective-permute-done((bf16[1,1,1,1,2,24,768]{6,5,4,3,2,1,0:T(8,128)(2,1)S(1)}, bf16[1,1,1,1,2,24,768]{6,5,4,3,2,1,0:T(8,128)(2,1)S(1)}, u32[]{:S(2)}, u32[]{:S(2)}) %collective-permute-start.6) | collective-permute-done | bytes 73760 | tf_op jit(solution)/shard_map/ppermute | solution.py:675
  41.4 1.7 collective-permute-done.7
  44.7 2.9 collective-permute-done.2
  49.1 9.7 %collective-permute-done.8 = bf16[2,1,1,2,2,24,768]{6,5,4,3,2,1,0:T(8,128)(2,1)S(1)} collective-permute-done((bf16[2,1,1,2,2,24,768]{6,5,4,3,2,1,0:T(8,128)(2,1)S(1)}, bf16[2,1,1,2,2,24,768]{6,5,4,3,2,1,0:T(8,128)(2,1)S(1)}, u32[]{:S(2)}, u32[]{:S(2)}) %collective-permute-start.8) | collective-permute-done | bytes 294944 | tf_op jit(solution)/shard_map/ppermute | solution.py:675
  61.2 4.1 convolution_convert_fusion.refs_2_
  65.9 5.1 broadcast_add_fusion.refs_1_.refs_5_
  71.0 20.1 %attention.2 = (bf16[768,2048]{1,0:T(8,128)(2,1)S(1)}, bf16[768,2048]{1,0:T(8,128)(2,1)}, f32[2048,128]{1,0:T(8,128)S(1)}) custom-call(s32[4]{0:T(128)S(1)} %and_select_fusion.refs_0_, f32[896,2048]{1,0:T(8,128)} %broadcast_add_fusion.refs_1_.refs_5_, bf16[768,2048]{1,0:T(8,128)(2,1)} %convolution_convert_fusion.refs_2_, ...), custom_call_target="tpu_custom_call" | custom-call | flops 25769803776 | bytes 5242880 | tf_op jit(solution)/shard_map/attention/pallas_call | solution.py:232
  91.1 1.7 copy-done.2
  93.8 12.4 %all-gather.3.cloned.1.call-done.up_ref.down_ref = bf16[768,6144]{1,0:T(8,128)(2,1)} async-done(((bf16[24,6144]{1,0:T(8,128)(2,1)}), bf16[768,6144]{1,0:T(8,128)(2,1)}) %all-gather.3.cloned.1.call-update) | async-done | bytes 9437200 | tf_op jit(solution)/shard_map/all_gather | solution.py:754
  106.2 77.4 %ffn.1 = (f32[2048,768]{1,0:T(8,128)}, f32[2048,768]{1,0:T(8,128)}, bf16[768,3072]{1,0:T(8,128)(2,1)}, bf16[768,3072]{1,0:T(8,128)(2,1)}, f32[1,3072]{1,0:T(1,128)}) custom-call(bf16[2048,768]{1,0:T(8,128)(2,1)} %get-tuple-element.42.x_ref, bf16[768,2048]{1,0:T(8,128)(2,1)} %get-tuple-element.43.xt_ref, bf16[2048,768]{1,0:T(8,128)(2,1)} %g_ref.7, ...), custom_call_target="tpu_custom_call" | custom-call | flops 57982058496 | bytes 46137344 | tf_op jit(solution)/shard_map/ffn/pallas_call | solution.py:331
  183.6 3.4 dynamic-slice_bitcast_fusion.1
  189.1 2.8 collective-permute-done.10
  191.9 3.3 fusion.3
  196.1 2.6 pad_maximum_fusion
  198.8 1.8 copy-done.3
  201.8 37.4 %attention.3 = (bf16[768,2048]{1,0:T(8,128)(2,1)S(1)}, bf16[768,2048]{1,0:T(8,128)(2,1)}, f32[2048,128]{1,0:T(8,128)}, bf16[128,2048]{1,0:T(8,128)(2,1)S(1)}) custom-call(s32[4]{0:T(128)S(1)} %and_select_fusion.refs_0_, f32[896,2048]{1,0:T(8,128)} %broadcast_add_fusion.refs_1_.refs_5_, ...), custom_call_target="tpu_custom_call", output_to_operand_aliasing={{0}: (7, {}), {1}: (8, {})} | custom-call | flops 51539607552 | bytes 10485760 | tf_op jit(solution)/shard_map/attention/pallas_call | solution.py:232
  241.7 28.2 %reduce-scatter.3.cloned.1.call-done = bf16[96,6144]{1,0:T(8,128)(2,1)} async-done(((bf16[384,6144]{1,0:T(8,128)(2,1)}), bf16[96,6144]{1,0:T(8,128)(2,1)}) %reduce-scatter.3.cloned.1.call-update) | async-done | bytes 1179664 | tf_op jit(solution)/shard_map/reduce_scatter | solution.py:781
  271.0 11.0 %grads.1 = (bf16[768,896]{1,0:T(8,128)(2,1)S(1)}, bf16[768,768]{1,0:T(8,128)(2,1)S(1)}, f32[8,896]{1,0:T(8,128)S(1)}) custom-call(bf16[2048,768]{1,0:T(8,128)(2,1)} %g_ref.7, bf16[768,2048]{1,0:T(8,128)(2,1)} %copy-done.4, bf16[768,2048]{1,0:T(8,128)(2,1)} %get-tuple-element.54.gq_ref, bf16[128,2048]{1,0:T(8,128)(2,1)S(1)} %copy-done.9, ...), custom_call_target="tpu_custom_call" | custom-call | flops 5234491392 | bytes 16777216 | tf_op jit(solution)/shard_map/grads/pallas_call | solution.py:443
  283.2 2.1 collective-permute-done.12
  285.5 41.9 %collective-permute-start.13 = (bf16[1,2,1,2,2,24,896]{6,5,4,3,2,1,0:T(8,128)(2,1)S(1)}, bf16[1,2,1,2,2,24,896]{6,5,4,3,2,1,0:T(8,128)(2,1)S(1)}, u32[]{:S(2)}, u32[]{:S(2)}) collective-permute-start(bf16[1,2,1,2,2,24,896]{6,5,4,3,2,1,0:T(8,128)(2,1)S(1)} %dynamic-slice_convert_fusion), channel_id=1, source_target_pairs={{0,16},{8,24},{16,0},{24,8},{1,17},{9,25},{17,1},{25,9},{2,18},{10... | collective-permute-start | bytes 1032200 | tf_op jit(solution)/shard_map/ppermute | solution.py:675
  327.4 8.4 %collective-permute-done.13 = bf16[1,2,1,2,2,24,896]{6,5,4,3,2,1,0:T(8,128)(2,1)S(1)} collective-permute-done((bf16[1,2,1,2,2,24,896]{6,5,4,3,2,1,0:T(8,128)(2,1)S(1)}, bf16[1,2,1,2,2,24,896]{6,5,4,3,2,1,0:T(8,128)(2,1)S(1)}, u32[]{:S(2)}, u32[]{:S(2)}) %collective-permute-start.13) | collective-permute-done | bytes 344096 | tf_op jit(solution)/shard_map/ppermute | solution.py:675
  335.9 3.1 collective-permute-start.14
  339.0 4.3 collective-permute-done.14
  349.2 1.9 copy.54
  354.1 16.1 %closing.1 = (bf16[2048,768]{1,0:T(8,128)(2,1)}, f32[2048,768]{1,0:T(8,128)}, f32[8,768]{1,0:T(8,128)S(1)}) custom-call(bf16[2048,768]{1,0:T(8,128)(2,1)} %x_ref.3, bf16[2048,768]{1,0:T(8,128)(2,1)} %g_ref.7, f32[2048,768]{1,0:T(8,128)} %get-tuple-element.47.y_ref, f32[2048,768]{1,0:T(8,128)} %get-tuple-element.48.df_ref, bf16[768,2048]{1,0:T(8,128)(2,1)} %copy-done.4, ...), custom_call_target="tpu_custom_call" | custom-call | flops 5234491392 | bytes 37748736 | tf_op jit(solution)/shard_map/closing/pallas_call | solution.py:505
  370.6 1.8 collective-permute-start.18
  372.4 12.0 %collective-permute-done.18 = bf16[2,1,1,2,2,24,768]{6,5,4,3,2,1,0:T(8,128)(2,1)S(1)} collective-permute-done((bf16[2,1,1,2,2,24,768]{6,5,4,3,2,1,0:T(8,128)(2,1)S(1)}, bf16[2,1,1,2,2,24,768]{6,5,4,3,2,1,0:T(8,128)(2,1)S(1)}, u32[]{:S(2)}, u32[]{:S(2)}) %collective-permute-start.18) | collective-permute-done | bytes 294944 | tf_op jit(solution)/shard_map/ppermute | solution.py:675
  385.8 3.9 collective-permute-done.19
  389.9 4.5 collective-permute-done.33
  394.4 2.7 collective-permute-start.34
  397.1 2.2 collective-permute-done.34
  399.3 2.9 collective-permute-start.35
  402.3 1.9 collective-permute-start.15
  405.2 7.0 %collective-permute-done.15 = bf16[1,1,1,1,2,24,896]{6,5,4,3,2,1,0:T(8,128)(2,1)S(1)} collective-permute-done((bf16[1,1,1,1,2,24,896]{6,5,4,3,2,1,0:T(8,128)(2,1)S(1)}, bf16[1,1,1,1,2,24,896]{6,5,4,3,2,1,0:T(8,128)(2,1)S(1)}, u32[]{:S(2)}, u32[]{:S(2)}) %collective-permute-start.15) | collective-permute-done | bytes 86048 | tf_op jit(solution)/shard_map/ppermute | solution.py:675
  413.0 6.6 %collective-permute-done.16 = bf16[1,1,1,1,1,24,896]{6,5,4,3,2,1,0:T(8,128)(2,1)S(1)} collective-permute-done((bf16[1,1,1,1,1,24,896]{6,5,4,3,2,1,0:T(8,128)(2,1)S(1)}, bf16[1,1,1,1,1,24,896]{6,5,4,3,2,1,0:T(8,128)(2,1)S(1)}, u32[]{:S(2)}, u32[]{:S(2)}) %collective-permute-start.16) | collective-permute-done | bytes 43040 | tf_op jit(solution)/shard_map/ppermute | solution.py:675
  421.3 3.8 collective-permute-done.36
  425.2 2.0 collective-permute-start.23
  427.2 5.2 collective-permute-done.27
  435.6 5.9 %collective-permute-done.28 = bf16[1,1,1,1,2,48,384]{6,5,4,3,2,1,0:T(8,128)(2,1)S(1)} collective-permute-done((bf16[1,1,1,1,2,48,384]{6,5,4,3,2,1,0:T(8,128)(2,1)S(1)}, bf16[1,1,1,1,2,48,384]{6,5,4,3,2,1,0:T(8,128)(2,1)S(1)}, u32[]{:S(2)}, u32[]{:S(2)}) %collective-permute-start.28) | collective-permute-done | bytes 73760 | tf_op jit(solution)/shard_map/ppermute | solution.py:675
  443.7 3.2 collective-permute-done.29
  447.1 4.1 collective-permute-done.25
  453.1 3.3 collective-permute-done.30
  456.5 3.6 collective-permute-done.26
  460.4 19.2 %square_ns.1 = (f32[768,768]{1,0:T(8,128)S(1)}, f32[768,128]{1,0:T(8,128)S(1)}) custom-call(bf16[768,768]{1,0:T(8,128)(2,1)S(1)} %pad_maximum_fusion.2.m_ref, bf16[768,128]{1,0:T(8,128)(2,1)S(1)} %slice.123.kv_ref), custom_call_target="tpu_custom_call" | custom-call | flops 15401484288 | bytes 6291456 | tf_op jit(solution)/shard_map/square_ns/pallas_call | solution.py:661
  479.7 29.5 %wide_ns.1 = (bf16[768,768]{1,0:T(8,128)(2,1)S(1)}, f32[1,768]{1,0:T(1,128)S(1)}) custom-call(s32[1]{0:T(128)} %bitcast.28.down_ref, bf16[768,6144]{1,0:T(8,128)(2,1)} %all-gather.5.cloned.1.call-done.m_ref), custom_call_target="tpu_custom_call" | custom-call | flops 21743271936 | bytes 6291456 | tf_op jit(solution)/shard_map/wide_ns/pallas_call | solution.py:613
  (282 shorter events, 54.2 us)
Async XLA Ops:
  7.2 99.0 %all-gather.3.cloned.1.call-start = ((), (), s32[]{:S(2)}) async-start(), calls=%async_computation.2 | async-start | bytes 9732096 | tf_op jit(solution)/shard_map/all_gather | solution.py:754
  10.5 259.4 %reduce-scatter.3.cloned.1.call-start = ((), (), s32[]{:S(2)}) async-start(), calls=%async_computation.3 | async-start | bytes 5898240 | tf_op jit(solution)/shard_map/reduce_scatter | solution.py:781
  10.6 14.4 %collective-permute-start.5 = (bf16[1,1,1,1,1,24,768]{6,5,4,3,2,1,0:T(8,128)(2,1)S(1)}, bf16[1,1,1,1,1,24,768]{6,5,4,3,2,1,0:T(8,128)(2,1)S(1)}, u32[]{:S(2)}, u32[]{:S(2)}) collective-permute-start(bf16[1,1,1,1,1,24,768]{6,5,4,3,2,1,0:T(8,128)(2,1)S(1)} %convert_bitcast_fusion), channel_id=1, source_target_pairs={{0,1},{1,0},{2,3},{3,2},{4,5},{5,4},{6,7},{7,6},{8,9},{9,8},{10,11... | collective-permute-start | bytes 110600 | tf_op jit(solution)/shard_map/ppermute | solution.py:675
  13.7 14.4 %collective-permute-start = (bf16[1,1,1,1,1,24,896]{6,5,4,3,2,1,0:T(8,128)(2,1)S(1)}, bf16[1,1,1,1,1,24,896]{6,5,4,3,2,1,0:T(8,128)(2,1)S(1)}, u32[]{:S(2)}, u32[]{:S(2)}) collective-permute-start(bf16[1,1,1,1,1,24,896]{6,5,4,3,2,1,0:T(8,128)(2,1)S(1)} %pad_maximum_fusion.25), channel_id=1, source_target_pairs={{0,1},{1,0},{2,3},{3,2},{4,5},{5,4},{6,7},{7,6},{8,9},{9,8},{10,11... | collective-permute-start | bytes 129032 | tf_op jit(solution)/shard_map/ppermute | solution.py:675
  24.9 40.6 %copy-start.5 = (bf16[768,2048]{1,0:T(8,128)(2,1)}, bf16[768,2048]{1,0:T(8,128)(2,1)S(1)}, u32[]{:S(2)}) copy-start(bf16[768,2048]{1,0:T(8,128)(2,1)S(1)} %get-tuple-element.45.nt_ref) | copy-start | bytes 9437188
  25.0 12.9 %collective-permute-start.6 = (bf16[1,1,1,1,2,24,768]{6,5,4,3,2,1,0:T(8,128)(2,1)S(1)}, bf16[1,1,1,1,2,24,768]{6,5,4,3,2,1,0:T(8,128)(2,1)S(1)}, u32[]{:S(2)}, u32[]{:S(2)}) collective-permute-start(bf16[1,1,1,1,2,24,768]{6,5,4,3,2,1,0:T(8,128)(2,1)S(1)} %pad_maximum_fusion.21), channel_id=1, source_target_pairs={{0,2},{1,3},{2,0},{3,1},{4,6},{5,7},{6,4},{7,5},{8,10},{9,11},{10,... | collective-permute-start | bytes 221192 | tf_op jit(solution)/shard_map/ppermute | solution.py:675
  28.1 11.6 %collective-permute-start.1 = (bf16[1,1,1,1,2,24,896]{6,5,4,3,2,1,0:T(8,128)(2,1)S(1)}, bf16[1,1,1,1,2,24,896]{6,5,4,3,2,1,0:T(8,128)(2,1)S(1)}, u32[]{:S(2)}, u32[]{:S(2)}) collective-permute-start(bf16[1,1,1,1,2,24,896]{6,5,4,3,2,1,0:T(8,128)(2,1)S(1)} %pad_maximum_fusion.20), channel_id=1, source_target_pairs={{0,2},{1,3},{2,0},{3,1},{4,6},{5,7},{6,4},{7,5},{8,10},{9,11},{10,... | collective-permute-start | bytes 258056 | tf_op jit(solution)/shard_map/ppermute | solution.py:675
  37.9 5.2 collective-permute-start.7
  39.8 7.7 %collective-permute-start.2 = (bf16[1,1,1,2,2,24,896]{6,5,4,3,2,1,0:T(8,128)(2,1)S(1)}, bf16[1,1,1,2,2,24,896]{6,5,4,3,2,1,0:T(8,128)(2,1)S(1)}, u32[]{:S(2)}, u32[]{:S(2)}) collective-permute-start(bf16[1,1,1,2,2,24,896]{6,5,4,3,2,1,0:T(8,128)(2,1)S(1)} %pad_maximum_fusion.16), channel_id=1, source_target_pairs={{0,8},{8,0},{16,24},{24,16},{1,9},{9,1},{17,25},{25,17},{2,10},{10... | collective-permute-start | bytes 516104 | tf_op jit(solution)/shard_map/ppermute | solution.py:675
  43.2 15.5 %collective-permute-start.8 = (bf16[2,1,1,2,2,24,768]{6,5,4,3,2,1,0:T(8,128)(2,1)S(1)}, bf16[2,1,1,2,2,24,768]{6,5,4,3,2,1,0:T(8,128)(2,1)S(1)}, u32[]{:S(2)}, u32[]{:S(2)}) collective-permute-start(bf16[2,1,1,2,2,24,768]{6,5,4,3,2,1,0:T(8,128)(2,1)S(1)} %pad_maximum_fusion.12), channel_id=1, source_target_pairs={{0,8},{8,0},{16,24},{24,16},{1,9},{9,1},{17,25},{25,17},{2,10},{10... | collective-permute-start | bytes 884744 | tf_op jit(solution)/shard_map/ppermute | solution.py:675
  47.7 11.3 %collective-permute-start.3 = (bf16[1,2,1,2,2,24,896]{6,5,4,3,2,1,0:T(8,128)(2,1)S(1)}, bf16[1,2,1,2,2,24,896]{6,5,4,3,2,1,0:T(8,128)(2,1)S(1)}, u32[]{:S(2)}, u32[]{:S(2)}) collective-permute-start(bf16[1,2,1,2,2,24,896]{6,5,4,3,2,1,0:T(8,128)(2,1)S(1)} %pad_maximum_fusion.10), channel_id=1, source_target_pairs={{0,16},{8,24},{16,0},{24,8},{1,17},{9,25},{17,1},{25,9},{2,18},{10... | collective-permute-start | bytes 1032200 | tf_op jit(solution)/shard_map/ppermute | solution.py:675
  58.9 2.1 collective-permute-start.9
  59.2 6.1 %collective-permute-start.4 = (bf16[2,2,1,2,2,24,896]{6,5,4,3,2,1,0:T(8,128)(2,1)S(1)}, bf16[2,2,1,2,2,24,896]{6,5,4,3,2,1,0:T(8,128)(2,1)S(1)}, u32[]{:S(2)}, u32[]{:S(2)}) collective-permute-start(bf16[2,2,1,2,2,24,896]{6,5,4,3,2,1,0:T(8,128)(2,1)S(1)} %pad_maximum_fusion.6), channel_id=1, source_target_pairs={{0,4},{4,0},{1,5},{5,1},{2,6},{6,2},{3,7},{7,3},{8,12},{12,8},{9,1... | collective-permute-start | bytes 2064392 | tf_op jit(solution)/shard_map/ppermute | solution.py:675
  187.1 4.9 collective-permute-start.10
  188.9 6.3 %collective-permute-start.11 = (bf16[4,96,3072]{2,1,0:T(8,128)(2,1)}, bf16[4,96,3072]{2,1,0:T(8,128)(2,1)S(1)}, u32[]{:S(2)}, u32[]{:S(2)}) collective-permute-start(bf16[4,96,3072]{2,1,0:T(8,128)(2,1)} %dynamic-slice_bitcast_fusion), channel_id=1, source_target_pairs={{0,4},{4,0},{1,5},{5,1},{2,6},{6,2},{3,7},{7,3},{8,12},{12,8},{9,1... | collective-permute-start | bytes 7077896 | tf_op jit(solution)/shard_map/ppermute | solution.py:675
  198.7 145.4 %reduce-scatter.5.cloned.1.call-start = ((), (), s32[]{:S(2)}) async-start(), calls=%async_computation.4 | async-start | bytes 1474560 | tf_op jit(solution)/shard_map/reduce_scatter | solution.py:787
  269.9 209.9 %all-gather.5.cloned.1.call-start = ((), (), s32[]{:S(2)}) async-start(), calls=%async_computation.5 | async-start | bytes 9732096 | tf_op jit(solution)/shard_map/all_gather | solution.py:825
  283.1 2.2 collective-permute-start.12
  285.5 50.3 %collective-permute-start.13 = (bf16[1,2,1,2,2,24,896]{6,5,4,3,2,1,0:T(8,128)(2,1)S(1)}, bf16[1,2,1,2,2,24,896]{6,5,4,3,2,1,0:T(8,128)(2,1)S(1)}, u32[]{:S(2)}, u32[]{:S(2)}) collective-permute-start(bf16[1,2,1,2,2,24,896]{6,5,4,3,2,1,0:T(8,128)(2,1)S(1)} %dynamic-slice_convert_fusion), channel_id=1, source_target_pairs={{0,16},{8,24},{16,0},{24,8},{1,17},{9,25},{17,1},{25,9},{2,18},{10... | collective-permute-start | bytes 1032200 | tf_op jit(solution)/shard_map/ppermute | solution.py:675
  335.9 7.4 %collective-permute-start.14 = (bf16[1,1,1,2,2,24,896]{6,5,4,3,2,1,0:T(8,128)(2,1)S(1)}, bf16[1,1,1,2,2,24,896]{6,5,4,3,2,1,0:T(8,128)(2,1)S(1)}, u32[]{:S(2)}, u32[]{:S(2)}) collective-permute-start(bf16[1,1,1,2,2,24,896]{6,5,4,3,2,1,0:T(8,128)(2,1)S(1)} %dynamic-slice_convert_fusion.2), channel_id=1, source_target_pairs={{0,8},{8,0},{16,24},{24,16},{1,9},{9,1},{17,25},{25,17},{2,10},{10... | collective-permute-start | bytes 516104 | tf_op jit(solution)/shard_map/ppermute | solution.py:675
  354.0 16.3 %collective-permute-start.17 = (bf16[2,2,1,2,2,24,768]{6,5,4,3,2,1,0:T(8,128)(2,1)S(1)}, bf16[2,2,1,2,2,24,768]{6,5,4,3,2,1,0:T(8,128)(2,1)S(1)}, u32[]{:S(2)}, u32[]{:S(2)}) collective-permute-start(bf16[2,2,1,2,2,24,768]{6,5,4,3,2,1,0:T(8,128)(2,1)S(1)} %constant_dynamic-slice_fusion.5), channel_id=1, source_target_pairs={{0,4},{4,0},{1,5},{5,1},{2,6},{6,2},{3,7},{7,3},{8,12},{12,8},{9,1... | collective-permute-start | bytes 1769480 | tf_op jit(solution)/shard_map/ppermute | solution.py:675
  370.5 31.8 %copy-start.24 = (f32[1,1,1,2,2,24,896]{6,5,4,3,2,1,0:T(8,128)S(1)}, f32[1,1,1,2,2,24,896]{6,5,4,3,2,1,0:T(8,128)}, u32[]{:S(2)}) copy-start(f32[1,1,1,2,2,24,896]{6,5,4,3,2,1,0:T(8,128)} %convert_add_fusion.6) | copy-start | bytes 1032196
  370.5 41.9 %copy-start.33 = (f32[24,768]{1,0:T(8,128)S(1)}, f32[24,768]{1,0:T(8,128)}, u32[]{:S(2)}) copy-start(f32[24,768]{1,0:T(8,128)} %param.28) | copy-start | bytes 221188
  370.5 49.1 %copy-start.42 = (f32[24,128]{1,0:T(8,128)S(1)}, f32[24,128]{1,0:T(8,128)}, u32[]{:S(2)}) copy-start(f32[24,128]{1,0:T(8,128)} %param.27) | copy-start | bytes 36868
  370.6 49.7 %copy-start.34 = (f32[24,768]{1,0:T(8,128)S(1)}, f32[24,768]{1,0:T(8,128)}, u32[]{:S(2)}) copy-start(f32[24,768]{1,0:T(8,128)} %param.26) | copy-start | bytes 221188
  370.6 13.8 %collective-permute-start.18 = (bf16[2,1,1,2,2,24,768]{6,5,4,3,2,1,0:T(8,128)(2,1)S(1)}, bf16[2,1,1,2,2,24,768]{6,5,4,3,2,1,0:T(8,128)(2,1)S(1)}, u32[]{:S(2)}, u32[]{:S(2)}) collective-permute-start(bf16[2,1,1,2,2,24,768]{6,5,4,3,2,1,0:T(8,128)(2,1)S(1)} %dynamic-slice_convert_fusion.1), channel_id=1, source_target_pairs={{0,8},{8,0},{16,24},{24,16},{1,9},{9,1},{17,25},{25,17},{2,10},{10... | collective-permute-start | bytes 884744 | tf_op jit(solution)/shard_map/ppermute | solution.py:675
  372.4 48.8 %copy-start.14 = (f32[2,768]{1,0:T(2,128)S(1)}, f32[2,768]{1,0:T(2,128)}, u32[]{:S(2)}) copy-start(f32[2,768]{1,0:T(2,128)} %shift_ref.1) | copy-start | bytes 18436
  384.5 5.2 collective-permute-start.19
  389.8 12.5 %collective-permute-start.20 = (bf16[1,1,1,1,2,24,768]{6,5,4,3,2,1,0:T(8,128)(2,1)S(1)}, bf16[1,1,1,1,2,24,768]{6,5,4,3,2,1,0:T(8,128)(2,1)S(1)}, u32[]{:S(2)}, u32[]{:S(2)}) collective-permute-start(bf16[1,1,1,1,2,24,768]{6,5,4,3,2,1,0:T(8,128)(2,1)S(1)} %dynamic-slice_convert_fusion.5), channel_id=1, source_target_pairs={{0,2},{1,3},{2,0},{3,1},{4,6},{5,7},{6,4},{7,5},{8,10},{9,11},{10,... | collective-permute-start | bytes 221192 | tf_op jit(solution)/shard_map/ppermute | solution.py:675
  389.9 4.6 collective-permute-start.33
  394.4 4.9 collective-permute-start.34
  399.3 21.7 %collective-permute-start.35 = (f32[8576]{0:T(1024)S(1)}, f32[8576]{0:T(1024)S(1)}, u32[]{:S(2)}, u32[]{:S(2)}) collective-permute-start(f32[8576]{0:T(1024)S(1)} %add.293), channel_id=1, source_target_pairs={{0,8},{8,0},{16,24},{24,16},{1,9},{9,1},{17,25},{25,17},{2,10},{10... | collective-permute-start | bytes 102920 | tf_op jit(solution)/shard_map/ppermute | solution.py:675
  402.3 9.9 %collective-permute-start.15 = (bf16[1,1,1,1,2,24,896]{6,5,4,3,2,1,0:T(8,128)(2,1)S(1)}, bf16[1,1,1,1,2,24,896]{6,5,4,3,2,1,0:T(8,128)(2,1)S(1)}, u32[]{:S(2)}, u32[]{:S(2)}) collective-permute-start(bf16[1,1,1,1,2,24,896]{6,5,4,3,2,1,0:T(8,128)(2,1)S(1)} %dynamic-slice_convert_fusion.4), channel_id=1, source_target_pairs={{0,2},{1,3},{2,0},{3,1},{4,6},{5,7},{6,4},{7,5},{8,10},{9,11},{10,... | collective-permute-start | bytes 258056 | tf_op jit(solution)/shard_map/ppermute | solution.py:675
  404.2 8.2 %collective-permute-start.21 = (bf16[1,1,1,1,1,24,768]{6,5,4,3,2,1,0:T(8,128)(2,1)S(1)}, bf16[1,1,1,1,1,24,768]{6,5,4,3,2,1,0:T(8,128)(2,1)S(1)}, u32[]{:S(2)}, u32[]{:S(2)}) collective-permute-start(bf16[1,1,1,1,1,24,768]{6,5,4,3,2,1,0:T(8,128)(2,1)S(1)} %dynamic-slice_convert_fusion.7), channel_id=1, source_target_pairs={{0,1},{1,0},{2,3},{3,2},{4,5},{5,4},{6,7},{7,6},{8,9},{9,8},{10,11... | collective-permute-start | bytes 110600 | tf_op jit(solution)/shard_map/ppermute | solution.py:675
  412.2 7.4 %collective-permute-start.16 = (bf16[1,1,1,1,1,24,896]{6,5,4,3,2,1,0:T(8,128)(2,1)S(1)}, bf16[1,1,1,1,1,24,896]{6,5,4,3,2,1,0:T(8,128)(2,1)S(1)}, u32[]{:S(2)}, u32[]{:S(2)}) collective-permute-start(bf16[1,1,1,1,1,24,896]{6,5,4,3,2,1,0:T(8,128)(2,1)S(1)} %dynamic-slice_convert_fusion.6), channel_id=1, source_target_pairs={{0,1},{1,0},{2,3},{3,2},{4,5},{5,4},{6,7},{7,6},{8,9},{9,8},{10,11... | collective-permute-start | bytes 129032 | tf_op jit(solution)/shard_map/ppermute | solution.py:675
  420.9 4.1 collective-permute-start.22
  421.0 4.0 collective-permute-start.36
  425.0 27.4 %collective-permute-start.37 = (f32[8576]{0:T(1024)S(1)}, f32[8576]{0:T(1024)S(1)}, u32[]{:S(2)}, u32[]{:S(2)}) collective-permute-start(f32[8576]{0:T(1024)S(1)} %add.295), channel_id=1, source_target_pairs={{0,4},{4,0},{1,5},{5,1},{2,6},{6,2},{3,7},{7,3},{8,12},{12,8},{9,1... | collective-permute-start | bytes 102920 | tf_op jit(solution)/shard_map/ppermute | solution.py:675
  425.1 7.3 %collective-permute-start.27 = (bf16[1,1,1,1,1,48,384]{6,5,4,3,2,1,0:T(8,128)(2,1)S(1)}, bf16[1,1,1,1,1,48,384]{6,5,4,3,2,1,0:T(8,128)(2,1)S(1)}, u32[]{:S(2)}, u32[]{:S(2)}) collective-permute-start(bf16[1,1,1,1,1,48,384]{6,5,4,3,2,1,0:T(8,128)(2,1)S(1)} %fusion.28), channel_id=1, source_target_pairs={{0,1},{1,0},{2,3},{3,2},{4,5},{5,4},{6,7},{7,6},{8,9},{9,8},{10,11... | collective-permute-start | bytes 110600 | tf_op jit(solution)/shard_map/ppermute | solution.py:675
  425.2 9.1 %collective-permute-start.23 = (bf16[1,1,1,1,1,48,512]{6,5,4,3,2,1,0:T(8,128)(2,1)S(1)}, bf16[1,1,1,1,1,48,512]{6,5,4,3,2,1,0:T(8,128)(2,1)S(1)}, u32[]{:S(2)}, u32[]{:S(2)}) collective-permute-start(bf16[1,1,1,1,1,48,512]{6,5,4,3,2,1,0:T(8,128)(2,1)S(1)} %fusion.26), channel_id=1, source_target_pairs={{0,1},{1,0},{2,3},{3,2},{4,5},{5,4},{6,7},{7,6},{8,9},{9,8},{10,11... | collective-permute-start | bytes 147464 | tf_op jit(solution)/shard_map/ppermute | solution.py:675
  432.5 9.0 %collective-permute-start.28 = (bf16[1,1,1,1,2,48,384]{6,5,4,3,2,1,0:T(8,128)(2,1)S(1)}, bf16[1,1,1,1,2,48,384]{6,5,4,3,2,1,0:T(8,128)(2,1)S(1)}, u32[]{:S(2)}, u32[]{:S(2)}) collective-permute-start(bf16[1,1,1,1,2,48,384]{6,5,4,3,2,1,0:T(8,128)(2,1)S(1)} %pad_maximum_fusion.22), channel_id=1, source_target_pairs={{0,2},{1,3},{2,0},{3,1},{4,6},{5,7},{6,4},{7,5},{8,10},{9,11},{10,... | collective-permute-start | bytes 221192 | tf_op jit(solution)/shard_map/ppermute | solution.py:675
  434.4 8.9 %collective-permute-start.24 = (bf16[1,1,1,1,2,48,512]{6,5,4,3,2,1,0:T(8,128)(2,1)S(1)}, bf16[1,1,1,1,2,48,512]{6,5,4,3,2,1,0:T(8,128)(2,1)S(1)}, u32[]{:S(2)}, u32[]{:S(2)}) collective-permute-start(bf16[1,1,1,1,2,48,512]{6,5,4,3,2,1,0:T(8,128)(2,1)S(1)} %pad_maximum_fusion.19), channel_id=1, source_target_pairs={{0,2},{1,3},{2,0},{3,1},{4,6},{5,7},{6,4},{7,5},{8,10},{9,11},{10,... | collective-permute-start | bytes 294920 | tf_op jit(solution)/shard_map/ppermute | solution.py:675
  441.5 5.4 %collective-permute-start.29 = (bf16[1,1,1,2,2,48,384]{6,5,4,3,2,1,0:T(8,128)(2,1)S(1)}, bf16[1,1,1,2,2,48,384]{6,5,4,3,2,1,0:T(8,128)(2,1)S(1)}, u32[]{:S(2)}, u32[]{:S(2)}) collective-permute-start(bf16[1,1,1,2,2,48,384]{6,5,4,3,2,1,0:T(8,128)(2,1)S(1)} %pad_maximum_fusion.18), channel_id=1, source_target_pairs={{0,16},{8,24},{16,0},{24,8},{1,17},{9,25},{17,1},{25,9},{2,18},{10... | collective-permute-start | bytes 442376 | tf_op jit(solution)/shard_map/ppermute | solution.py:675
  443.3 7.9 %collective-permute-start.25 = (bf16[1,1,1,2,2,48,512]{6,5,4,3,2,1,0:T(8,128)(2,1)S(1)}, bf16[1,1,1,2,2,48,512]{6,5,4,3,2,1,0:T(8,128)(2,1)S(1)}, u32[]{:S(2)}, u32[]{:S(2)}) collective-permute-start(bf16[1,1,1,2,2,48,512]{6,5,4,3,2,1,0:T(8,128)(2,1)S(1)} %pad_maximum_fusion.15), channel_id=1, source_target_pairs={{0,8},{8,0},{16,24},{24,16},{1,9},{9,1},{17,25},{25,17},{2,10},{10... | collective-permute-start | bytes 589832 | tf_op jit(solution)/shard_map/ppermute | solution.py:675
  447.0 9.4 %collective-permute-start.30 = (bf16[2,1,1,2,2,48,384]{6,5,4,3,2,1,0:T(8,128)(2,1)S(1)}, bf16[2,1,1,2,2,48,384]{6,5,4,3,2,1,0:T(8,128)(2,1)S(1)}, u32[]{:S(2)}, u32[]{:S(2)}) collective-permute-start(bf16[2,1,1,2,2,48,384]{6,5,4,3,2,1,0:T(8,128)(2,1)S(1)} %pad_maximum_fusion.13), channel_id=1, source_target_pairs={{0,8},{8,0},{16,24},{24,16},{1,9},{9,1},{17,25},{25,17},{2,10},{10... | collective-permute-start | bytes 884744 | tf_op jit(solution)/shard_map/ppermute | solution.py:675
  451.3 8.9 %collective-permute-start.26 = (bf16[1,2,1,2,2,48,512]{6,5,4,3,2,1,0:T(8,128)(2,1)S(1)}, bf16[1,2,1,2,2,48,512]{6,5,4,3,2,1,0:T(8,128)(2,1)S(1)}, u32[]{:S(2)}, u32[]{:S(2)}) collective-permute-start(bf16[1,2,1,2,2,48,512]{6,5,4,3,2,1,0:T(8,128)(2,1)S(1)} %pad_maximum_fusion.9), channel_id=1, source_target_pairs={{0,16},{8,24},{16,0},{24,8},{1,17},{9,25},{17,1},{25,9},{2,18},{10... | collective-permute-start | bytes 1179656 | tf_op jit(solution)/shard_map/ppermute | solution.py:675
  479.6 34.5 %collective-permute-start.31 = (f32[24,768]{1,0:T(8,128)S(1)}, f32[24,768]{1,0:T(8,128)S(1)}, u32[]{:S(2)}, u32[]{:S(2)}) collective-permute-start(f32[24,768]{1,0:T(8,128)S(1)} %constant_dynamic-slice_fusion.4), channel_id=1, source_target_pairs={{0,4},{4,0},{1,5},{5,1},{2,6},{6,2},{3,7},{7,3},{8,12},{12,8},{9,1... | collective-permute-start | bytes 221192 | tf_op jit(solution)/shard_map/ppermute | solution.py:675
  512.9 1.9 collective-permute-start.32
  (39 other events, 215.5 us)
Sparse Core Ops, SparseCore 0:
  11.4 94.7 all-gather.2
  198.8 70.9 reduce-scatter.2
  272.2 66.8 reduce-scatter.4
  349.2 87.6 all-gather.4

commit v2 on v1

--- a/solution.py
+++ b/solution.py
@@ -375,6 +375,30 @@
 QKV = D + 2 * HEAD_DIM
 
 
+def merge_kernel(_, up_ref, down_ref, up_in_ref, down_in_ref, out_ref):
+    out_ref[:, 0:FF] = (up_ref[...].astype(F32) + up_in_ref[...].astype(F32)).astype(BF)
+    out_ref[:, FF:] = (down_ref[...].astype(F32) + down_in_ref[...].astype(F32)).astype(BF)
+
+
+def merge(core, d_up, d_down, up_in, down_in, rows):
+    kept = pl.BlockSpec((rows, FF), lambda i, c: (2 * i + c[0], 0))
+    came = pl.BlockSpec((rows, FF), lambda i, c: (i, 0))
+    count = up_in.shape[0] // rows
+    return pl.pallas_call(
+        merge_kernel,
+        grid_spec=pltpu.PrefetchScalarGridSpec(
+            num_scalar_prefetch=1,
+            grid=(count,),
+            in_specs=[kept, kept, came, came],
+            out_specs=pl.BlockSpec((rows, 2 * FF), lambda i, c: (i, 0)),
+        ),
+        out_shape=jax.ShapeDtypeStruct((count * rows, 2 * FF), BF),
+        compiler_params=pltpu.CompilerParams(vmem_limit_bytes=32 * MIB),
+        cost_estimate=pl.CostEstimate(flops=2 * D * FF, bytes_accessed=14 * MIB, transcendentals=0),
+        name="merge",
+    )(core, d_up, d_down, up_in, down_in)
+
+
 def prepare_kernel(x_ref, g_ref, gain_ref, shift_ref, na_t_ref, nf_ref, nf_t_ref, g_t_ref):
     x = x_ref[...].astype(F32)
     centred = x - jnp.mean(x, axis=-1, keepdims=True)
@@ -408,7 +432,7 @@
     )(x, g, gains, shifts)
 
 
-def grads_kernel(g_ref, mix_ref, gq_ref, gkv_ref, nt_ref, dqkv_ref, dout_ref, bsum_ref, qkv_acc, out_acc):
+def grads_kernel(g_ref, mix_ref, gq_ref, gkv_ref, nt_ref, _, dqkv_ref, dout_ref, bsum_ref, qkv_acc, out_acc):
     i = pl.program_id(0)
     gq = gq_ref[...]
     gkv = gkv_ref[...]
@@ -433,7 +457,7 @@
         dout_ref[...] = out_acc[...].astype(BF)
 
 
-def grads(g, mix, gq, gkv, nt):
+def grads(g, mix, gq, gkv, nt, after):
     block = 1024
     cols = pl.BlockSpec((D, block), lambda i: (0, i))
 
@@ -445,7 +469,7 @@
         grid=(TOK // block,),
         in_specs=[
             pl.BlockSpec((block, D), lambda i: (i, 0)), cols, cols,
-            pl.BlockSpec((128, block), lambda i: (0, i)), cols,
+            pl.BlockSpec((128, block), lambda i: (0, i)), cols, pl.BlockSpec(memory_space=pl.ANY),
         ],
         out_specs=[fixed((D, QKV)), fixed((D, D)), fixed((8, QKV))],
         scratch_shapes=[pltpu.VMEM((D, QKV), F32), pltpu.VMEM((D, D), F32)],
@@ -460,11 +484,11 @@
             flops=2 * TOK * D * (QKV + D), bytes_accessed=16 * MIB, transcendentals=0
         ),
         name="grads",
-    )(g, mix, gq, gkv, nt)
+    )(g, mix, gq, gkv, nt, after)
 
 
 def final_kernel(
-    x_ref, g_ref, y_ref, df_ref, mix_ref, gq_ref, gkv_ref, wt_ref, wo_ref, gain_ref, bias_ref,
+    x_ref, g_ref, y_ref, df_ref, mix_ref, gq_ref, gkv_ref, wt_ref, wo_ref, gain_ref, bias_ref, _,
     out_ref, ig_ref, sums_ref,
 ):
     i = pl.program_id(0)
@@ -490,7 +514,7 @@
         sums_ref[r : r + 1, :] += jnp.sum(v, axis=0, keepdims=True)
 
 
-def final(x, g, y, d_ffn, mix, gq, gkv, wt, wo, gains, bias):
+def final(x, g, y, d_ffn, mix, gq, gkv, wt, wo, gains, bias, after):
     block = 512
 
     def rows(i):
@@ -511,7 +535,7 @@
             pl.BlockSpec((D, block), cols), pl.BlockSpec((D, block), cols),
             pl.BlockSpec((128, block), cols),
             pl.BlockSpec((QKV, D), fixed), pl.BlockSpec((D, D), fixed),
-            pl.BlockSpec((2, D), fixed), pl.BlockSpec((1, D), fixed),
+            pl.BlockSpec((2, D), fixed), pl.BlockSpec((1, D), fixed), pl.BlockSpec(memory_space=pl.ANY),
         ],
         out_specs=[
             pl.BlockSpec((block, D), rows), pl.BlockSpec((block, D), rows), pl.BlockSpec((8, D), fixed),
@@ -527,7 +551,7 @@
             flops=2 * TOK * D * (QKV + D), bytes_accessed=36 * MIB, transcendentals=TOK
         ),
         name="closing",
-    )(x, g, y, d_ffn, mix, gq, gkv, wt, wo, gains, bias)
+    )(x, g, y, d_ffn, mix, gq, gkv, wt, wo, gains, bias, after)
 
 
 def eye_block(rows, n, row_lo):
@@ -705,14 +729,12 @@
 
     def scatter(self, x, order):
         x = x.reshape((2,) * len(self.axes) + (-1,) + x.shape[1:])
-        passed = []
         for place in order:
             bit = self.bit(place)
             away = lax.dynamic_index_in_dim(x, 1 - bit, place, keepdims=True).astype(BF)
             keep = lax.dynamic_index_in_dim(x, bit, place, keepdims=True).astype(F32)
             x = keep + self.swap(away, place).astype(F32)
-            passed.append(x)
-        return x.reshape((-1,) + x.shape[len(self.axes) + 1 :]), passed
+        return x.reshape((-1,) + x.shape[len(self.axes) + 1 :])
 
 
 def locate(lengths):
@@ -771,29 +793,35 @@
     y, d_ffn, d_up, d_down, d_bias_up = ffn(
         n_ffn, n_ffn_t, cotangent, g_t, ffn_weights, up_columns(bias_expand[None, :]), so_far[0]
     )
-    halves = [d.reshape(chips, 2, narrow * own, FF) for d in (d_up, d_down)]
-    away = [lax.dynamic_index_in_dim(h, 1 - core, 1, keepdims=False) for h in halves]
-    keep = [lax.dynamic_index_in_dim(h, core, 1, keepdims=False) for h in halves]
-    halves = [
-        (k.astype(F32) + swap(a, "core", 1).astype(F32)).astype(BF) for k, a in zip(keep, away)
+    came = [
+        swap(
+            lax.dynamic_index_in_dim(d.reshape(chips, 2, narrow * own, FF), 1 - core, 1, keepdims=False),
+            "core", 1,
+        ).reshape(D // 2, FF)
+        for d in (d_up, d_down)
     ]
-    packed = jnp.concatenate(halves, axis=2).reshape(-1, 2 * FF)
+    core_id = core.astype(jnp.int32).reshape(1)
+    packed = merge(core_id, d_up, d_down, *came, narrow * own)
     ffn_grads = lax.psum_scatter(packed, "chip", scatter_dimension=0, tiled=True)
-
+    so_far = attention(first_block, qkv_t, grad_mixed_t, cos, sin, packed, 1, 1, so_far)
+    ffn_grads, _ = lax.optimization_barrier((ffn_grads, so_far[2]))
     mix_t, gq_t, _, gkv_t = attention(
-        first_block, qkv_t, grad_mixed_t, cos, sin, packed, 1, HEADS // NH - 1, so_far
+        first_block, qkv_t, grad_mixed_t, cos, sin, ffn_grads, 2, HEADS // NH - 2, so_far
     )
-    ffn_grads, _ = lax.optimization_barrier((ffn_grads, gkv_t))
     ffn_grads = lax.psum_scatter(ffn_grads, "narrow", scatter_dimension=0, tiled=True)
-    d_qkv, d_out, bias_sums = grads(cotangent, mix_t, gq_t, gkv_t, n_attn_t)
+    ffn_grads = lax.optimization_barrier((ffn_grads, gkv_t))[0].astype(F32)
+    new_expand = MUON_MOMENTUM * momentum_expand + up_columns_back(ffn_grads[:, :FF])
+    new_reduce = MUON_MOMENTUM * momentum_reduce + ffn_grads[:, FF:].reshape(-1, D)
+    ffn_momenta = jnp.concatenate([new_expand, new_reduce.reshape(own, 4 * D)], axis=1).astype(BF)
+    ffn_whole = lax.all_gather(ffn_momenta, ("chip", "core", "narrow"), axis=0, tiled=True)
+    d_qkv, d_out, bias_sums = grads(cotangent, mix_t, gq_t, gkv_t, n_attn_t, ffn_momenta)
     scatter_up = [grid.core] + grid.chip + grid.narrow
     scatter_down = [grid.core] + grid.chip[::-1] + grid.narrow
-    qkv_sum, passed = grid.scatter(d_qkv, scatter_up)
-    out_sum, _ = grid.scatter(d_out, scatter_down)
-    ffn_grads = lax.optimization_barrier((ffn_grads, passed[len(grid.chip)]))[0].astype(F32)
+    qkv_sum = grid.scatter(d_qkv, scatter_up)
+    out_sum = grid.scatter(d_out, scatter_down)
     block_output, input_grad, sums = final(
         block_input, cotangent, y, d_ffn, mix_t, gq_t, gkv_t, w_qkv.T, w_out,
-        norm_gains, (bias_output + bias_reduce)[None, :],
+        norm_gains, (bias_output + bias_reduce)[None, :], bias_sums,
     )
     vector_grad = jnp.concatenate(
         [sums[0], sums[1], sums[2], sums[3], bias_sums[0], sums[4], up_columns_back(d_bias_up)[0], sums[4]]
@@ -801,8 +829,6 @@
     for step in up_first:
         vector_grad = vector_grad + grid.swap(vector_grad, step)
 
-    new_expand = MUON_MOMENTUM * momentum_expand + up_columns_back(ffn_grads[:, :FF])
-    new_reduce = MUON_MOMENTUM * momentum_reduce + ffn_grads[:, FF:].reshape(-1, D)
     new_query = MUON_MOMENTUM * momentum_query + qkv_sum[:, :D]
     new_keyval = MUON_MOMENTUM * momentum_keyval + qkv_sum[:, D:QKV]
     new_output = MUON_MOMENTUM * momentum_output + out_sum
@@ -822,11 +848,7 @@
             [lax.dynamic_slice_in_dim(m, r * own, own, 0) for r in (rank, sibling)], axis=0
         )
 
-    ffn_whole = lax.all_gather(
-        jnp.concatenate([new_expand, new_reduce.reshape(own, 4 * D)], axis=1).astype(BF),
-        ("chip", "core", "narrow"), axis=0, tiled=True,
-    )
-    u, q0 = wide_ns(core.astype(jnp.int32).reshape(1), ffn_whole)
+    u, q0 = wide_ns(core_id, ffn_whole)
     rows_m = both_rows(ffn_whole)
     as_up = dot(both_rows(u), ffn_whole[:, :FF])
     as_down = jnp.concatenate(

time: 529 us -> 525 us (level)
  starting transfers between devices: 77.9 us -> 60 us
  waiting for transfers between devices: 151 us -> 161 us
  local copies, waits for them, and re-layouts: 26.2 us -> 31.5 us
    reduce_scatter x1, waiting for transfers between devices: 28.2 us -> 49.8 us  [per_device(): lax.psum_scatter(packed, 'chip', scatter_dimension=0, tiled=True)]
    ppermute x38, starting transfers between devices: 77.7 us -> 59.8 us  [swap(): lax.ppermute(x, axis, [(i, i ^ bit) for i in range(lax.axis_size(axis))])]
    ppermute x38, waiting for transfers between devices: 111 us -> 94 us  [swap(): lax.ppermute(x, axis, [(i, i ^ bit) for i in range(lax.axis_size(axis))])]
    unnamed x95 -> x97, local copies, waits for them, and re-layouts: 10.5 us -> 18.7 us
    reduce_scatter x1, waiting for transfers between devices: 0.01 us -> 7.42 us  [per_device(): lax.psum_scatter(ffn_grads, 'narrow', scatter_dimension=0, tiled=True)]
    pallas_call x2 -> x3, Pallas kernels: 57.5 us -> 60.7 us  [attention(): pl.pallas_call(partial(attention_kernel, opening, closing), grid_spec=plt...]
  transfers between devices with their start and end apart: 42 -> 42, of which waited for: 27 -> 26; matrix products, arithmetic and copies ran while one was open for 6% -> 6% of each run, Pallas kernels for 27% -> 28%
where the time goes in v2:
time: 525 us; the launch traced here: 520 us
  Pallas kernels  224 us (43%)
  waiting for transfers between devices  161 us (31%)
  starting transfers between devices  60 us (11%)
  local copies, waits for them, and re-layouts  31.5 us (6%)
  other arithmetic  16.5 us (3%)
  between operations  15.3 us (3%)
  matrix products  11.3 us (2%)
    ppermute x38, waiting for transfers between devices, swap(): lax.ppermute(x, axis, [(i, i ^ bit) for i in range(lax.axis_size(axis))])  94 us
    pallas_call x1, Pallas kernels, ffn(): pl.pallas_call(ffn_kernel, grid=(FF // FC,), in_specs=[whole((TOK, D)), w...  77.5 us
    pallas_call x3, Pallas kernels, attention(): pl.pallas_call(partial(attention_kernel, opening, closing), grid_spec=plt...  60.7 us
    ppermute x38, starting transfers between devices, swap(): lax.ppermute(x, axis, [(i, i ^ bit) for i in range(lax.axis_size(axis))])  59.8 us
    reduce_scatter x1, waiting for transfers between devices, per_device(): lax.psum_scatter(packed, 'chip', scatter_dimension=0, tiled=True)  49.8 us
    pallas_call x1, Pallas kernels, wide_ns(): pl.pallas_call(wide_kernel, grid_spec=pltpu.PrefetchScalarGridSpec(num_sc...  29.3 us
    pallas_call x1, Pallas kernels, square_ns(): pl.pallas_call(square_kernel, in_specs=[pl.BlockSpec(memory_space=pltpu.V...  19.4 us
    unnamed x97, local copies, waits for them, and re-layouts  18.7 us
  transfers between devices with their start and end apart: 42, of which 26 were waited for; matrix products, arithmetic and copies ran while one was open for 6% of the time, Pallas kernels for 28%

profile of v2, /device:TPU:0, one launch (start us, length us, event | category | flops | bytes accessed | tf_op | source)
XLA Modules:
  0.0 519.7 jit_solution(13473988559196675382)
XLA Ops:
  10.5 3.1 collective-permute-start.5
  15.9 9.0 %prepare.1 = (bf16[768,2048]{1,0:T(8,128)(2,1)S(1)}, bf16[2048,768]{1,0:T(8,128)(2,1)}, bf16[768,2048]{1,0:T(8,128)(2,1)}, bf16[768,2048]{1,0:T(8,128)(2,1)}) custom-call(bf16[2048,768]{1,0:T(8,128)(2,1)} %x_ref.3, bf16[2048,768]{1,0:T(8,128)(2,1)} %g_ref.7, f32[2,768]{1,0:T(2,128)S(1)} %copy-done.13, f32[2,768]{1,0:T(2,128)S(1)} %copy-done.15), custom_call_target="tpu_custom_call" | custom-call | flops 31457280 | bytes 18874368 | tf_op jit(solution)/shard_map/prepare/pallas_call | solution.py:419
  24.9 3.1 collective-permute-start.6
  28.1 9.7 %collective-permute-done.6 = bf16[1,1,1,1,2,24,768]{6,5,4,3,2,1,0:T(8,128)(2,1)S(1)} collective-permute-done((bf16[1,1,1,1,2,24,768]{6,5,4,3,2,1,0:T(8,128)(2,1)S(1)}, bf16[1,1,1,1,2,24,768]{6,5,4,3,2,1,0:T(8,128)(2,1)S(1)}, u32[]{:S(2)}, u32[]{:S(2)}) %collective-permute-start.6) | collective-permute-done | bytes 73760 | tf_op jit(solution)/shard_map/ppermute | solution.py:699
  44.7 2.7 collective-permute-done.2
  48.9 9.8 %collective-permute-done.8 = bf16[2,1,1,2,2,24,768]{6,5,4,3,2,1,0:T(8,128)(2,1)S(1)} collective-permute-done((bf16[2,1,1,2,2,24,768]{6,5,4,3,2,1,0:T(8,128)(2,1)S(1)}, bf16[2,1,1,2,2,24,768]{6,5,4,3,2,1,0:T(8,128)(2,1)S(1)}, u32[]{:S(2)}, u32[]{:S(2)}) %collective-permute-start.8) | collective-permute-done | bytes 294944 | tf_op jit(solution)/shard_map/ppermute | solution.py:699
  61.0 2.1 copy-done.21
  63.1 4.0 convolution_convert_fusion.refs_2_
  68.0 5.0 broadcast_add_fusion.refs_1_.refs_5_
  73.1 20.2 %attention.3 = (bf16[768,2048]{1,0:T(8,128)(2,1)S(1)}, bf16[768,2048]{1,0:T(8,128)(2,1)}, f32[2048,128]{1,0:T(8,128)S(1)}) custom-call(s32[4]{0:T(128)S(1)} %and_select_fusion.refs_0_, f32[896,2048]{1,0:T(8,128)} %broadcast_add_fusion.refs_1_.refs_5_, bf16[768,2048]{1,0:T(8,128)(2,1)} %convolution_convert_fusion.refs_2_, ...), custom_call_target="tpu_custom_call" | custom-call | flops 25769803776 | bytes 5242880 | tf_op jit(solution)/shard_map/attention/pallas_call | solution.py:232
  93.2 1.7 copy-done.6
  95.9 10.2 %all-gather.3.cloned.1.call-done.up_ref.down_ref = bf16[768,6144]{1,0:T(8,128)(2,1)} async-done(((bf16[24,6144]{1,0:T(8,128)(2,1)}), bf16[768,6144]{1,0:T(8,128)(2,1)}) %all-gather.3.cloned.1.call-update) | async-done | bytes 9437200 | tf_op jit(solution)/shard_map/all_gather | solution.py:776
  106.1 77.5 %ffn.1 = (f32[2048,768]{1,0:T(8,128)}, f32[2048,768]{1,0:T(8,128)}, bf16[768,3072]{1,0:T(8,128)(2,1)}, bf16[768,3072]{1,0:T(8,128)(2,1)}, f32[1,3072]{1,0:T(1,128)}) custom-call(bf16[2048,768]{1,0:T(8,128)(2,1)} %get-tuple-element.45.x_ref, bf16[768,2048]{1,0:T(8,128)(2,1)} %get-tuple-element.46.xt_ref, bf16[2048,768]{1,0:T(8,128)(2,1)} %g_ref.7, ...), custom_call_target="tpu_custom_call" | custom-call | flops 57982058496 | bytes 46137344 | tf_op jit(solution)/shard_map/ffn/pallas_call | solution.py:331
  183.6 2.0 dynamic-slice_bitcast_fusion
  187.1 3.1 collective-permute-done.11
  190.2 3.4 collective-permute-done.10
  194.7 2.2 copy-done
  197.0 1.8 copy-done.7
  200.0 19.8 %attention.4 = (bf16[768,2048]{1,0:T(8,128)(2,1)S(1)}, bf16[768,2048]{1,0:T(8,128)(2,1)}, f32[2048,128]{1,0:T(8,128)S(1)}) custom-call(s32[4]{0:T(128)S(1)} %and_select_fusion.refs_0_, f32[896,2048]{1,0:T(8,128)} %broadcast_add_fusion.refs_1_.refs_5_, ...), custom_call_target="tpu_custom_call", output_to_operand_aliasing={{0}: (7, {}), {1}: (8, {})} | custom-call | flops 25769803776 | bytes 5242880 | tf_op jit(solution)/shard_map/attention/pallas_call | solution.py:232
  222.5 49.8 %reduce-scatter.3.cloned.1.call-done.refs_6_ = bf16[96,6144]{1,0:T(8,128)(2,1)} async-done(((bf16[384,6144]{1,0:T(8,128)(2,1)}), bf16[96,6144]{1,0:T(8,128)(2,1)}) %reduce-scatter.3.cloned.1.call-update) | async-done | bytes 1179664 | tf_op jit(solution)/shard_map/reduce_scatter | solution.py:805
  274.9 20.7 %attention.5 = (bf16[768,2048]{1,0:T(8,128)(2,1)}, bf16[768,2048]{1,0:T(8,128)(2,1)}, f32[2048,128]{1,0:T(8,128)}, bf16[128,2048]{1,0:T(8,128)(2,1)S(1)}) custom-call(s32[4]{0:T(128)S(1)} %and_select_fusion.refs_0_, f32[896,2048]{1,0:T(8,128)} %broadcast_add_fusion.refs_1_.refs_5_, ...), custom_call_target="tpu_custom_call", output_to_operand_aliasing={{0}: (7, {}), {1}: (8, {})} | custom-call | flops 25769803776 | bytes 5242880 | tf_op jit(solution)/shard_map/attention/pallas_call | solution.py:232
  296.4 7.4 %reduce-scatter.5.cloned.1.call-done = bf16[24,6144]{1,0:T(8,128)(2,1)} async-done(((bf16[96,6144]{1,0:T(8,128)(2,1)}), bf16[24,6144]{1,0:T(8,128)(2,1)}) %reduce-scatter.5.cloned.1.call-update) | async-done | bytes 294928 | tf_op jit(solution)/shard_map/reduce_scatter | solution.py:811
  313.0 11.3 %grads.1 = (bf16[768,896]{1,0:T(8,128)(2,1)S(1)}, bf16[768,768]{1,0:T(8,128)(2,1)S(1)}, f32[8,896]{1,0:T(8,128)S(1)}) custom-call(bf16[2048,768]{1,0:T(8,128)(2,1)} %g_ref.7, bf16[768,2048]{1,0:T(8,128)(2,1)} %get-tuple-element.60.mix_ref, bf16[768,2048]{1,0:T(8,128)(2,1)} %get-tuple-element.61.gq_ref, bf16[128,2048]{1,0:T(8,128)(2,1)S(1)} %copy-done.12, ...), custom_call_target="tpu_custom_call" | custom-call | flops 5234491392 | bytes 16777216 | tf_op jit(solution)/shard_map/grads/pallas_call | solution.py:467
  325.8 15.4 %closing.1 = (bf16[2048,768]{1,0:T(8,128)(2,1)}, f32[2048,768]{1,0:T(8,128)}, f32[8,768]{1,0:T(8,128)S(1)}) custom-call(bf16[2048,768]{1,0:T(8,128)(2,1)} %x_ref.3, bf16[2048,768]{1,0:T(8,128)(2,1)} %g_ref.7, f32[2048,768]{1,0:T(8,128)} %get-tuple-element.50.y_ref, f32[2048,768]{1,0:T(8,128)} %get-tuple-element.51.df_ref, ...), custom_call_target="tpu_custom_call" | custom-call | flops 5234491392 | bytes 37748736 | tf_op jit(solution)/shard_map/closing/pallas_call | solution.py:529
  341.5 3.1 collective-permute-start.18
  344.6 17.5 %collective-permute-start.33 = (f32[8576]{0:T(1024)S(1)}, f32[8576]{0:T(1024)S(1)}, u32[]{:S(2)}, u32[]{:S(2)}) collective-permute-start(f32[8576]{0:T(1024)S(1)} %constant_dynamic-update-slice_fusion), channel_id=1, source_target_pairs={{0,1},{1,0},{2,3},{3,2},{4,5},{5,4},{6,7},{7,6},{8,9},{9,8},{10,11... | collective-permute-start | bytes 102920 | tf_op jit(solution)/shard_map/ppermute | solution.py:699
  362.2 3.3 collective-permute-done.33
  365.5 3.4 collective-permute-start.34
  368.8 3.1 collective-permute-done.34
  371.9 2.2 collective-permute-start.35
  378.6 3.1 collective-permute-done.19
  382.8 11.0 %collective-permute-done.13 = bf16[1,2,1,2,2,24,896]{6,5,4,3,2,1,0:T(8,128)(2,1)S(1)} collective-permute-done((bf16[1,2,1,2,2,24,896]{6,5,4,3,2,1,0:T(8,128)(2,1)S(1)}, bf16[1,2,1,2,2,24,896]{6,5,4,3,2,1,0:T(8,128)(2,1)S(1)}, u32[]{:S(2)}, u32[]{:S(2)}) %collective-permute-start.13) | collective-permute-done | bytes 344096 | tf_op jit(solution)/shard_map/ppermute | solution.py:699
  394.0 9.3 %collective-permute-done.14 = bf16[1,1,1,2,2,24,896]{6,5,4,3,2,1,0:T(8,128)(2,1)S(1)} collective-permute-done((bf16[1,1,1,2,2,24,896]{6,5,4,3,2,1,0:T(8,128)(2,1)S(1)}, bf16[1,1,1,2,2,24,896]{6,5,4,3,2,1,0:T(8,128)(2,1)S(1)}, u32[]{:S(2)}, u32[]{:S(2)}) %collective-permute-start.14) | collective-permute-done | bytes 172064 | tf_op jit(solution)/shard_map/ppermute | solution.py:699
  404.5 3.0 collective-permute-start.21
  407.5 4.9 collective-permute-done.15
  413.9 3.4 collective-permute-done.16
  420.1 2.6 collective-permute-done.36
  424.9 2.2 collective-permute-done.27
  427.1 2.1 collective-permute-start.28
  429.3 1.8 collective-permute-start.24
  431.1 3.7 collective-permute-done.28
  435.0 2.5 collective-permute-done.24
  438.2 1.9 collective-permute-done.29
  441.0 4.4 collective-permute-done.25
  447.8 2.5 collective-permute-done.30
  450.5 4.2 collective-permute-done.26
  454.9 19.4 %square_ns.1 = (f32[768,768]{1,0:T(8,128)S(1)}, f32[768,128]{1,0:T(8,128)S(1)}) custom-call(bf16[768,768]{1,0:T(8,128)(2,1)S(1)} %pad_maximum_fusion.1.m_ref, bf16[768,128]{1,0:T(8,128)(2,1)S(1)} %slice.123.kv_ref), custom_call_target="tpu_custom_call" | custom-call | flops 15401484288 | bytes 6291456 | tf_op jit(solution)/shard_map/square_ns/pallas_call | solution.py:685
  474.4 29.3 %wide_ns.1 = (bf16[768,768]{1,0:T(8,128)(2,1)S(1)}, f32[1,768]{1,0:T(1,128)S(1)}) custom-call(s32[1]{0:T(128)} %bitcast.10._.down_ref, bf16[768,6144]{1,0:T(8,128)(2,1)} %all-gather.5.cloned.1.call-done.m_ref), custom_call_target="tpu_custom_call" | custom-call | flops 21743271936 | bytes 6291456 | tf_op jit(solution)/shard_map/wide_ns/pallas_call | solution.py:637
  (283 shorter events, 65.7 us)
Async XLA Ops:
  7.2 98.9 %all-gather.3.cloned.1.call-start = ((), (), s32[]{:S(2)}) async-start(), calls=%async_computation.2 | async-start | bytes 9732096 | tf_op jit(solution)/shard_map/all_gather | solution.py:776
  10.4 261.9 %reduce-scatter.3.cloned.1.call-start = ((), (), s32[]{:S(2)}) async-start(), calls=%async_computation.3 | async-start | bytes 5898240 | tf_op jit(solution)/shard_map/reduce_scatter | solution.py:805
  10.5 14.3 %collective-permute-start.5 = (bf16[1,1,1,1,1,24,768]{6,5,4,3,2,1,0:T(8,128)(2,1)S(1)}, bf16[1,1,1,1,1,24,768]{6,5,4,3,2,1,0:T(8,128)(2,1)S(1)}, u32[]{:S(2)}, u32[]{:S(2)}) collective-permute-start(bf16[1,1,1,1,1,24,768]{6,5,4,3,2,1,0:T(8,128)(2,1)S(1)} %convert_bitcast_fusion), channel_id=1, source_target_pairs={{0,1},{1,0},{2,3},{3,2},{4,5},{5,4},{6,7},{7,6},{8,9},{9,8},{10,11... | collective-permute-start | bytes 110600 | tf_op jit(solution)/shard_map/ppermute | solution.py:699
  13.6 14.3 %collective-permute-start = (bf16[1,1,1,1,1,24,896]{6,5,4,3,2,1,0:T(8,128)(2,1)S(1)}, bf16[1,1,1,1,1,24,896]{6,5,4,3,2,1,0:T(8,128)(2,1)S(1)}, u32[]{:S(2)}, u32[]{:S(2)}) collective-permute-start(bf16[1,1,1,1,1,24,896]{6,5,4,3,2,1,0:T(8,128)(2,1)S(1)} %pad_maximum_fusion.24), channel_id=1, source_target_pairs={{0,1},{1,0},{2,3},{3,2},{4,5},{5,4},{6,7},{7,6},{8,9},{9,8},{10,11... | collective-permute-start | bytes 129032 | tf_op jit(solution)/shard_map/ppermute | solution.py:699
  24.8 42.7 %copy-start.5 = (bf16[768,2048]{1,0:T(8,128)(2,1)}, bf16[768,2048]{1,0:T(8,128)(2,1)S(1)}, u32[]{:S(2)}) copy-start(bf16[768,2048]{1,0:T(8,128)(2,1)S(1)} %get-tuple-element.48.nt_ref) | copy-start | bytes 9437188
  24.9 12.9 %collective-permute-start.6 = (bf16[1,1,1,1,2,24,768]{6,5,4,3,2,1,0:T(8,128)(2,1)S(1)}, bf16[1,1,1,1,2,24,768]{6,5,4,3,2,1,0:T(8,128)(2,1)S(1)}, u32[]{:S(2)}, u32[]{:S(2)}) collective-permute-start(bf16[1,1,1,1,2,24,768]{6,5,4,3,2,1,0:T(8,128)(2,1)S(1)} %pad_maximum_fusion.20), channel_id=1, source_target_pairs={{0,2},{1,3},{2,0},{3,1},{4,6},{5,7},{6,4},{7,5},{8,10},{9,11},{10,... | collective-permute-start | bytes 221192 | tf_op jit(solution)/shard_map/ppermute | solution.py:699
  28.0 11.7 %collective-permute-start.1 = (bf16[1,1,1,1,2,24,896]{6,5,4,3,2,1,0:T(8,128)(2,1)S(1)}, bf16[1,1,1,1,2,24,896]{6,5,4,3,2,1,0:T(8,128)(2,1)S(1)}, u32[]{:S(2)}, u32[]{:S(2)}) collective-permute-start(bf16[1,1,1,1,2,24,896]{6,5,4,3,2,1,0:T(8,128)(2,1)S(1)} %pad_maximum_fusion.19), channel_id=1, source_target_pairs={{0,2},{1,3},{2,0},{3,1},{4,6},{5,7},{6,4},{7,5},{8,10},{9,11},{10,... | collective-permute-start | bytes 258056 | tf_op jit(solution)/shard_map/ppermute | solution.py:699
  37.8 5.2 %collective-permute-start.7 = (bf16[1,1,1,2,2,24,768]{6,5,4,3,2,1,0:T(8,128)(2,1)S(1)}, bf16[1,1,1,2,2,24,768]{6,5,4,3,2,1,0:T(8,128)(2,1)S(1)}, u32[]{:S(2)}, u32[]{:S(2)}) collective-permute-start(bf16[1,1,1,2,2,24,768]{6,5,4,3,2,1,0:T(8,128)(2,1)S(1)} %pad_maximum_fusion.16), channel_id=1, source_target_pairs={{0,16},{8,24},{16,0},{24,8},{1,17},{9,25},{17,1},{25,9},{2,18},{10... | collective-permute-start | bytes 442376 | tf_op jit(solution)/shard_map/ppermute | solution.py:699
  39.8 7.7 %collective-permute-start.2 = (bf16[1,1,1,2,2,24,896]{6,5,4,3,2,1,0:T(8,128)(2,1)S(1)}, bf16[1,1,1,2,2,24,896]{6,5,4,3,2,1,0:T(8,128)(2,1)S(1)}, u32[]{:S(2)}, u32[]{:S(2)}) collective-permute-start(bf16[1,1,1,2,2,24,896]{6,5,4,3,2,1,0:T(8,128)(2,1)S(1)} %pad_maximum_fusion.15), channel_id=1, source_target_pairs={{0,8},{8,0},{16,24},{24,16},{1,9},{9,1},{17,25},{25,17},{2,10},{10... | collective-permute-start | bytes 516104 | tf_op jit(solution)/shard_map/ppermute | solution.py:699
  43.1 15.5 %collective-permute-start.8 = (bf16[2,1,1,2,2,24,768]{6,5,4,3,2,1,0:T(8,128)(2,1)S(1)}, bf16[2,1,1,2,2,24,768]{6,5,4,3,2,1,0:T(8,128)(2,1)S(1)}, u32[]{:S(2)}, u32[]{:S(2)}) collective-permute-start(bf16[2,1,1,2,2,24,768]{6,5,4,3,2,1,0:T(8,128)(2,1)S(1)} %pad_maximum_fusion.11), channel_id=1, source_target_pairs={{0,8},{8,0},{16,24},{24,16},{1,9},{9,1},{17,25},{25,17},{2,10},{10... | collective-permute-start | bytes 884744 | tf_op jit(solution)/shard_map/ppermute | solution.py:699
  47.5 11.3 %collective-permute-start.3 = (bf16[1,2,1,2,2,24,896]{6,5,4,3,2,1,0:T(8,128)(2,1)S(1)}, bf16[1,2,1,2,2,24,896]{6,5,4,3,2,1,0:T(8,128)(2,1)S(1)}, u32[]{:S(2)}, u32[]{:S(2)}) collective-permute-start(bf16[1,2,1,2,2,24,896]{6,5,4,3,2,1,0:T(8,128)(2,1)S(1)} %pad_maximum_fusion.9), channel_id=1, source_target_pairs={{0,16},{8,24},{16,0},{24,8},{1,17},{9,25},{17,1},{25,9},{2,18},{10... | collective-permute-start | bytes 1032200 | tf_op jit(solution)/shard_map/ppermute | solution.py:699
  58.7 2.1 collective-permute-start.9
  59.0 8.2 %collective-permute-start.4 = (bf16[2,2,1,2,2,24,896]{6,5,4,3,2,1,0:T(8,128)(2,1)S(1)}, bf16[2,2,1,2,2,24,896]{6,5,4,3,2,1,0:T(8,128)(2,1)S(1)}, u32[]{:S(2)}, u32[]{:S(2)}) collective-permute-start(bf16[2,2,1,2,2,24,896]{6,5,4,3,2,1,0:T(8,128)(2,1)S(1)} %pad_maximum_fusion.5), channel_id=1, source_target_pairs={{0,4},{4,0},{1,5},{5,1},{2,6},{6,2},{3,7},{7,3},{8,12},{12,8},{9,1... | collective-permute-start | bytes 2064392 | tf_op jit(solution)/shard_map/ppermute | solution.py:699
  185.6 4.6 collective-permute-start.11
  186.8 6.8 %collective-permute-start.10 = (bf16[4,96,3072]{2,1,0:T(8,128)(2,1)S(1)}, bf16[4,96,3072]{2,1,0:T(8,128)(2,1)S(1)}, u32[]{:S(2)}, u32[]{:S(2)}) collective-permute-start(bf16[4,96,3072]{2,1,0:T(8,128)(2,1)S(1)} %dynamic-slice_bitcast_fusion.1), channel_id=1, source_target_pairs={{0,4},{4,0},{1,5},{5,1},{2,6},{6,2},{3,7},{7,3},{8,12},{12,8},{9,1... | collective-permute-start | bytes 7077896 | tf_op jit(solution)/shard_map/ppermute | solution.py:699
  196.9 106.9 %reduce-scatter.5.cloned.1.call-start = ((), (), s32[]{:S(2)}) async-start(), calls=%async_computation.4 | async-start | bytes 1474560 | tf_op jit(solution)/shard_map/reduce_scatter | solution.py:811
  272.3 202.1 %all-gather.5.cloned.1.call-start = ((), (), s32[]{:S(2)}) async-start(), calls=%async_computation.5 | async-start | bytes 9732096 | tf_op jit(solution)/shard_map/all_gather | solution.py:816
  324.3 17.0 %collective-permute-start.17 = (bf16[2,2,1,2,2,24,768]{6,5,4,3,2,1,0:T(8,128)(2,1)S(1)}, bf16[2,2,1,2,2,24,768]{6,5,4,3,2,1,0:T(8,128)(2,1)S(1)}, u32[]{:S(2)}, u32[]{:S(2)}) collective-permute-start(bf16[2,2,1,2,2,24,768]{6,5,4,3,2,1,0:T(8,128)(2,1)S(1)} %constant_dynamic-slice_fusion.5), channel_id=1, source_target_pairs={{0,4},{4,0},{1,5},{5,1},{2,6},{6,2},{3,7},{7,3},{8,12},{12,8},{9,1... | collective-permute-start | bytes 1769480 | tf_op jit(solution)/shard_map/ppermute | solution.py:699
  325.3 50.5 %collective-permute-start.12 = (bf16[2,2,1,2,2,24,896]{6,5,4,3,2,1,0:T(8,128)(2,1)}, bf16[2,2,1,2,2,24,896]{6,5,4,3,2,1,0:T(8,128)(2,1)}, u32[]{:S(2)}, u32[]{:S(2)}) collective-permute-start(bf16[2,2,1,2,2,24,896]{6,5,4,3,2,1,0:T(8,128)(2,1)} %constant_dynamic-slice_fusion.6), channel_id=1, source_target_pairs={{0,4},{4,0},{1,5},{5,1},{2,6},{6,2},{3,7},{7,3},{8,12},{12,8},{9,1... | collective-permute-start | bytes 2064392 | tf_op jit(solution)/shard_map/ppermute | solution.py:699
  341.5 32.6 %collective-permute-start.18 = (bf16[2,1,1,2,2,24,768]{6,5,4,3,2,1,0:T(8,128)(2,1)S(1)}, bf16[2,1,1,2,2,24,768]{6,5,4,3,2,1,0:T(8,128)(2,1)}, u32[]{:S(2)}, u32[]{:S(2)}) collective-permute-start(bf16[2,1,1,2,2,24,768]{6,5,4,3,2,1,0:T(8,128)(2,1)S(1)} %dynamic-slice_convert_fusion.1), channel_id=1, source_target_pairs={{0,8},{8,0},{16,24},{24,16},{1,9},{9,1},{17,25},{25,17},{2,10},{10... | collective-permute-start | bytes 884744 | tf_op jit(solution)/shard_map/ppermute | solution.py:699
  344.6 20.8 %collective-permute-start.33 = (f32[8576]{0:T(1024)S(1)}, f32[8576]{0:T(1024)S(1)}, u32[]{:S(2)}, u32[]{:S(2)}) collective-permute-start(f32[8576]{0:T(1024)S(1)} %constant_dynamic-update-slice_fusion), channel_id=1, source_target_pairs={{0,1},{1,0},{2,3},{3,2},{4,5},{5,4},{6,7},{7,6},{8,9},{9,8},{10,11... | collective-permute-start | bytes 102920 | tf_op jit(solution)/shard_map/ppermute | solution.py:699
  365.5 6.5 %collective-permute-start.34 = (f32[8576]{0:T(1024)S(1)}, f32[8576]{0:T(1024)S(1)}, u32[]{:S(2)}, u32[]{:S(2)}) collective-permute-start(f32[8576]{0:T(1024)S(1)} %add.279), channel_id=1, source_target_pairs={{0,2},{1,3},{2,0},{3,1},{4,6},{5,7},{6,4},{7,5},{8,10},{9,11},{10,... | collective-permute-start | bytes 102920 | tf_op jit(solution)/shard_map/ppermute | solution.py:699
  371.9 46.7 %collective-permute-start.35 = (f32[8576]{0:T(1024)S(1)}, f32[8576]{0:T(1024)S(1)}, u32[]{:S(2)}, u32[]{:S(2)}) collective-permute-start(f32[8576]{0:T(1024)S(1)} %add.280), channel_id=1, source_target_pairs={{0,8},{8,0},{16,24},{24,16},{1,9},{9,1},{17,25},{25,17},{2,10},{10... | collective-permute-start | bytes 102920 | tf_op jit(solution)/shard_map/ppermute | solution.py:699
  375.2 6.5 %collective-permute-start.19 = (bf16[1,1,1,2,2,24,768]{6,5,4,3,2,1,0:T(8,128)(2,1)S(1)}, bf16[1,1,1,2,2,24,768]{6,5,4,3,2,1,0:T(8,128)(2,1)S(1)}, u32[]{:S(2)}, u32[]{:S(2)}) collective-permute-start(bf16[1,1,1,2,2,24,768]{6,5,4,3,2,1,0:T(8,128)(2,1)S(1)} %dynamic-slice_convert_fusion.3), channel_id=1, source_target_pairs={{0,16},{8,24},{16,0},{24,8},{1,17},{9,25},{17,1},{25,9},{2,18},{10... | collective-permute-start | bytes 442376 | tf_op jit(solution)/shard_map/ppermute | solution.py:699
  377.1 16.7 %collective-permute-start.13 = (bf16[1,2,1,2,2,24,896]{6,5,4,3,2,1,0:T(8,128)(2,1)S(1)}, bf16[1,2,1,2,2,24,896]{6,5,4,3,2,1,0:T(8,128)(2,1)S(1)}, u32[]{:S(2)}, u32[]{:S(2)}) collective-permute-start(bf16[1,2,1,2,2,24,896]{6,5,4,3,2,1,0:T(8,128)(2,1)S(1)} %dynamic-slice_convert_fusion), channel_id=1, source_target_pairs={{0,16},{8,24},{16,0},{24,8},{1,17},{9,25},{17,1},{25,9},{2,18},{10... | collective-permute-start | bytes 1032200 | tf_op jit(solution)/shard_map/ppermute | solution.py:699
  381.8 12.2 %collective-permute-start.20 = (bf16[1,1,1,1,2,24,768]{6,5,4,3,2,1,0:T(8,128)(2,1)S(1)}, bf16[1,1,1,1,2,24,768]{6,5,4,3,2,1,0:T(8,128)(2,1)S(1)}, u32[]{:S(2)}, u32[]{:S(2)}) collective-permute-start(bf16[1,1,1,1,2,24,768]{6,5,4,3,2,1,0:T(8,128)(2,1)S(1)} %dynamic-slice_convert_fusion.5), channel_id=1, source_target_pairs={{0,2},{1,3},{2,0},{3,1},{4,6},{5,7},{6,4},{7,5},{8,10},{9,11},{10,... | collective-permute-start | bytes 221192 | tf_op jit(solution)/shard_map/ppermute | solution.py:699
  393.8 19.4 %copy-start.35 = (f32[24,768]{1,0:T(8,128)S(1)}, f32[24,768]{1,0:T(8,128)}, u32[]{:S(2)}) copy-start(f32[24,768]{1,0:T(8,128)} %param.28) | copy-start | bytes 221188
  393.8 23.5 %copy-start.43 = (f32[24,128]{1,0:T(8,128)S(1)}, f32[24,128]{1,0:T(8,128)}, u32[]{:S(2)}) copy-start(f32[24,128]{1,0:T(8,128)} %param.27) | copy-start | bytes 36868
  393.8 24.1 %copy-start.36 = (f32[24,768]{1,0:T(8,128)S(1)}, f32[24,768]{1,0:T(8,128)}, u32[]{:S(2)}) copy-start(f32[24,768]{1,0:T(8,128)} %param.26) | copy-start | bytes 221188
  393.9 9.4 %collective-permute-start.14 = (bf16[1,1,1,2,2,24,896]{6,5,4,3,2,1,0:T(8,128)(2,1)S(1)}, bf16[1,1,1,2,2,24,896]{6,5,4,3,2,1,0:T(8,128)(2,1)S(1)}, u32[]{:S(2)}, u32[]{:S(2)}) collective-permute-start(bf16[1,1,1,2,2,24,896]{6,5,4,3,2,1,0:T(8,128)(2,1)S(1)} %dynamic-slice_convert_fusion.2), channel_id=1, source_target_pairs={{0,8},{8,0},{16,24},{24,16},{1,9},{9,1},{17,25},{25,17},{2,10},{10... | collective-permute-start | bytes 516104 | tf_op jit(solution)/shard_map/ppermute | solution.py:699
  394.0 26.1 %copy-start.16 = (f32[2,768]{1,0:T(2,128)S(1)}, f32[2,768]{1,0:T(2,128)}, u32[]{:S(2)}) copy-start(f32[2,768]{1,0:T(2,128)} %shift_ref.1) | copy-start | bytes 18436
  403.3 9.1 %collective-permute-start.15 = (bf16[1,1,1,1,2,24,896]{6,5,4,3,2,1,0:T(8,128)(2,1)S(1)}, bf16[1,1,1,1,2,24,896]{6,5,4,3,2,1,0:T(8,128)(2,1)S(1)}, u32[]{:S(2)}, u32[]{:S(2)}) collective-permute-start(bf16[1,1,1,1,2,24,896]{6,5,4,3,2,1,0:T(8,128)(2,1)S(1)} %dynamic-slice_convert_fusion.4), channel_id=1, source_target_pairs={{0,2},{1,3},{2,0},{3,1},{4,6},{5,7},{6,4},{7,5},{8,10},{9,11},{10,... | collective-permute-start | bytes 258056 | tf_op jit(solution)/shard_map/ppermute | solution.py:699
  404.5 8.8 %collective-permute-start.21 = (bf16[1,1,1,1,1,24,768]{6,5,4,3,2,1,0:T(8,128)(2,1)S(1)}, bf16[1,1,1,1,1,24,768]{6,5,4,3,2,1,0:T(8,128)(2,1)S(1)}, u32[]{:S(2)}, u32[]{:S(2)}) collective-permute-start(bf16[1,1,1,1,1,24,768]{6,5,4,3,2,1,0:T(8,128)(2,1)S(1)} %dynamic-slice_convert_fusion.7), channel_id=1, source_target_pairs={{0,1},{1,0},{2,3},{3,2},{4,5},{5,4},{6,7},{7,6},{8,9},{9,8},{10,11... | collective-permute-start | bytes 110600 | tf_op jit(solution)/shard_map/ppermute | solution.py:699
  412.5 4.8 collective-permute-start.16
  418.6 4.1 collective-permute-start.22
  418.7 4.0 collective-permute-start.36
  422.7 24.4 %collective-permute-start.37 = (f32[8576]{0:T(1024)S(1)}, f32[8576]{0:T(1024)S(1)}, u32[]{:S(2)}, u32[]{:S(2)}) collective-permute-start(f32[8576]{0:T(1024)S(1)} %add.282), channel_id=1, source_target_pairs={{0,4},{4,0},{1,5},{5,1},{2,6},{6,2},{3,7},{7,3},{8,12},{12,8},{9,1... | collective-permute-start | bytes 102920 | tf_op jit(solution)/shard_map/ppermute | solution.py:699
  422.8 4.3 collective-permute-start.27
  423.7 5.5 %collective-permute-start.23 = (bf16[1,1,1,1,1,48,512]{6,5,4,3,2,1,0:T(8,128)(2,1)S(1)}, bf16[1,1,1,1,1,48,512]{6,5,4,3,2,1,0:T(8,128)(2,1)S(1)}, u32[]{:S(2)}, u32[]{:S(2)}) collective-permute-start(bf16[1,1,1,1,1,48,512]{6,5,4,3,2,1,0:T(8,128)(2,1)S(1)} %fusion.24), channel_id=1, source_target_pairs={{0,1},{1,0},{2,3},{3,2},{4,5},{5,4},{6,7},{7,6},{8,9},{9,8},{10,11... | collective-permute-start | bytes 147464 | tf_op jit(solution)/shard_map/ppermute | solution.py:699
  427.1 7.7 %collective-permute-start.28 = (bf16[1,1,1,1,2,48,384]{6,5,4,3,2,1,0:T(8,128)(2,1)S(1)}, bf16[1,1,1,1,2,48,384]{6,5,4,3,2,1,0:T(8,128)(2,1)S(1)}, u32[]{:S(2)}, u32[]{:S(2)}) collective-permute-start(bf16[1,1,1,1,2,48,384]{6,5,4,3,2,1,0:T(8,128)(2,1)S(1)} %pad_maximum_fusion.21), channel_id=1, source_target_pairs={{0,2},{1,3},{2,0},{3,1},{4,6},{5,7},{6,4},{7,5},{8,10},{9,11},{10,... | collective-permute-start | bytes 221192 | tf_op jit(solution)/shard_map/ppermute | solution.py:699
  429.3 8.2 %collective-permute-start.24 = (bf16[1,1,1,1,2,48,512]{6,5,4,3,2,1,0:T(8,128)(2,1)S(1)}, bf16[1,1,1,1,2,48,512]{6,5,4,3,2,1,0:T(8,128)(2,1)S(1)}, u32[]{:S(2)}, u32[]{:S(2)}) collective-permute-start(bf16[1,1,1,1,2,48,512]{6,5,4,3,2,1,0:T(8,128)(2,1)S(1)} %pad_maximum_fusion.18), channel_id=1, source_target_pairs={{0,2},{1,3},{2,0},{3,1},{4,6},{5,7},{6,4},{7,5},{8,10},{9,11},{10,... | collective-permute-start | bytes 294920 | tf_op jit(solution)/shard_map/ppermute | solution.py:699
  434.9 5.2 %collective-permute-start.29 = (bf16[1,1,1,2,2,48,384]{6,5,4,3,2,1,0:T(8,128)(2,1)S(1)}, bf16[1,1,1,2,2,48,384]{6,5,4,3,2,1,0:T(8,128)(2,1)S(1)}, u32[]{:S(2)}, u32[]{:S(2)}) collective-permute-start(bf16[1,1,1,2,2,48,384]{6,5,4,3,2,1,0:T(8,128)(2,1)S(1)} %pad_maximum_fusion.17), channel_id=1, source_target_pairs={{0,16},{8,24},{16,0},{24,8},{1,17},{9,25},{17,1},{25,9},{2,18},{10... | collective-permute-start | bytes 442376 | tf_op jit(solution)/shard_map/ppermute | solution.py:699
  437.5 9.6 %copy-start.39 = (f32[8576]{0:T(1024)S(1)}, f32[8576]{0:T(1024)}, u32[]{:S(2)}) copy-start(f32[8576]{0:T(1024)} %param.35) | copy-start | bytes 102916
  437.5 7.9 %collective-permute-start.25 = (bf16[1,1,1,2,2,48,512]{6,5,4,3,2,1,0:T(8,128)(2,1)S(1)}, bf16[1,1,1,2,2,48,512]{6,5,4,3,2,1,0:T(8,128)(2,1)S(1)}, u32[]{:S(2)}, u32[]{:S(2)}) collective-permute-start(bf16[1,1,1,2,2,48,512]{6,5,4,3,2,1,0:T(8,128)(2,1)S(1)} %pad_maximum_fusion.14), channel_id=1, source_target_pairs={{0,8},{8,0},{16,24},{24,16},{1,9},{9,1},{17,25},{25,17},{2,10},{10... | collective-permute-start | bytes 589832 | tf_op jit(solution)/shard_map/ppermute | solution.py:699
  440.2 10.1 %collective-permute-start.30 = (bf16[2,1,1,2,2,48,384]{6,5,4,3,2,1,0:T(8,128)(2,1)S(1)}, bf16[2,1,1,2,2,48,384]{6,5,4,3,2,1,0:T(8,128)(2,1)S(1)}, u32[]{:S(2)}, u32[]{:S(2)}) collective-permute-start(bf16[2,1,1,2,2,48,384]{6,5,4,3,2,1,0:T(8,128)(2,1)S(1)} %pad_maximum_fusion.13), channel_id=1, source_target_pairs={{0,8},{8,0},{16,24},{24,16},{1,9},{9,1},{17,25},{25,17},{2,10},{10... | collective-permute-start | bytes 884744 | tf_op jit(solution)/shard_map/ppermute | solution.py:699
  445.5 9.2 %collective-permute-start.26 = (bf16[1,2,1,2,2,48,512]{6,5,4,3,2,1,0:T(8,128)(2,1)S(1)}, bf16[1,2,1,2,2,48,512]{6,5,4,3,2,1,0:T(8,128)(2,1)S(1)}, u32[]{:S(2)}, u32[]{:S(2)}) collective-permute-start(bf16[1,2,1,2,2,48,512]{6,5,4,3,2,1,0:T(8,128)(2,1)S(1)} %pad_maximum_fusion.8), channel_id=1, source_target_pairs={{0,16},{8,24},{16,0},{24,8},{1,17},{9,25},{17,1},{25,9},{2,18},{10... | collective-permute-start | bytes 1179656 | tf_op jit(solution)/shard_map/ppermute | solution.py:699
  474.3 36.4 %collective-permute-start.31 = (f32[24,768]{1,0:T(8,128)S(1)}, f32[24,768]{1,0:T(8,128)S(1)}, u32[]{:S(2)}, u32[]{:S(2)}) collective-permute-start(f32[24,768]{1,0:T(8,128)S(1)} %constant_dynamic-slice_fusion.4), channel_id=1, source_target_pairs={{0,4},{4,0},{1,5},{5,1},{2,6},{6,2},{3,7},{7,3},{8,12},{12,8},{9,1... | collective-permute-start | bytes 221192 | tf_op jit(solution)/shard_map/ppermute | solution.py:699
  509.5 1.9 collective-permute-start.32
  (40 other events, 114.7 us)
Sparse Core Ops, SparseCore 0:
  11.4 94.6 all-gather.2
  197.1 75.1 reduce-scatter.2
  274.6 29.1 reduce-scatter.4
  309.3 110.8 all-gather.4

commit v3 on v2

--- a/solution.py
+++ b/solution.py
@@ -803,35 +803,36 @@
     core_id = core.astype(jnp.int32).reshape(1)
     packed = merge(core_id, d_up, d_down, *came, narrow * own)
     ffn_grads = lax.psum_scatter(packed, "chip", scatter_dimension=0, tiled=True)
-    so_far = attention(first_block, qkv_t, grad_mixed_t, cos, sin, packed, 1, 1, so_far)
-    ffn_grads, _ = lax.optimization_barrier((ffn_grads, so_far[2]))
     mix_t, gq_t, _, gkv_t = attention(
-        first_block, qkv_t, grad_mixed_t, cos, sin, ffn_grads, 2, HEADS // NH - 2, so_far
+        first_block, qkv_t, grad_mixed_t, cos, sin, packed, 1, HEADS // NH - 1, so_far
     )
+    ffn_grads, _ = lax.optimization_barrier((ffn_grads, gkv_t))
+    d_qkv, d_out, bias_sums = grads(cotangent, mix_t, gq_t, gkv_t, n_attn_t, ffn_grads)
     ffn_grads = lax.psum_scatter(ffn_grads, "narrow", scatter_dimension=0, tiled=True)
-    ffn_grads = lax.optimization_barrier((ffn_grads, gkv_t))[0].astype(F32)
+    scatter_up = [grid.core] + grid.chip + grid.narrow
+    scatter_down = [grid.core] + grid.chip[::-1] + grid.narrow
+    qkv_sum = grid.scatter(d_qkv, scatter_up)
+    block_output, input_grad, sums = final(
+        block_input, cotangent, y, d_ffn, mix_t, gq_t, gkv_t, w_qkv.T, w_out,
+        norm_gains, (bias_output + bias_reduce)[None, :], bias_sums,
+    )
+    vector = jnp.concatenate(
+        [sums[0], sums[1], sums[2], sums[3], bias_sums[0], sums[4], up_columns_back(d_bias_up)[0], sums[4]]
+    )
+    entries = vector.shape[0]
+    share = -(-entries // devices)
+    vector = jnp.pad(vector, (0, share * devices - entries)).reshape(devices, share)
+    vector = jnp.pad(vector, ((0, 0), (0, own * 128 - share))).reshape(D, 128)
+    out_sum = grid.scatter(jnp.concatenate([d_out, vector.astype(BF)], axis=1), scatter_down)
+
+    ffn_grads = lax.optimization_barrier((ffn_grads, sums))[0].astype(F32)
     new_expand = MUON_MOMENTUM * momentum_expand + up_columns_back(ffn_grads[:, :FF])
     new_reduce = MUON_MOMENTUM * momentum_reduce + ffn_grads[:, FF:].reshape(-1, D)
     ffn_momenta = jnp.concatenate([new_expand, new_reduce.reshape(own, 4 * D)], axis=1).astype(BF)
     ffn_whole = lax.all_gather(ffn_momenta, ("chip", "core", "narrow"), axis=0, tiled=True)
-    d_qkv, d_out, bias_sums = grads(cotangent, mix_t, gq_t, gkv_t, n_attn_t, ffn_momenta)
-    scatter_up = [grid.core] + grid.chip + grid.narrow
-    scatter_down = [grid.core] + grid.chip[::-1] + grid.narrow
-    qkv_sum = grid.scatter(d_qkv, scatter_up)
-    out_sum = grid.scatter(d_out, scatter_down)
-    block_output, input_grad, sums = final(
-        block_input, cotangent, y, d_ffn, mix_t, gq_t, gkv_t, w_qkv.T, w_out,
-        norm_gains, (bias_output + bias_reduce)[None, :], bias_sums,
-    )
-    vector_grad = jnp.concatenate(
-        [sums[0], sums[1], sums[2], sums[3], bias_sums[0], sums[4], up_columns_back(d_bias_up)[0], sums[4]]
-    )
-    for step in up_first:
-        vector_grad = vector_grad + grid.swap(vector_grad, step)
-
     new_query = MUON_MOMENTUM * momentum_query + qkv_sum[:, :D]
     new_keyval = MUON_MOMENTUM * momentum_keyval + qkv_sum[:, D:QKV]
-    new_output = MUON_MOMENTUM * momentum_output + out_sum
+    new_output = MUON_MOMENTUM * momentum_output + out_sum[:, :D]
 
     def for_core(first, second):
         mine = jnp.where(core == 0, first, second)
@@ -860,12 +861,16 @@
     o_expand = jnp.where(core == 0, mine, theirs)
     o_reduce = jnp.where(core == 0, theirs, mine).reshape(-1, D)
 
-    low_keyval = new_keyval.astype(BF)
+    first_sum = out_sum[:, D:]
+    high = first_sum.astype(BF)
+    extra = jnp.concatenate(
+        [new_keyval.astype(BF), high, (first_sum - high.astype(F32)).astype(BF)], axis=1
+    )
     pair = for_core(
-        jnp.concatenate([new_query.astype(BF), low_keyval], axis=1),
-        jnp.concatenate([new_output.astype(BF), low_keyval], axis=1),
+        jnp.concatenate([new_query.astype(BF), extra], axis=1),
+        jnp.concatenate([new_output.astype(BF), extra], axis=1),
     )
-    wide = 512
+    wide = 640
     whole = jnp.concatenate(
         [
             grid.gather(pair[:, :wide], grid.narrow[::-1] + grid.chip[::-1]),
@@ -880,6 +885,10 @@
     o_query = jnp.where(core == 0, mine, theirs)
     o_output = jnp.where(core == 0, theirs, mine)
     o_keyval = lax.dynamic_slice_in_dim(o_kv, row_lo + core * own, own, 0)
+    vector_grad = (
+        whole[:, QKV : QKV + 128].astype(F32) + whole[:, QKV + 128 :].astype(F32)
+    ).reshape(chips, narrow, 2, own * 128).swapaxes(1, 2).reshape(devices, own * 128)
+    vector_grad = vector_grad[:, :share].reshape(-1)[:entries]
 
     new_momenta = (new_query, new_keyval, new_output, new_expand, new_reduce)
     new_weights = []

time: 525 us -> 526 us (level)
  starting transfers between devices: 60 us -> 45.6 us
  Pallas kernels: 224 us -> 234 us
    reduce_scatter x1, waiting for transfers between devices: 49.8 us -> 5.57 us  [per_device(): lax.psum_scatter(packed, 'chip', scatter_dimension=0, tiled=True)]
    reduce_scatter x1, waiting for transfers between devices: 7.42 us -> 38.3 us  [per_device(): lax.psum_scatter(ffn_grads, 'narrow', scatter_dimension=0, tiled=True)]
    ppermute x38 -> x33, waiting for transfers between devices: 94 us -> 116 us  [swap(): lax.ppermute(x, axis, [(i, i ^ bit) for i in range(lax.axis_size(axis))])]
    ppermute x38 -> x33, starting transfers between devices: 59.8 us -> 45.4 us  [swap(): lax.ppermute(x, axis, [(i, i ^ bit) for i in range(lax.axis_size(axis))])]
    pallas_call x3 -> x2, Pallas kernels: 60.7 us -> 71 us  [attention(): pl.pallas_call(partial(attention_kernel, opening, closing), grid_spec=plt...]
    unnamed x97 -> x91, local copies, waits for them, and re-layouts: 18.7 us -> 16.6 us
  transfers between devices with their start and end apart: 42 -> 37, of which waited for: 26 -> 27; matrix products, arithmetic and copies ran while one was open for 6% -> 6% of each run, Pallas kernels for 28% -> 30%
where the time goes in v3:
time: 526 us; the launch traced here: 521 us
  Pallas kernels  234 us (44%)
  waiting for transfers between devices  165 us (31%)
  starting transfers between devices  45.6 us (9%)
  local copies, waits for them, and re-layouts  32.2 us (6%)
  other arithmetic  17.7 us (3%)
  between operations  15.6 us (3%)
  matrix products  11.4 us (2%)
    ppermute x33, waiting for transfers between devices, swap(): lax.ppermute(x, axis, [(i, i ^ bit) for i in range(lax.axis_size(axis))])  116 us
    pallas_call x1, Pallas kernels, ffn(): pl.pallas_call(ffn_kernel, grid=(FF // FC,), in_specs=[whole((TOK, D)), w...  77.4 us
    pallas_call x2, Pallas kernels, attention(): pl.pallas_call(partial(attention_kernel, opening, closing), grid_spec=plt...  71 us
    ppermute x33, starting transfers between devices, swap(): lax.ppermute(x, axis, [(i, i ^ bit) for i in range(lax.axis_size(axis))])  45.4 us
    reduce_scatter x1, waiting for transfers between devices, per_device(): lax.psum_scatter(ffn_grads, 'narrow', scatter_dimension=0, tiled=True)  38.3 us
    pallas_call x1, Pallas kernels, wide_ns(): pl.pallas_call(wide_kernel, grid_spec=pltpu.PrefetchScalarGridSpec(num_sc...  29.4 us
    pallas_call x1, Pallas kernels, square_ns(): pl.pallas_call(square_kernel, in_specs=[pl.BlockSpec(memory_space=pltpu.V...  19.2 us
    unnamed x91, local copies, waits for them, and re-layouts  16.6 us
  transfers between devices with their start and end apart: 37, of which 27 were waited for; matrix products, arithmetic and copies ran while one was open for 6% of the time, Pallas kernels for 30%

profile of v3, /device:TPU:0, one launch (start us, length us, event | category | flops | bytes accessed | tf_op | source)
XLA Modules:
  0.0 521.1 jit_solution(2335606835376101094)
XLA Ops:
  10.5 3.1 collective-permute-start.5
  15.9 9.0 %prepare.1 = (bf16[768,2048]{1,0:T(8,128)(2,1)S(1)}, bf16[2048,768]{1,0:T(8,128)(2,1)}, bf16[768,2048]{1,0:T(8,128)(2,1)}, bf16[768,2048]{1,0:T(8,128)(2,1)}) custom-call(bf16[2048,768]{1,0:T(8,128)(2,1)} %x_ref.3, bf16[2048,768]{1,0:T(8,128)(2,1)} %g_ref.7, f32[2,768]{1,0:T(2,128)S(1)} %copy-done.14, f32[2,768]{1,0:T(2,128)S(1)} %copy-done.16), custom_call_target="tpu_custom_call" | custom-call | flops 31457280 | bytes 18874368 | tf_op jit(solution)/shard_map/prepare/pallas_call | solution.py:419
  24.9 3.1 collective-permute-start.6
  28.2 9.7 %collective-permute-done.6 = bf16[1,1,1,1,2,24,768]{6,5,4,3,2,1,0:T(8,128)(2,1)S(1)} collective-permute-done((bf16[1,1,1,1,2,24,768]{6,5,4,3,2,1,0:T(8,128)(2,1)S(1)}, bf16[1,1,1,1,2,24,768]{6,5,4,3,2,1,0:T(8,128)(2,1)S(1)}, u32[]{:S(2)}, u32[]{:S(2)}) %collective-permute-start.6) | collective-permute-done | bytes 73760 | tf_op jit(solution)/shard_map/ppermute | solution.py:699
  41.4 1.7 collective-permute-done.7
  44.6 2.9 collective-permute-done.2
  49.0 9.8 %collective-permute-done.8 = bf16[2,1,1,2,2,24,768]{6,5,4,3,2,1,0:T(8,128)(2,1)S(1)} collective-permute-done((bf16[2,1,1,2,2,24,768]{6,5,4,3,2,1,0:T(8,128)(2,1)S(1)}, bf16[2,1,1,2,2,24,768]{6,5,4,3,2,1,0:T(8,128)(2,1)S(1)}, u32[]{:S(2)}, u32[]{:S(2)}) %collective-permute-start.8) | collective-permute-done | bytes 294944 | tf_op jit(solution)/shard_map/ppermute | solution.py:699
  61.1 2.1 copy-done.20
  63.2 4.1 convolution_convert_fusion.refs_2_
  68.1 5.0 broadcast_add_fusion.refs_1_.refs_5_
  73.2 24.6 %attention.2 = (bf16[768,2048]{1,0:T(8,128)(2,1)S(1)}, bf16[768,2048]{1,0:T(8,128)(2,1)}, f32[2048,128]{1,0:T(8,128)S(1)}) custom-call(s32[4]{0:T(128)S(1)} %and_select_fusion.refs_0_, f32[896,2048]{1,0:T(8,128)} %broadcast_add_fusion.refs_1_.refs_5_, bf16[768,2048]{1,0:T(8,128)(2,1)} %convolution_convert_fusion.refs_2_, ...), custom_call_target="tpu_custom_call" | custom-call | flops 25769803776 | bytes 5242880 | tf_op jit(solution)/shard_map/attention/pallas_call | solution.py:232
  97.8 1.7 copy-done.6
  100.4 5.7 %all-gather.3.cloned.1.call-done.up_ref.down_ref = bf16[768,6144]{1,0:T(8,128)(2,1)} async-done(((bf16[24,6144]{1,0:T(8,128)(2,1)}), bf16[768,6144]{1,0:T(8,128)(2,1)}) %all-gather.3.cloned.1.call-update) | async-done | bytes 9437200 | tf_op jit(solution)/shard_map/all_gather | solution.py:776
  106.1 77.4 %ffn.1 = (f32[2048,768]{1,0:T(8,128)}, f32[2048,768]{1,0:T(8,128)}, bf16[768,3072]{1,0:T(8,128)(2,1)}, bf16[768,3072]{1,0:T(8,128)(2,1)}, f32[1,3072]{1,0:T(1,128)}) custom-call(bf16[2048,768]{1,0:T(8,128)(2,1)} %get-tuple-element.42.x_ref, bf16[768,2048]{1,0:T(8,128)(2,1)} %get-tuple-element.43.xt_ref, bf16[2048,768]{1,0:T(8,128)(2,1)} %g_ref.7, ...), custom_call_target="tpu_custom_call" | custom-call | flops 57982058496 | bytes 46137344 | tf_op jit(solution)/shard_map/ffn/pallas_call | solution.py:331
  183.5 2.0 dynamic-slice_bitcast_fusion
  185.5 17.2 %collective-permute-start.11 = (bf16[4,96,3072]{2,1,0:T(8,128)(2,1)S(1)}, bf16[4,96,3072]{2,1,0:T(8,128)(2,1)S(1)}, u32[]{:S(2)}, u32[]{:S(2)}) collective-permute-start(bf16[4,96,3072]{2,1,0:T(8,128)(2,1)S(1)} %dynamic-slice_bitcast_fusion), channel_id=1, source_target_pairs={{0,4},{4,0},{1,5},{5,1},{2,6},{6,2},{3,7},{7,3},{8,12},{12,8},{9,1... | collective-permute-start | bytes 7077896 | tf_op jit(solution)/shard_map/ppermute | solution.py:699
  203.9 2.9 collective-permute-done.11
  206.8 3.4 collective-permute-done.10
  211.3 2.2 copy-done
  213.6 1.8 copy-done.7
  216.6 46.4 %attention.3 = (bf16[768,2048]{1,0:T(8,128)(2,1)S(1)}, bf16[768,2048]{1,0:T(8,128)(2,1)}, f32[2048,128]{1,0:T(8,128)}, bf16[128,2048]{1,0:T(8,128)(2,1)S(1)}) custom-call(s32[4]{0:T(128)S(1)} %and_select_fusion.refs_0_, f32[896,2048]{1,0:T(8,128)} %broadcast_add_fusion.refs_1_.refs_5_, ...), custom_call_target="tpu_custom_call", output_to_operand_aliasing={{0}: (7, {}), {1}: (8, {})} | custom-call | flops 51539607552 | bytes 10485760 | tf_op jit(solution)/shard_map/attention/pallas_call | solution.py:232
  265.5 5.6 %reduce-scatter.3.cloned.1.call-done._ = bf16[96,6144]{1,0:T(8,128)(2,1)} async-done(((bf16[384,6144]{1,0:T(8,128)(2,1)}), bf16[96,6144]{1,0:T(8,128)(2,1)}) %reduce-scatter.3.cloned.1.call-update) | async-done | bytes 1179664 | tf_op jit(solution)/shard_map/reduce_scatter | solution.py:805
  271.2 2.0 copy.49
  274.5 11.0 %grads.1 = (bf16[768,896]{1,0:T(8,128)(2,1)S(1)}, bf16[768,768]{1,0:T(8,128)(2,1)S(1)}, f32[8,896]{1,0:T(8,128)S(1)}) custom-call(bf16[2048,768]{1,0:T(8,128)(2,1)} %g_ref.7, bf16[768,2048]{1,0:T(8,128)(2,1)} %copy-done.8, bf16[768,2048]{1,0:T(8,128)(2,1)} %get-tuple-element.54.gq_ref, bf16[128,2048]{1,0:T(8,128)(2,1)S(1)} %copy-done.13, ...), custom_call_target="tpu_custom_call" | custom-call | flops 5234491392 | bytes 16777216 | tf_op jit(solution)/shard_map/grads/pallas_call | solution.py:467
  286.5 15.4 %closing.1 = (bf16[2048,768]{1,0:T(8,128)(2,1)}, f32[2048,768]{1,0:T(8,128)}, f32[8,768]{1,0:T(8,128)S(1)}) custom-call(bf16[2048,768]{1,0:T(8,128)(2,1)} %x_ref.3, bf16[2048,768]{1,0:T(8,128)(2,1)} %g_ref.7, f32[2048,768]{1,0:T(8,128)} %get-tuple-element.47.y_ref, f32[2048,768]{1,0:T(8,128)} %get-tuple-element.48.df_ref, bf16[768,2048]{1,0:T(8,128)(2,1)} %copy-done.8, ...), custom_call_target="tpu_custom_call" | custom-call | flops 5234491392 | bytes 37748736 | tf_op jit(solution)/shard_map/closing/pallas_call | solution.py:529
  301.9 38.3 %reduce-scatter.5.cloned.1.call-done = bf16[24,6144]{1,0:T(8,128)(2,1)} async-done(((bf16[96,6144]{1,0:T(8,128)(2,1)}), bf16[24,6144]{1,0:T(8,128)(2,1)}) %reduce-scatter.5.cloned.1.call-update) | async-done | bytes 294928 | tf_op jit(solution)/shard_map/reduce_scatter | solution.py:811
  340.2 1.7 fusion.39
  344.5 1.7 fusion.35
  346.3 1.8 fusion.34
  355.0 1.8 collective-permute-done.17
  358.3 2.8 collective-permute-start.18
  361.4 10.1 %collective-permute-done.18 = bf16[2,1,1,2,2,24,896]{6,5,4,3,2,1,0:T(8,128)(2,1)S(1)} collective-permute-done((bf16[2,1,1,2,2,24,896]{6,5,4,3,2,1,0:T(8,128)(2,1)S(1)}, bf16[2,1,1,2,2,24,896]{6,5,4,3,2,1,0:T(8,128)(2,1)S(1)}, u32[]{:S(2)}, u32[]{:S(2)}) %collective-permute-start.18) | collective-permute-done | bytes 344096 | tf_op jit(solution)/shard_map/ppermute | solution.py:699
  373.2 5.0 collective-permute-done.19
  378.9 2.5 collective-permute-start.15
  381.4 10.4 %collective-permute-done.20 = bf16[1,1,1,1,2,24,896]{6,5,4,3,2,1,0:T(8,128)(2,1)S(1)} collective-permute-done((bf16[1,1,1,1,2,24,896]{6,5,4,3,2,1,0:T(8,128)(2,1)S(1)}, bf16[1,1,1,1,2,24,896]{6,5,4,3,2,1,0:T(8,128)(2,1)S(1)}, u32[]{:S(2)}, u32[]{:S(2)}) %collective-permute-start.20) | collective-permute-done | bytes 86048 | tf_op jit(solution)/shard_map/ppermute | solution.py:699
  392.0 4.3 collective-permute-done.15
  396.4 3.7 collective-permute-done.21
  404.9 2.0 collective-permute-start.23
  406.9 6.1 %collective-permute-done.27 = bf16[1,1,1,1,1,48,512]{6,5,4,3,2,1,0:T(8,128)(2,1)S(1)} collective-permute-done((bf16[1,1,1,1,1,48,512]{6,5,4,3,2,1,0:T(8,128)(2,1)S(1)}, bf16[1,1,1,1,1,48,512]{6,5,4,3,2,1,0:T(8,128)(2,1)S(1)}, u32[]{:S(2)}, u32[]{:S(2)}) %collective-permute-start.27) | collective-permute-done | bytes 49184 | tf_op jit(solution)/shard_map/ppermute | solution.py:699
  413.4 3.1 collective-permute-done.23
  416.6 12.8 %collective-permute-done.28 = bf16[1,1,1,1,2,48,512]{6,5,4,3,2,1,0:T(8,128)(2,1)S(1)} collective-permute-done((bf16[1,1,1,1,2,48,512]{6,5,4,3,2,1,0:T(8,128)(2,1)S(1)}, bf16[1,1,1,1,2,48,512]{6,5,4,3,2,1,0:T(8,128)(2,1)S(1)}, u32[]{:S(2)}, u32[]{:S(2)}) %collective-permute-start.28) | collective-permute-done | bytes 98336 | tf_op jit(solution)/shard_map/ppermute | solution.py:699
  429.6 9.0 %collective-permute-done.24 = bf16[1,1,1,1,2,48,640]{6,5,4,3,2,1,0:T(8,128)(2,1)S(1)} collective-permute-done((bf16[1,1,1,1,2,48,640]{6,5,4,3,2,1,0:T(8,128)(2,1)S(1)}, bf16[1,1,1,1,2,48,640]{6,5,4,3,2,1,0:T(8,128)(2,1)S(1)}, u32[]{:S(2)}, u32[]{:S(2)}) %collective-permute-start.24) | collective-permute-done | bytes 122912 | tf_op jit(solution)/shard_map/ppermute | solution.py:699
  438.9 2.1 collective-permute-start.30
  441.0 6.7 %collective-permute-done.25 = bf16[1,1,1,2,2,48,640]{6,5,4,3,2,1,0:T(8,128)(2,1)S(1)} collective-permute-done((bf16[1,1,1,2,2,48,640]{6,5,4,3,2,1,0:T(8,128)(2,1)S(1)}, bf16[1,1,1,2,2,48,640]{6,5,4,3,2,1,0:T(8,128)(2,1)S(1)}, u32[]{:S(2)}, u32[]{:S(2)}) %collective-permute-start.25) | collective-permute-done | bytes 245792 | tf_op jit(solution)/shard_map/ppermute | solution.py:699
  447.9 5.0 collective-permute-done.30
  454.5 2.2 collective-permute-done.26
  458.1 19.2 %square_ns.1 = (f32[768,768]{1,0:T(8,128)S(1)}, f32[768,128]{1,0:T(8,128)S(1)}) custom-call(bf16[768,768]{1,0:T(8,128)(2,1)S(1)} %pad_maximum_fusion.2.m_ref, bf16[768,128]{1,0:T(8,128)(2,1)S(1)} %slice.155.kv_ref), custom_call_target="tpu_custom_call" | custom-call | flops 15401484288 | bytes 6291456 | tf_op jit(solution)/shard_map/square_ns/pallas_call | solution.py:685
  477.5 29.4 %wide_ns.1 = (bf16[768,768]{1,0:T(8,128)(2,1)S(1)}, f32[1,768]{1,0:T(1,128)S(1)}) custom-call(s32[1]{0:T(128)} %bitcast.10._.down_ref, bf16[768,6144]{1,0:T(8,128)(2,1)} %all-gather.5.cloned.1.call-done.m_ref), custom_call_target="tpu_custom_call" | custom-call | flops 21743271936 | bytes 6291456 | tf_op jit(solution)/shard_map/wide_ns/pallas_call | solution.py:637
  (275 shorter events, 54.1 us)
Async XLA Ops:
  7.2 98.9 %all-gather.3.cloned.1.call-start = ((), (), s32[]{:S(2)}) async-start(), calls=%async_computation.2 | async-start | bytes 9732096 | tf_op jit(solution)/shard_map/all_gather | solution.py:776
  10.4 260.6 %reduce-scatter.3.cloned.1.call-start = ((), (), s32[]{:S(2)}) async-start(), calls=%async_computation.3 | async-start | bytes 5898240 | tf_op jit(solution)/shard_map/reduce_scatter | solution.py:805
  10.5 14.4 %collective-permute-start.5 = (bf16[1,1,1,1,1,24,768]{6,5,4,3,2,1,0:T(8,128)(2,1)S(1)}, bf16[1,1,1,1,1,24,768]{6,5,4,3,2,1,0:T(8,128)(2,1)S(1)}, u32[]{:S(2)}, u32[]{:S(2)}) collective-permute-start(bf16[1,1,1,1,1,24,768]{6,5,4,3,2,1,0:T(8,128)(2,1)S(1)} %convert_bitcast_fusion), channel_id=1, source_target_pairs={{0,1},{1,0},{2,3},{3,2},{4,5},{5,4},{6,7},{7,6},{8,9},{9,8},{10,11... | collective-permute-start | bytes 110600 | tf_op jit(solution)/shard_map/ppermute | solution.py:699
  13.6 14.4 %collective-permute-start = (bf16[1,1,1,1,1,24,896]{6,5,4,3,2,1,0:T(8,128)(2,1)S(1)}, bf16[1,1,1,1,1,24,896]{6,5,4,3,2,1,0:T(8,128)(2,1)S(1)}, u32[]{:S(2)}, u32[]{:S(2)}) collective-permute-start(bf16[1,1,1,1,1,24,896]{6,5,4,3,2,1,0:T(8,128)(2,1)S(1)} %pad_maximum_fusion.30), channel_id=1, source_target_pairs={{0,1},{1,0},{2,3},{3,2},{4,5},{5,4},{6,7},{7,6},{8,9},{9,8},{10,11... | collective-permute-start | bytes 129032 | tf_op jit(solution)/shard_map/ppermute | solution.py:699
  24.9 42.7 %copy-start.5 = (bf16[768,2048]{1,0:T(8,128)(2,1)}, bf16[768,2048]{1,0:T(8,128)(2,1)S(1)}, u32[]{:S(2)}) copy-start(bf16[768,2048]{1,0:T(8,128)(2,1)S(1)} %get-tuple-element.45.nt_ref) | copy-start | bytes 9437188
  24.9 12.9 %collective-permute-start.6 = (bf16[1,1,1,1,2,24,768]{6,5,4,3,2,1,0:T(8,128)(2,1)S(1)}, bf16[1,1,1,1,2,24,768]{6,5,4,3,2,1,0:T(8,128)(2,1)S(1)}, u32[]{:S(2)}, u32[]{:S(2)}) collective-permute-start(bf16[1,1,1,1,2,24,768]{6,5,4,3,2,1,0:T(8,128)(2,1)S(1)} %pad_maximum_fusion.22), channel_id=1, source_target_pairs={{0,2},{1,3},{2,0},{3,1},{4,6},{5,7},{6,4},{7,5},{8,10},{9,11},{10,... | collective-permute-start | bytes 221192 | tf_op jit(solution)/shard_map/ppermute | solution.py:699
  28.1 11.7 %collective-permute-start.1 = (bf16[1,1,1,1,2,24,896]{6,5,4,3,2,1,0:T(8,128)(2,1)S(1)}, bf16[1,1,1,1,2,24,896]{6,5,4,3,2,1,0:T(8,128)(2,1)S(1)}, u32[]{:S(2)}, u32[]{:S(2)}) collective-permute-start(bf16[1,1,1,1,2,24,896]{6,5,4,3,2,1,0:T(8,128)(2,1)S(1)} %pad_maximum_fusion.21), channel_id=1, source_target_pairs={{0,2},{1,3},{2,0},{3,1},{4,6},{5,7},{6,4},{7,5},{8,10},{9,11},{10,... | collective-permute-start | bytes 258056 | tf_op jit(solution)/shard_map/ppermute | solution.py:699
  37.9 5.2 collective-permute-start.7
  39.8 7.7 %collective-permute-start.2 = (bf16[1,1,1,2,2,24,896]{6,5,4,3,2,1,0:T(8,128)(2,1)S(1)}, bf16[1,1,1,2,2,24,896]{6,5,4,3,2,1,0:T(8,128)(2,1)S(1)}, u32[]{:S(2)}, u32[]{:S(2)}) collective-permute-start(bf16[1,1,1,2,2,24,896]{6,5,4,3,2,1,0:T(8,128)(2,1)S(1)} %pad_maximum_fusion.17), channel_id=1, source_target_pairs={{0,8},{8,0},{16,24},{24,16},{1,9},{9,1},{17,25},{25,17},{2,10},{10... | collective-permute-start | bytes 516104 | tf_op jit(solution)/shard_map/ppermute | solution.py:699
  43.2 15.6 %collective-permute-start.8 = (bf16[2,1,1,2,2,24,768]{6,5,4,3,2,1,0:T(8,128)(2,1)S(1)}, bf16[2,1,1,2,2,24,768]{6,5,4,3,2,1,0:T(8,128)(2,1)S(1)}, u32[]{:S(2)}, u32[]{:S(2)}) collective-permute-start(bf16[2,1,1,2,2,24,768]{6,5,4,3,2,1,0:T(8,128)(2,1)S(1)} %pad_maximum_fusion.13), channel_id=1, source_target_pairs={{0,8},{8,0},{16,24},{24,16},{1,9},{9,1},{17,25},{25,17},{2,10},{10... | collective-permute-start | bytes 884744 | tf_op jit(solution)/shard_map/ppermute | solution.py:699
  47.6 11.3 %collective-permute-start.3 = (bf16[1,2,1,2,2,24,896]{6,5,4,3,2,1,0:T(8,128)(2,1)S(1)}, bf16[1,2,1,2,2,24,896]{6,5,4,3,2,1,0:T(8,128)(2,1)S(1)}, u32[]{:S(2)}, u32[]{:S(2)}) collective-permute-start(bf16[1,2,1,2,2,24,896]{6,5,4,3,2,1,0:T(8,128)(2,1)S(1)} %pad_maximum_fusion.11), channel_id=1, source_target_pairs={{0,16},{8,24},{16,0},{24,8},{1,17},{9,25},{17,1},{25,9},{2,18},{10... | collective-permute-start | bytes 1032200 | tf_op jit(solution)/shard_map/ppermute | solution.py:699
  58.8 2.1 collective-permute-start.9
  59.1 8.2 %collective-permute-start.4 = (bf16[2,2,1,2,2,24,896]{6,5,4,3,2,1,0:T(8,128)(2,1)S(1)}, bf16[2,2,1,2,2,24,896]{6,5,4,3,2,1,0:T(8,128)(2,1)S(1)}, u32[]{:S(2)}, u32[]{:S(2)}) collective-permute-start(bf16[2,2,1,2,2,24,896]{6,5,4,3,2,1,0:T(8,128)(2,1)S(1)} %pad_maximum_fusion.7), channel_id=1, source_target_pairs={{0,4},{4,0},{1,5},{5,1},{2,6},{6,2},{3,7},{7,3},{8,12},{12,8},{9,1... | collective-permute-start | bytes 2064392 | tf_op jit(solution)/shard_map/ppermute | solution.py:699
  183.5 19.2 %copy-start.1 = (bf16[768,3072]{1,0:T(8,128)(2,1)S(1)}, bf16[768,3072]{1,0:T(8,128)(2,1)}, u32[]{:S(2)}) copy-start(bf16[768,3072]{1,0:T(8,128)(2,1)} %get-tuple-element.49.up_ref) | copy-start | bytes 14155780
  185.5 21.3 %collective-permute-start.11 = (bf16[4,96,3072]{2,1,0:T(8,128)(2,1)S(1)}, bf16[4,96,3072]{2,1,0:T(8,128)(2,1)S(1)}, u32[]{:S(2)}, u32[]{:S(2)}) collective-permute-start(bf16[4,96,3072]{2,1,0:T(8,128)(2,1)S(1)} %dynamic-slice_bitcast_fusion), channel_id=1, source_target_pairs={{0,4},{4,0},{1,5},{5,1},{2,6},{6,2},{3,7},{7,3},{8,12},{12,8},{9,1... | collective-permute-start | bytes 7077896 | tf_op jit(solution)/shard_map/ppermute | solution.py:699
  202.6 7.5 %copy-start.2 = (bf16[768,3072]{1,0:T(8,128)(2,1)S(1)}, bf16[768,3072]{1,0:T(8,128)(2,1)}, u32[]{:S(2)}) copy-start(bf16[768,3072]{1,0:T(8,128)(2,1)} %get-tuple-element.50.down_ref) | copy-start | bytes 14155780
  202.8 7.4 %collective-permute-start.10 = (bf16[4,96,3072]{2,1,0:T(8,128)(2,1)S(1)}, bf16[4,96,3072]{2,1,0:T(8,128)(2,1)S(1)}, u32[]{:S(2)}, u32[]{:S(2)}) collective-permute-start(bf16[4,96,3072]{2,1,0:T(8,128)(2,1)S(1)} %dynamic-slice_bitcast_fusion.1), channel_id=1, source_target_pairs={{0,4},{4,0},{1,5},{5,1},{2,6},{6,2},{3,7},{7,3},{8,12},{12,8},{9,1... | collective-permute-start | bytes 7077896 | tf_op jit(solution)/shard_map/ppermute | solution.py:699
  213.5 126.7 %reduce-scatter.5.cloned.1.call-start = ((), (), s32[]{:S(2)}) async-start(), calls=%async_computation.4 | async-start | bytes 1474560 | tf_op jit(solution)/shard_map/reduce_scatter | solution.py:811
  216.6 54.5 %copy-start.27 = (f32[5504]{0:T(1024)S(1)}, f32[5504]{0:T(1024)}, u32[]{:S(2)}) copy-start(f32[5504]{0:T(1024)} %param.33) | copy-start | bytes 66052
  271.1 206.3 %all-gather.5.cloned.1.call-start = ((), (), s32[]{:S(2)}) async-start(), calls=%async_computation.5 | async-start | bytes 9732096 | tf_op jit(solution)/shard_map/all_gather | solution.py:832
  274.5 12.0 %copy-start.4 = (bf16[2,2,2,2,2,24,768]{6,5,4,3,2,1,0:T(8,128)(2,1)S(1)}, bf16[2,2,2,2,2,24,768]{6,5,4,3,2,1,0:T(8,128)(2,1)}, u32[]{:S(2)}) copy-start(bf16[2,2,2,2,2,24,768]{6,5,4,3,2,1,0:T(8,128)(2,1)} %copy-done.3) | copy-start | bytes 3538948
  274.5 12.0 %copy-start.15 = (f32[2,768]{1,0:T(2,128)S(1)}, f32[2,768]{1,0:T(2,128)}, u32[]{:S(2)}) copy-start(f32[2,768]{1,0:T(2,128)} %gain_ref.3) | copy-start | bytes 18436
  353.0 3.8 collective-permute-start.17
  354.8 6.3 %collective-permute-start.12 = (bf16[2,2,1,2,2,24,896]{6,5,4,3,2,1,0:T(8,128)(2,1)S(1)}, bf16[2,2,1,2,2,24,896]{6,5,4,3,2,1,0:T(8,128)(2,1)S(1)}, u32[]{:S(2)}, u32[]{:S(2)}) collective-permute-start(bf16[2,2,1,2,2,24,896]{6,5,4,3,2,1,0:T(8,128)(2,1)S(1)} %constant_dynamic-slice_fusion.6), channel_id=1, source_target_pairs={{0,4},{4,0},{1,5},{5,1},{2,6},{6,2},{3,7},{7,3},{8,12},{12,8},{9,1... | collective-permute-start | bytes 2064392 | tf_op jit(solution)/shard_map/ppermute | solution.py:699
  358.3 13.2 %collective-permute-start.18 = (bf16[2,1,1,2,2,24,896]{6,5,4,3,2,1,0:T(8,128)(2,1)S(1)}, bf16[2,1,1,2,2,24,896]{6,5,4,3,2,1,0:T(8,128)(2,1)S(1)}, u32[]{:S(2)}, u32[]{:S(2)}) collective-permute-start(bf16[2,1,1,2,2,24,896]{6,5,4,3,2,1,0:T(8,128)(2,1)S(1)} %dynamic-slice_convert_fusion), channel_id=1, source_target_pairs={{0,8},{8,0},{16,24},{24,16},{1,9},{9,1},{17,25},{25,17},{2,10},{10... | collective-permute-start | bytes 1032200 | tf_op jit(solution)/shard_map/ppermute | solution.py:699
  361.3 11.5 %collective-permute-start.13 = (bf16[1,2,1,2,2,24,896]{6,5,4,3,2,1,0:T(8,128)(2,1)S(1)}, bf16[1,2,1,2,2,24,896]{6,5,4,3,2,1,0:T(8,128)(2,1)S(1)}, u32[]{:S(2)}, u32[]{:S(2)}) collective-permute-start(bf16[1,2,1,2,2,24,896]{6,5,4,3,2,1,0:T(8,128)(2,1)S(1)} %dynamic-slice_convert_fusion.1), channel_id=1, source_target_pairs={{0,16},{8,24},{16,0},{24,8},{1,17},{9,25},{17,1},{25,9},{2,18},{10... | collective-permute-start | bytes 1032200 | tf_op jit(solution)/shard_map/ppermute | solution.py:699
  371.6 6.6 %collective-permute-start.19 = (bf16[1,1,1,2,2,24,896]{6,5,4,3,2,1,0:T(8,128)(2,1)S(1)}, bf16[1,1,1,2,2,24,896]{6,5,4,3,2,1,0:T(8,128)(2,1)S(1)}, u32[]{:S(2)}, u32[]{:S(2)}) collective-permute-start(bf16[1,1,1,2,2,24,896]{6,5,4,3,2,1,0:T(8,128)(2,1)S(1)} %dynamic-slice_convert_fusion.2), channel_id=1, source_target_pairs={{0,16},{8,24},{16,0},{24,8},{1,17},{9,25},{17,1},{25,9},{2,18},{10... | collective-permute-start | bytes 516104 | tf_op jit(solution)/shard_map/ppermute | solution.py:699
  372.9 6.0 %collective-permute-start.14 = (bf16[1,1,1,2,2,24,896]{6,5,4,3,2,1,0:T(8,128)(2,1)S(1)}, bf16[1,1,1,2,2,24,896]{6,5,4,3,2,1,0:T(8,128)(2,1)S(1)}, u32[]{:S(2)}, u32[]{:S(2)}) collective-permute-start(bf16[1,1,1,2,2,24,896]{6,5,4,3,2,1,0:T(8,128)(2,1)S(1)} %dynamic-slice_convert_fusion.3), channel_id=1, source_target_pairs={{0,8},{8,0},{16,24},{24,16},{1,9},{9,1},{17,25},{25,17},{2,10},{10... | collective-permute-start | bytes 516104 | tf_op jit(solution)/shard_map/ppermute | solution.py:699
  378.2 23.4 %copy-start.40 = (f32[24,128]{1,0:T(8,128)S(1)}, f32[24,128]{1,0:T(8,128)}, u32[]{:S(2)}) copy-start(f32[24,128]{1,0:T(8,128)} %param.27) | copy-start | bytes 36868
  378.2 24.0 %copy-start.32 = (f32[24,768]{1,0:T(8,128)S(1)}, f32[24,768]{1,0:T(8,128)}, u32[]{:S(2)}) copy-start(f32[24,768]{1,0:T(8,128)} %param.28) | copy-start | bytes 221188
  378.3 24.6 %copy-start.33 = (f32[24,768]{1,0:T(8,128)S(1)}, f32[24,768]{1,0:T(8,128)}, u32[]{:S(2)}) copy-start(f32[24,768]{1,0:T(8,128)} %param.26) | copy-start | bytes 221188
  378.3 13.6 %collective-permute-start.20 = (bf16[1,1,1,1,2,24,896]{6,5,4,3,2,1,0:T(8,128)(2,1)S(1)}, bf16[1,1,1,1,2,24,896]{6,5,4,3,2,1,0:T(8,128)(2,1)S(1)}, u32[]{:S(2)}, u32[]{:S(2)}) collective-permute-start(bf16[1,1,1,1,2,24,896]{6,5,4,3,2,1,0:T(8,128)(2,1)S(1)} %dynamic-slice_convert_fusion.4), channel_id=1, source_target_pairs={{0,2},{1,3},{2,0},{3,1},{4,6},{5,7},{6,4},{7,5},{8,10},{9,11},{10,... | collective-permute-start | bytes 258056 | tf_op jit(solution)/shard_map/ppermute | solution.py:699
  378.9 17.4 %collective-permute-start.15 = (bf16[1,1,1,1,2,24,896]{6,5,4,3,2,1,0:T(8,128)(2,1)S(1)}, bf16[1,1,1,1,2,24,896]{6,5,4,3,2,1,0:T(8,128)(2,1)S(1)}, u32[]{:S(2)}, u32[]{:S(2)}) collective-permute-start(bf16[1,1,1,1,2,24,896]{6,5,4,3,2,1,0:T(8,128)(2,1)S(1)} %dynamic-slice_convert_fusion.5), channel_id=1, source_target_pairs={{0,2},{1,3},{2,0},{3,1},{4,6},{5,7},{6,4},{7,5},{8,10},{9,11},{10,... | collective-permute-start | bytes 258056 | tf_op jit(solution)/shard_map/ppermute | solution.py:699
  391.9 8.2 %collective-permute-start.21 = (bf16[1,1,1,1,1,24,896]{6,5,4,3,2,1,0:T(8,128)(2,1)S(1)}, bf16[1,1,1,1,1,24,896]{6,5,4,3,2,1,0:T(8,128)(2,1)S(1)}, u32[]{:S(2)}, u32[]{:S(2)}) collective-permute-start(bf16[1,1,1,1,1,24,896]{6,5,4,3,2,1,0:T(8,128)(2,1)S(1)} %dynamic-slice_convert_fusion.6), channel_id=1, source_target_pairs={{0,1},{1,0},{2,3},{3,2},{4,5},{5,4},{6,7},{7,6},{8,9},{9,8},{10,11... | collective-permute-start | bytes 129032 | tf_op jit(solution)/shard_map/ppermute | solution.py:699
  396.3 5.2 %collective-permute-start.16 = (bf16[1,1,1,1,1,24,896]{6,5,4,3,2,1,0:T(8,128)(2,1)S(1)}, bf16[1,1,1,1,1,24,896]{6,5,4,3,2,1,0:T(8,128)(2,1)S(1)}, u32[]{:S(2)}, u32[]{:S(2)}) collective-permute-start(bf16[1,1,1,1,1,24,896]{6,5,4,3,2,1,0:T(8,128)(2,1)S(1)} %dynamic-slice_convert_fusion.7), channel_id=1, source_target_pairs={{0,1},{1,0},{2,3},{3,2},{4,5},{5,4},{6,7},{7,6},{8,9},{9,8},{10,11... | collective-permute-start | bytes 129032 | tf_op jit(solution)/shard_map/ppermute | solution.py:699
  403.5 1.3 collective-permute-start.22
  404.8 8.2 %collective-permute-start.27 = (bf16[1,1,1,1,1,48,512]{6,5,4,3,2,1,0:T(8,128)(2,1)S(1)}, bf16[1,1,1,1,1,48,512]{6,5,4,3,2,1,0:T(8,128)(2,1)S(1)}, u32[]{:S(2)}, u32[]{:S(2)}) collective-permute-start(bf16[1,1,1,1,1,48,512]{6,5,4,3,2,1,0:T(8,128)(2,1)S(1)} %fusion.25), channel_id=1, source_target_pairs={{0,1},{1,0},{2,3},{3,2},{4,5},{5,4},{6,7},{7,6},{8,9},{9,8},{10,11... | collective-permute-start | bytes 147464 | tf_op jit(solution)/shard_map/ppermute | solution.py:699
  404.9 11.6 %collective-permute-start.23 = (bf16[1,1,1,1,1,48,640]{6,5,4,3,2,1,0:T(8,128)(2,1)S(1)}, bf16[1,1,1,1,1,48,640]{6,5,4,3,2,1,0:T(8,128)(2,1)S(1)}, u32[]{:S(2)}, u32[]{:S(2)}) collective-permute-start(bf16[1,1,1,1,1,48,640]{6,5,4,3,2,1,0:T(8,128)(2,1)S(1)} %fusion.24), channel_id=1, source_target_pairs={{0,1},{1,0},{2,3},{3,2},{4,5},{5,4},{6,7},{7,6},{8,9},{9,8},{10,11... | collective-permute-start | bytes 184328 | tf_op jit(solution)/shard_map/ppermute | solution.py:699
  413.1 16.4 %collective-permute-start.28 = (bf16[1,1,1,1,2,48,512]{6,5,4,3,2,1,0:T(8,128)(2,1)S(1)}, bf16[1,1,1,1,2,48,512]{6,5,4,3,2,1,0:T(8,128)(2,1)S(1)}, u32[]{:S(2)}, u32[]{:S(2)}) collective-permute-start(bf16[1,1,1,1,2,48,512]{6,5,4,3,2,1,0:T(8,128)(2,1)S(1)} %pad_maximum_fusion.20), channel_id=1, source_target_pairs={{0,2},{1,3},{2,0},{3,1},{4,6},{5,7},{6,4},{7,5},{8,10},{9,11},{10,... | collective-permute-start | bytes 294920 | tf_op jit(solution)/shard_map/ppermute | solution.py:699
  416.6 22.0 %collective-permute-start.24 = (bf16[1,1,1,1,2,48,640]{6,5,4,3,2,1,0:T(8,128)(2,1)S(1)}, bf16[1,1,1,1,2,48,640]{6,5,4,3,2,1,0:T(8,128)(2,1)S(1)}, u32[]{:S(2)}, u32[]{:S(2)}) collective-permute-start(bf16[1,1,1,1,2,48,640]{6,5,4,3,2,1,0:T(8,128)(2,1)S(1)} %pad_maximum_fusion.19), channel_id=1, source_target_pairs={{0,2},{1,3},{2,0},{3,1},{4,6},{5,7},{6,4},{7,5},{8,10},{9,11},{10,... | collective-permute-start | bytes 368648 | tf_op jit(solution)/shard_map/ppermute | solution.py:699
  429.5 11.4 %copy-start.17 = (f32[2,768]{1,0:T(2,128)S(1)}, f32[2,768]{1,0:T(2,128)}, u32[]{:S(2)}) copy-start(f32[2,768]{1,0:T(2,128)} %shift_ref.1) | copy-start | bytes 18436
  429.5 9.2 %collective-permute-start.29 = (bf16[1,1,1,2,2,48,512]{6,5,4,3,2,1,0:T(8,128)(2,1)S(1)}, bf16[1,1,1,2,2,48,512]{6,5,4,3,2,1,0:T(8,128)(2,1)S(1)}, u32[]{:S(2)}, u32[]{:S(2)}) collective-permute-start(bf16[1,1,1,2,2,48,512]{6,5,4,3,2,1,0:T(8,128)(2,1)S(1)} %pad_maximum_fusion.16), channel_id=1, source_target_pairs={{0,16},{8,24},{16,0},{24,8},{1,17},{9,25},{17,1},{25,9},{2,18},{10... | collective-permute-start | bytes 589832 | tf_op jit(solution)/shard_map/ppermute | solution.py:699
  438.7 9.0 %collective-permute-start.25 = (bf16[1,1,1,2,2,48,640]{6,5,4,3,2,1,0:T(8,128)(2,1)S(1)}, bf16[1,1,1,2,2,48,640]{6,5,4,3,2,1,0:T(8,128)(2,1)S(1)}, u32[]{:S(2)}, u32[]{:S(2)}) collective-permute-start(bf16[1,1,1,2,2,48,640]{6,5,4,3,2,1,0:T(8,128)(2,1)S(1)} %pad_maximum_fusion.15), channel_id=1, source_target_pairs={{0,8},{8,0},{16,24},{24,16},{1,9},{9,1},{17,25},{25,17},{2,10},{10... | collective-permute-start | bytes 737288 | tf_op jit(solution)/shard_map/ppermute | solution.py:699
  438.9 14.0 %collective-permute-start.30 = (bf16[2,1,1,2,2,48,512]{6,5,4,3,2,1,0:T(8,128)(2,1)S(1)}, bf16[2,1,1,2,2,48,512]{6,5,4,3,2,1,0:T(8,128)(2,1)S(1)}, u32[]{:S(2)}, u32[]{:S(2)}) collective-permute-start(bf16[2,1,1,2,2,48,512]{6,5,4,3,2,1,0:T(8,128)(2,1)S(1)} %pad_maximum_fusion.10), channel_id=1, source_target_pairs={{0,8},{8,0},{16,24},{24,16},{1,9},{9,1},{17,25},{25,17},{2,10},{10... | collective-permute-start | bytes 1179656 | tf_op jit(solution)/shard_map/ppermute | solution.py:699
  447.8 9.0 %collective-permute-start.26 = (bf16[1,2,1,2,2,48,640]{6,5,4,3,2,1,0:T(8,128)(2,1)S(1)}, bf16[1,2,1,2,2,48,640]{6,5,4,3,2,1,0:T(8,128)(2,1)}, u32[]{:S(2)}, u32[]{:S(2)}) collective-permute-start(bf16[1,2,1,2,2,48,640]{6,5,4,3,2,1,0:T(8,128)(2,1)S(1)} %pad_maximum_fusion.9), channel_id=1, source_target_pairs={{0,16},{8,24},{16,0},{24,8},{1,17},{9,25},{17,1},{25,9},{2,18},{10... | collective-permute-start | bytes 1474568 | tf_op jit(solution)/shard_map/ppermute | solution.py:699
  477.3 34.5 %collective-permute-start.31 = (f32[24,768]{1,0:T(8,128)S(1)}, f32[24,768]{1,0:T(8,128)S(1)}, u32[]{:S(2)}, u32[]{:S(2)}) collective-permute-start(f32[24,768]{1,0:T(8,128)S(1)} %constant_dynamic-slice_fusion.4), channel_id=1, source_target_pairs={{0,4},{4,0},{1,5},{5,1},{2,6},{6,2},{3,7},{7,3},{8,12},{12,8},{9,1... | collective-permute-start | bytes 221192 | tf_op jit(solution)/shard_map/ppermute | solution.py:699
  477.4 29.5 %copy-start.36 = (bf16[768,6144]{1,0:T(8,128)(2,1)S(1)}, bf16[768,6144]{1,0:T(8,128)(2,1)}, u32[]{:S(2)}) copy-start(bf16[768,6144]{1,0:T(8,128)(2,1)} %all-gather.5.cloned.1.call-done.m_ref) | copy-start | bytes 28311556
  510.7 1.9 collective-permute-start.32
  (32 other events, 92.0 us)
Sparse Core Ops, SparseCore 0:
  11.4 94.6 all-gather.2
  213.7 57.3 reduce-scatter.2
  273.4 66.7 reduce-scatter.4
  349.0 96.6 all-gather.4
